TPU v7x, 128 devices: a whole 4x4x4 slice. The times are simulated.
128 devices in a mesh: seq: 32 (over x, z, core), head: 4 (over y).
Axes of the slice: x: 4, y: 4, z: 4, core: 2. Of those that a mesh axis runs over, the one named last changes fastest.
Arguments:
- tokens: bfloat16 [8192, 2048], P('seq'), may hold values from -6 to 6
- mixer_gain: float32 [2048], replicated, may hold values from 0.5 to 1.5
- in_weight: bfloat16 [2048, 16, 768], P('seq', 'head'), may hold values from -0.125 to 0.125
- rate_weight: bfloat16 [2048, 2, 16], P('seq', None, 'head'), may hold values from -0.125 to 0.125
- conv_weight: float32 [4, 16, 512], P(None, 'head'), may hold values from -2 to 2
- decay_log: float32 [16], P('head'), may hold values from -9 to -3
- decay_bias: float32 [16], P('head'), may hold values from -1 to 1
- out_gain: float32 [256], replicated, may hold values from 0.5 to 1.5
- out_weight: bfloat16 [2048, 16, 256], P('seq', 'head'), may hold values from -0.1875 to 0.1875
- ffn_gain: float32 [2048], replicated, may hold values from 0.5 to 1.5
- gate_up_weight: bfloat16 [2048, 2, 5632], P('seq', None, 'head'), may hold values from -0.125 to 0.125
- down_weight: bfloat16 [2048, 5632], P('seq', 'head'), may hold values from -0.078125 to 0.078125
- cotangent: bfloat16 [8192, 2048], P('seq'), may hold values from -6 to 6
Outputs:
- output: bfloat16 [8192, 2048], P('seq')
- grad_tokens: float32 [8192, 2048], P('seq')
- grad_mixer_gain: float32 [2048], replicated
- grad_in_weight: float32 [2048, 16, 768], P('seq', 'head')
- grad_rate_weight: float32 [2048, 2, 16], P('seq', None, 'head')
- grad_conv_weight: float32 [4, 16, 512], P(None, 'head')
- grad_decay_log: float32 [16], P('head')
- grad_decay_bias: float32 [16], P('head')
- grad_out_gain: float32 [256], replicated
- grad_out_weight: float32 [2048, 16, 256], P('seq', 'head')
- grad_ffn_gain: float32 [2048], replicated
- grad_gate_up_weight: float32 [2048, 2, 5632], P('seq', None, 'head')
- grad_down_weight: float32 [2048, 5632], P('seq', 'head')
All inputs are finite; a program needn't handle non-finite values.
Results may differ from a plain program's by a relative error of at most 0.035.
Values may be sent and summed in bfloat16 or wider, within the bound.
A program may use at most 256 MiB of HBM per device.

v0:
```python
import jax
import jax.numpy as jnp
from jax import lax
from jax.sharding import PartitionSpec as P

DK = 128
DV = 256
CH = 64
KW = 4
CONV = 512


HIGH = lax.Precision.HIGHEST


def from_behind(block, axis, distance):
    devices = range(lax.axis_size(axis))
    route = [(i - distance, i) for i in devices if i - distance in devices]
    return lax.ppermute(block, axis, route)


def carried_in(value, axis, combine, identity):
    peers, mine = (lax.axis_size(axis), lax.axis_index(axis))
    everything = jax.tree.map(
        lambda part, kind: lax.all_gather(part.astype(kind), axis),
        value,
        (jnp.bfloat16, jnp.bfloat16),
    )
    start = jax.tree.map(
        lambda part, zero: jnp.broadcast_to(jnp.asarray(zero, part.dtype), part.shape),
        value,
        identity,
    )

    def turn(k, before):
        reached = k < mine
        new = combine(
            before, jax.tree.map(lambda part, own: part[k].astype(own.dtype), everything, value)
        )
        return jax.tree.map(lambda a, b: jnp.where(reached, a, b), new, before)

    return lax.fori_loop(0, peers, turn, start)


def carried_in_2(value, axis, combine, identity):
    peers, mine = (lax.axis_size(axis), lax.axis_index(axis))
    everything = jax.tree.map(
        lambda part, kind: lax.all_gather(part.astype(kind), axis),
        value,
        jax.tree.map(lambda a: jnp.bfloat16 if a.dtype == jnp.float32 else a.dtype, value),
    )
    start = jax.tree.map(
        lambda part, zero: jnp.broadcast_to(jnp.asarray(zero, part.dtype), part.shape),
        value,
        identity,
    )

    def turn(k, before):
        at = peers - 1 - k
        reached = at > mine
        new = combine(
            before, jax.tree.map(lambda part, own: part[at].astype(own.dtype), everything, value)
        )
        return jax.tree.map(lambda a, b: jnp.where(reached, a, b), new, before)

    return lax.fori_loop(0, peers, turn, start)


def rms(values, gain):
    return values * lax.rsqrt(jnp.mean(values * values, axis=-1, keepdims=True) + 1e-05) * gain


def out_norm(mixer_out, gate_pre, gain):
    return rms(mixer_out, gain) * jax.nn.silu(gate_pre)


def group_rule(state, queries, keys, values, beta, decay):
    size = queries.shape[0]
    gamma = jnp.cumsum(decay, axis=0).T
    rows = lax.broadcasted_iota(jnp.int32, (size, size), 0)
    columns = lax.broadcasted_iota(jnp.int32, (size, size), 1)
    inclusive = (columns <= rows).astype(jnp.float32)
    strict = (columns < rows).astype(jnp.float32)
    spread = gamma[:, :, None] - gamma[:, None, :]
    decays = jnp.exp(spread * inclusive) * inclusive
    head_queries = jnp.transpose(queries, (1, 0, 2))
    head_keys = jnp.transpose(keys, (1, 0, 2))
    head_values = jnp.transpose(values, (1, 0, 2))
    head_beta = beta.T[:, :, None]
    key_products = jnp.einsum("hcd,hed->hce", head_keys, head_keys, precision=HIGH)
    lower = head_beta * decays * strict * key_products
    identity = jnp.eye(size, dtype=jnp.float32)
    growth = jnp.exp(gamma)[:, :, None]
    targets = head_beta * (
        head_values - growth * jnp.einsum("hcd,hdw->hcw", head_keys, state, precision=HIGH)
    )
    written = jax.scipy.linalg.solve_triangular(
        lower + identity, targets, lower=True, unit_diagonal=True
    )
    scores = jnp.einsum("hcd,hed->hce", head_queries, head_keys, precision=HIGH) * decays
    result = growth * jnp.einsum("hcd,hdw->hcw", head_queries, state, precision=HIGH)
    result = result + jnp.einsum("hce,hew->hcw", scores, written, precision=HIGH)
    final = gamma[:, -1]
    weights = jnp.exp(final[:, None] - gamma)[:, :, None]
    new_state = jnp.exp(final)[:, None, None] * state
    new_state = new_state + jnp.einsum("hcd,hcw->hdw", head_keys * weights, written, precision=HIGH)
    return (new_state, jnp.transpose(result, (1, 0, 2)))


def mixer_inputs(padded, rate_pre, conv_weight, decay_log, decay_bias):
    length = padded.shape[0] - (KW - 1)
    mixed = sum((conv_weight[j] * padded[j : j + length] for j in range(KW)))
    active = jax.nn.silu(mixed)
    query_part = active[..., :DK]
    key_part = active[..., DK : 2 * DK]
    queries = (
        query_part
        * lax.rsqrt(jnp.sum(query_part * query_part, axis=-1, keepdims=True) + 1e-06)
        * DK ** (-0.5)
    )
    keys = key_part * lax.rsqrt(jnp.sum(key_part * key_part, axis=-1, keepdims=True) + 1e-06)
    values = active[..., 2 * DK :]
    beta = jax.nn.sigmoid(rate_pre[:, 1])
    decay = -jnp.exp(decay_log) * jax.nn.softplus(rate_pre[:, 0] + decay_bias)
    return (queries, keys, values, beta, decay)


def run_blocks(state, queries, keys, values, beta, decay):
    length = queries.shape[0]
    count = length // CH

    def split(array):
        return array.reshape((count, CH) + array.shape[1:])

    def block(carry, pieces):
        return group_rule(carry, *pieces)

    final, outputs = lax.scan(
        block, state, (split(queries), split(keys), split(values), split(beta), split(decay))
    )
    return (final, outputs.reshape((length,) + outputs.shape[2:]))


def local_rule(queries, keys, values, beta, decay, entering):
    final, outputs = run_blocks(entering, queries, keys, values, beta, decay)
    return (outputs, final)


def compose(earlier, later):
    return (
        jnp.einsum("hij,hjk->hik", later[0], earlier[0], precision=HIGH),
        jnp.einsum("hij,hjk->hik", later[0], earlier[1], precision=HIGH) + later[1],
    )


def rounded(values):
    return lax.optimization_barrier(values.astype(jnp.bfloat16)).astype(jnp.float32)


def per_device(
    tokens,
    mixer_gain,
    in_weight,
    rate_weight,
    conv_weight,
    decay_log,
    decay_bias,
    out_gain,
    out_weight,
    ffn_gain,
    gate_up_weight,
    down_weight,
    cotangent,
):
    count_rows = tokens.shape[0]
    heads = in_weight.shape[1]
    source = tokens.astype(jnp.float32)
    normed = rms(source, mixer_gain).astype(jnp.bfloat16)
    in_full, rate_full, out_full = (
        lax.all_gather(in_weight, "seq", axis=0, tiled=True),
        lax.all_gather(rate_weight, "seq", axis=0, tiled=True),
        lax.all_gather(out_weight, "seq", axis=0, tiled=True),
    )
    projected = jnp.einsum("td,dhc->thc", normed, in_full, preferred_element_type=jnp.float32)
    rate_pre = jnp.einsum("td,dgh->tgh", normed, rate_full, preferred_element_type=jnp.float32)
    conv_in = lax.optimization_barrier(projected[..., :CONV].astype(jnp.bfloat16))
    gate_pre = projected[..., CONV:]
    rim = from_behind(conv_in[count_rows - (KW - 1) :], "seq", 1)
    padded = jnp.concatenate([rim, conv_in], axis=0).astype(jnp.float32)
    mixed_args = (padded, rate_pre, conv_weight, decay_log, decay_bias)
    queries_raw, keys_raw, values_raw, beta, decay = mixer_inputs(*mixed_args)
    queries = rounded(queries_raw)
    keys = rounded(keys_raw)
    values = rounded(values_raw)
    unit_block = jnp.broadcast_to(jnp.eye(DK, dtype=jnp.float32), (heads, DK, DK))
    zero_block = jnp.zeros((heads, DK, DV), jnp.float32)
    start_joint = jnp.concatenate([unit_block, zero_block], axis=2)
    values_joint = jnp.concatenate(
        [jnp.zeros((count_rows, heads, DK), jnp.float32), values], axis=2
    )
    summary, outputs_joint = run_blocks(start_joint, queries, keys, values_joint, beta, decay)
    transfer = summary[..., :DK]
    offset = summary[..., DK:]
    prefix = carried_in((transfer, offset), "seq", compose, (unit_block, zero_block))
    entering = prefix[1]
    query_map = outputs_joint[..., :DK]
    mixer_out = outputs_joint[..., DK:] + jnp.einsum(
        "thd,hdw->thw", query_map, entering, precision=HIGH
    )
    gated = out_norm(mixer_out, gate_pre, out_gain).astype(jnp.bfloat16)
    branch_part = jnp.einsum("thw,dhw->td", gated, out_full, preferred_element_type=jnp.float32)
    middle = source + lax.psum(branch_part.astype(jnp.bfloat16), "head").astype(jnp.float32)
    second = rms(middle, ffn_gain).astype(jnp.bfloat16)
    gate_up_full, down_full = (
        lax.all_gather(gate_up_weight, "seq", axis=0, tiled=True),
        lax.all_gather(down_weight, "seq", axis=0, tiled=True),
    )
    gate_up = jnp.einsum("td,dgf->tgf", second, gate_up_full, preferred_element_type=jnp.float32)
    hidden = (jax.nn.silu(gate_up[:, 0]) * gate_up[:, 1]).astype(jnp.bfloat16)
    ffn_part = jnp.einsum("tf,df->td", hidden, down_full, preferred_element_type=jnp.float32)
    result = middle + lax.psum(ffn_part.astype(jnp.bfloat16), "head").astype(jnp.float32)
    output = result.astype(jnp.bfloat16)
    gate_up_full, down_full = (
        lax.all_gather(gate_up_weight, "seq", axis=0, tiled=True),
        lax.all_gather(down_weight, "seq", axis=0, tiled=True),
    )
    incoming = cotangent.astype(jnp.float32)
    grad_hidden = jnp.einsum("td,df->tf", cotangent, down_full, preferred_element_type=jnp.float32)
    gate_value = gate_up[:, 0]
    sigmoid_gate = jax.nn.sigmoid(gate_value)
    grad_gate = (
        grad_hidden * gate_up[:, 1] * sigmoid_gate * (1.0 + gate_value * (1.0 - sigmoid_gate))
    )
    grad_up = grad_hidden * gate_value * sigmoid_gate
    grad_gate_up = jnp.stack([grad_gate, grad_up], axis=1).astype(jnp.bfloat16)
    second_part = jnp.einsum(
        "tgf,dgf->td", grad_gate_up, gate_up_full, preferred_element_type=jnp.float32
    )
    grad_second = lax.psum(second_part.astype(jnp.bfloat16), "head").astype(jnp.float32)
    unused_second, second_back = jax.vjp(rms, middle, ffn_gain)
    grad_from_norm, grad_ffn_gain = second_back(grad_second)
    grad_middle = incoming + grad_from_norm
    in_full, rate_full, out_full = (
        lax.all_gather(in_weight, "seq", axis=0, tiled=True),
        lax.all_gather(rate_weight, "seq", axis=0, tiled=True),
        lax.all_gather(out_weight, "seq", axis=0, tiled=True),
    )
    grad_branch = grad_middle.astype(jnp.bfloat16)
    grad_gated = jnp.einsum(
        "td,dhw->thw", grad_branch, out_full, preferred_element_type=jnp.float32
    )
    unused_gated, gate_back = jax.vjp(out_norm, mixer_out, gate_pre, out_gain)
    grad_mixer_out, grad_gate_pre, grad_out_gain = gate_back(grad_gated)
    carried = jnp.einsum("thd,thw->hdw", query_map, grad_mixer_out, precision=HIGH)
    suffix = carried_in_2(
        (jnp.swapaxes(transfer, 1, 2), carried), "seq", compose, (unit_block, zero_block)
    )
    leaving = suffix[1]
    unused_rule, rule_back = jax.vjp(local_rule, queries, keys, values, beta, decay, entering)
    grad_queries, grad_keys, grad_values, grad_beta, grad_decay, unused_state = rule_back(
        (grad_mixer_out, leaving)
    )
    unused_mix, mix_back = jax.vjp(mixer_inputs, *mixed_args)
    grad_padded, grad_rate_pre, grad_conv, grad_decay_log, grad_decay_bias = mix_back(
        (grad_queries, grad_keys, grad_values, grad_beta, grad_decay)
    )
    returned = from_behind(grad_padded[: KW - 1], "seq", -1)
    grad_conv_in = grad_padded[KW - 1 :] + jnp.pad(
        returned, ((count_rows - (KW - 1), 0), (0, 0), (0, 0))
    )
    grad_projected = jnp.concatenate([grad_conv_in, grad_gate_pre], axis=2).astype(jnp.bfloat16)
    grad_rate = grad_rate_pre.astype(jnp.bfloat16)
    normed_part = jnp.einsum(
        "thc,dhc->td", grad_projected, in_full, preferred_element_type=jnp.float32
    )
    normed_part = normed_part + jnp.einsum(
        "tgh,dgh->td", grad_rate, rate_full, preferred_element_type=jnp.float32
    )
    grad_normed, grad_out_gain = (
        lax.psum(normed_part.astype(jnp.bfloat16), "head").astype(jnp.float32),
        lax.psum(grad_out_gain.astype(jnp.bfloat16), "head").astype(jnp.float32),
    )
    unused_first, first_back = jax.vjp(rms, source, mixer_gain)
    grad_source, grad_mixer_gain = first_back(grad_normed)
    grad_tokens = grad_middle + grad_source
    grad_down = jnp.einsum("td,tf->df", cotangent, hidden, preferred_element_type=jnp.float32)
    grad_gate_up_weight = jnp.einsum(
        "td,tgf->dgf", second, grad_gate_up, preferred_element_type=jnp.float32
    )
    grad_out_weight = jnp.einsum(
        "td,thw->dhw", grad_branch, gated, preferred_element_type=jnp.float32
    )
    grad_in_weight = jnp.einsum(
        "td,thc->dhc", normed, grad_projected, preferred_element_type=jnp.float32
    )
    grad_rate_weight = jnp.einsum(
        "td,tgh->dgh", normed, grad_rate, preferred_element_type=jnp.float32
    )
    summed = (
        lax.psum_scatter(
            grad_in_weight.astype(jnp.bfloat16), "seq", scatter_dimension=0, tiled=True
        ).astype(jnp.float32),
        lax.psum_scatter(
            grad_rate_weight.astype(jnp.bfloat16), "seq", scatter_dimension=0, tiled=True
        ).astype(jnp.float32),
        lax.psum_scatter(
            grad_out_weight.astype(jnp.bfloat16), "seq", scatter_dimension=0, tiled=True
        ).astype(jnp.float32),
        lax.psum_scatter(
            grad_gate_up_weight.astype(jnp.bfloat16), "seq", scatter_dimension=0, tiled=True
        ).astype(jnp.float32),
        lax.psum_scatter(
            grad_down.astype(jnp.bfloat16), "seq", scatter_dimension=0, tiled=True
        ).astype(jnp.float32),
    )
    smalls = (
        lax.psum(grad_mixer_gain.astype(jnp.bfloat16), "seq").astype(jnp.float32),
        lax.psum(grad_ffn_gain.astype(jnp.bfloat16), "seq").astype(jnp.float32),
        lax.psum(grad_out_gain.astype(jnp.bfloat16), "seq").astype(jnp.float32),
        lax.psum(grad_conv.astype(jnp.bfloat16), "seq").astype(jnp.float32),
        lax.psum(grad_decay_log.astype(jnp.bfloat16), "seq").astype(jnp.float32),
        lax.psum(grad_decay_bias.astype(jnp.bfloat16), "seq").astype(jnp.float32),
    )
    return (
        output,
        grad_tokens,
        smalls[0],
        summed[0],
        summed[1],
        smalls[3],
        smalls[4],
        smalls[5],
        smalls[2],
        summed[2],
        smalls[1],
        summed[3],
        summed[4],
    )


def solution(mesh):
    in_specs = (
        P("seq", None),
        P(),
        P("seq", "head", None),
        P("seq", None, "head"),
        P(None, "head", None),
        P("head"),
        P("head"),
        P(),
        P("seq", "head", None),
        P(),
        P("seq", None, "head"),
        P("seq", "head"),
        P("seq", None),
    )
    out_specs = (
        P("seq", None),
        P("seq", None),
        P(),
        P("seq", "head", None),
        P("seq", None, "head"),
        P(None, "head", None),
        P("head"),
        P("head"),
        P(),
        P("seq", "head", None),
        P(),
        P("seq", None, "head"),
        P("seq", "head"),
    )
    return jax.shard_map(
        per_device, mesh=mesh, in_specs=in_specs, out_specs=out_specs, check_vma=False
    )
```

profile of v0, /device:TPU:1, one launch (start us, length us, event | category | flops | bytes accessed | tf_op | source)
XLA Modules:
  0.0 1453.2 jit_solution(18023431145449948039)
XLA Ops:
  10.0 28.3 %all_gather.44 = bf16[2048,2,4]{2,1,0:T(2,128)(2,1)S(1)} all-gather(bf16[64,2,4]{2,1,0:T(2,128)(2,1)S(1)} %copy.214), channel_id=1, replica_groups=mesh['seq'=32,'head'=4] {'seq'}, dimensions={0}, use_global_device_ids=true | all-gather | bytes 33792 | tf_op jit(solution)/shard_map/all_gather | solution.py:181
  42.0 36.2 %all-gather.13.cloned.1.call-done = bf16[2048,4,768]{2,0,1:T(8,128)(2,1)} async-done(((bf16[64,4,768]{2,0,1:T(8,128)(2,1)}), bf16[2048,4,768]{2,0,1:T(8,128)(2,1)}) %all-gather.13.cloned.1.call-update) | async-done | bytes 12582928 | tf_op jit(solution)/shard_map/all_gather | solution.py:180
  97.7 136.3 %while.126 = (s32[]{:T(128)}, f32[4,128,384]{2,1,0:T(8,128)S(1)}, f32[4,64,4,384]{3,1,0,2:T(8,128)}, f32[4,64,4]{2,1,0:T(8,128)}, f32[4,64,4,128]{3,1,2,0:T(8,12...) while((s32[]{:T(128)}, f32[4,128,384]{2,1,0:T(8,128)S(1)}, ...), condition=%wide.region_5.6_spmd, body=%wide.region_3.5_spmd.sunk | while | flops 655495232 | bytes 9583861 | solution.py:138
  105.5 21.0 %custom-call.55 = f32[4,1,64,64]{2,3,1,0:T(8,128)} custom-call(f32[4,1,64,64]{3,2,1,0:T(8,128)} %fusion.387), custom_call_target="InvertDiagBlocksLowerTriangular" | custom-call | tf_op jit(solution)/shard_map/while/body/eval_jaxpr/jit(_solve_triangular)/vmap()/triangular_solve | solution.py:97
  139.6 21.0 %custom-call.55 = f32[4,1,64,64]{2,3,1,0:T(8,128)} custom-call(f32[4,1,64,64]{3,2,1,0:T(8,128)} %fusion.387), custom_call_target="InvertDiagBlocksLowerTriangular" | custom-call | tf_op jit(solution)/shard_map/while/body/eval_jaxpr/jit(_solve_triangular)/vmap()/triangular_solve | solution.py:97
  173.6 21.0 %custom-call.55 = f32[4,1,64,64]{2,3,1,0:T(8,128)} custom-call(f32[4,1,64,64]{3,2,1,0:T(8,128)} %fusion.387), custom_call_target="InvertDiagBlocksLowerTriangular" | custom-call | tf_op jit(solution)/shard_map/while/body/eval_jaxpr/jit(_solve_triangular)/vmap()/triangular_solve | solution.py:97
  207.7 21.0 %custom-call.55 = f32[4,1,64,64]{2,3,1,0:T(8,128)} custom-call(f32[4,1,64,64]{3,2,1,0:T(8,128)} %fusion.387), custom_call_target="InvertDiagBlocksLowerTriangular" | custom-call | tf_op jit(solution)/shard_map/while/body/eval_jaxpr/jit(_solve_triangular)/vmap()/triangular_solve | solution.py:97
  237.7 45.2 %all-gather.21.cloned.1.call-done = bf16[128,128,128]{2,1,0:T(8,128)(2,1)} async-done(((bf16[4,128,128]{2,1,0:T(8,128)(2,1)}), bf16[128,128,128]{2,1,0:T(8,128)(2,1)}) %all-gather.21.cloned.1.call-update) | async-done | bytes 4194320 | tf_op jit(solution)/shard_map/all_gather | solution.py:25
  283.0 55.2 %all-gather.23.cloned.1.call-done = bf16[128,128,256]{2,1,0:T(8,128)(2,1)} async-done(((bf16[4,128,256]{2,1,0:T(8,128)(2,1)}), bf16[128,128,256]{2,1,0:T(8,128)(2,1)}) %all-gather.23.cloned.1.call-update) | async-done | bytes 8388624 | tf_op jit(solution)/shard_map/all_gather | solution.py:25
  338.2 84.0 %while.129 = (s32[]{:T(128)}, f32[4,128,256]{2,1,0:T(8,128)S(1)}, s32[]{:T(128)}, bf16[32,4,128,128]{3,2,1,0:T(8,128)(2,1)}, bf16[32,4,128,256]{3,2,1,0:T(8,128)(2,1)}, /*index=5*/s32[]{:T(128)}, s32[]{:T(128)}) while((s32[]{:T(128)}, f32[4,128,256]{2,1,0:T(8,128)S(1)}, s32[]{:T(128)}, bf16[32,4,128,128]{3,2,1,0:T(8,128)(2,1)}, ...), condition=%wide.region_7.8_spmd.clone, body=%wide.region_6.7_spmd.clone.sunk | while | flops 201981952 | bytes 3017319 | solution.py:42
  435.5 41.0 %all-reduce.23.cloned.1.call-done = bf16[256,2048]{1,0:T(8,128)(2,1)} async-done(((bf16[256,2048]{1,0:T(8,128)(2,1)}), bf16[256,2048]{1,0:T(8,128)(2,1)}) %all-reduce.23.cloned.1.call-update) | async-done | bytes 1048592 | tf_op jit(solution)/shard_map/psum | solution.py:212
  478.5 64.2 %all-gather.17.cloned.1.call-done = bf16[2048,2,1408]{2,0,1:T(8,128)(2,1)} async-done(((bf16[64,2,1408]{2,0,1:T(8,128)(2,1)}), bf16[2048,2,1408]{2,0,1:T(8,128)(2,1)}) %all-gather.17.cloned.1.call-update) | async-done | bytes 11534352 | tf_op jit(solution)/shard_map/all_gather | solution.py:215
  542.7 9.8 fusion.253
  552.5 40.6 %all-gather.19.cloned.1.call-done = bf16[2048,1408]{1,0:T(8,128)(2,1)} async-done(((bf16[64,1408]{1,0:T(8,128)(2,1)}), bf16[2048,1408]{1,0:T(8,128)(2,1)}) %all-gather.19.cloned.1.call-update) | async-done | bytes 5767184 | tf_op jit(solution)/shard_map/all_gather | solution.py:216
  612.0 40.5 %all-reduce.25.cloned.1.call-done = bf16[256,2048]{1,0:T(8,128)(2,1)} async-done(((bf16[256,2048]{1,0:T(8,128)(2,1)}), bf16[256,2048]{1,0:T(8,128)(2,1)}) %all-reduce.25.cloned.1.call-update) | async-done | bytes 1048592 | tf_op jit(solution)/shard_map/psum | solution.py:239
  683.3 8.4 copy.271
  691.8 185.2 %while.127 = (s32[]{:T(128)}, f32[4,128,256]{2,1,0:T(8,128)S(1)}, f32[4,4,64,64]{3,2,1,0:T(8,128)}, f32[4,4,64,128]{3,2,1,0:T(8,128)}, f32[4,4,64,64]{3,2,1,0:T(...) while((s32[]{:T(128)}, f32[4,128,256]{2,1,0:T(8,128)S(1)}, ...), condition=%wide.region_19.20_spmd.clone.clone, body=%wide.region_17.19_spmd.clone.clone.sunk | while | flops 403722304 | bytes 8961033 | solution.py:138
  703.5 21.0 %custom-call.56 = f32[4,1,64,64]{2,3,1,0:T(8,128)} custom-call(f32[4,1,64,64]{3,2,1,0:T(8,128)} %add_bitcast_fusion.4), custom_call_target="InvertDiagBlocksLowerTriangular" | custom-call | tf_op jit(solution)/shard_map/jvp()/while/body/eval_jaxpr/jit(_solve_triangular)/vmap()/triangular_solve | solution.py:97
  749.7 21.0 %custom-call.56 = f32[4,1,64,64]{2,3,1,0:T(8,128)} custom-call(f32[4,1,64,64]{3,2,1,0:T(8,128)} %add_bitcast_fusion.4), custom_call_target="InvertDiagBlocksLowerTriangular" | custom-call | tf_op jit(solution)/shard_map/jvp()/while/body/eval_jaxpr/jit(_solve_triangular)/vmap()/triangular_solve | solution.py:97
  795.9 21.0 %custom-call.56 = f32[4,1,64,64]{2,3,1,0:T(8,128)} custom-call(f32[4,1,64,64]{3,2,1,0:T(8,128)} %add_bitcast_fusion.4), custom_call_target="InvertDiagBlocksLowerTriangular" | custom-call | tf_op jit(solution)/shard_map/jvp()/while/body/eval_jaxpr/jit(_solve_triangular)/vmap()/triangular_solve | solution.py:97
  842.2 21.0 %custom-call.56 = f32[4,1,64,64]{2,3,1,0:T(8,128)} custom-call(f32[4,1,64,64]{3,2,1,0:T(8,128)} %add_bitcast_fusion.4), custom_call_target="InvertDiagBlocksLowerTriangular" | custom-call | tf_op jit(solution)/shard_map/jvp()/while/body/eval_jaxpr/jit(_solve_triangular)/vmap()/triangular_solve | solution.py:97
  877.0 9.8 convolution_convert_fusion
  893.0 50.6 %while.130 = (s32[]{:T(128)}, f32[4,128,256]{2,1,0:T(8,128)S(1)}, s32[]{:T(128)}, bf16[32,4,128,128]{3,2,1,0:T(8,128)(2,1)}, bf16[32,4,128,256]{3,2,1,0:T(8,128)...) while((s32[]{:T(128)}, f32[4,128,256]{2,1,0:T(8,128)S(1)}, s32[]{:T(128)}, ...), condition=%wide.region_16.17_spmd.clone, body=%wide.region_15.16_spmd.clone.sunk | while | flops 201981952 | bytes 3017381 | solution.py:66
  947.1 205.1 %while.128 = (s32[]{:T(128)}, f32[4,128,256]{2,1,0:T(8,128)S(1)}, f32[4,64,4,128]{3,1,0,2:T(8,128)}, f32[4,64,4,128]{3,1,0,2:T(8,128)}, f32[4,64,4,256]{3,1,0,2:...) while((s32[]{:T(128)}, f32[4,128,256]{2,1,0:T(8,128)S(1)}, ...), condition=%wide.region_31.32_spmd.clone.clone, body=%wide.region_20.31_spmd.clone.clone.sunk | while | flops 921023552 | bytes 27009296 | solution.py:138
  959.1 19.7 %custom-call.57 = f32[4,1,64,64]{2,3,1,0:T(8,128)S(1)} custom-call(f32[4,1,64,64]{3,2,1,0:T(8,128)S(1)} %add_bitcast_fusion.5), custom_call_target="InvertDiagBlocksLowerTriangular" | custom-call | tf_op jit(solution)/shard_map/transpose(jvp())/while/body/eval_jaxpr/jit(_solve_triangular)/vmap()/triangular_solve | solution.py:97
  1010.4 19.7 %custom-call.57 = f32[4,1,64,64]{2,3,1,0:T(8,128)S(1)} custom-call(f32[4,1,64,64]{3,2,1,0:T(8,128)S(1)} %add_bitcast_fusion.5), custom_call_target="InvertDiagBlocksLowerTriangular" | custom-call | tf_op jit(solution)/shard_map/transpose(jvp())/while/body/eval_jaxpr/jit(_solve_triangular)/vmap()/triangular_solve | solution.py:97
  1061.7 19.7 %custom-call.57 = f32[4,1,64,64]{2,3,1,0:T(8,128)S(1)} custom-call(f32[4,1,64,64]{3,2,1,0:T(8,128)S(1)} %add_bitcast_fusion.5), custom_call_target="InvertDiagBlocksLowerTriangular" | custom-call | tf_op jit(solution)/shard_map/transpose(jvp())/while/body/eval_jaxpr/jit(_solve_triangular)/vmap()/triangular_solve | solution.py:97
  1112.9 19.7 %custom-call.57 = f32[4,1,64,64]{2,3,1,0:T(8,128)S(1)} custom-call(f32[4,1,64,64]{3,2,1,0:T(8,128)S(1)} %add_bitcast_fusion.5), custom_call_target="InvertDiagBlocksLowerTriangular" | custom-call | tf_op jit(solution)/shard_map/transpose(jvp())/while/body/eval_jaxpr/jit(_solve_triangular)/vmap()/triangular_solve | solution.py:97
  1171.8 9.0 fusion.194
  1205.7 39.9 %reduce-scatter.16.cloned.1.call-done = bf16[64,8]{1,0:T(8,128)(2,1)} async-done(((bf16[2048,8]{1,0:T(8,128)(2,1)}), bf16[64,8]{1,0:T(8,128)(2,1)}) %reduce-scatter.16.cloned.1.call-update) | async-done | bytes 1040
  1247.0 61.4 %all-reduce.27.cloned.1.call-done = (bf16[256,2048]{1,0:T(8,128)(2,1)}, bf16[256,2048]{1,0:T(8,128)(2,1)}) async-done(((bf16[256,2048]{1,0:T(8,128)(2,1)}, bf16[256,2048]{1,0:T(8,128)(2,1)}), (bf16[256,2048]{1,0:T(8,128)(2,1)}, bf16[256,2048]{1,0:T(8,128)(2,1)})) %all-reduce.27.cloned.1.call-update) | async-done | bytes 2097168 | tf_op jit(solution)/shard_map/psum | solution.py:221
  1310.6 125.1 %all-reduce.17 = (bf16[2048]{0:T(1024)(128)(2,1)S(1)}, bf16[4,4,512]{2,1,0:T(4,128)(2,1)S(1)}, bf16[4]{0:T(256)(128)(2,1)S(1)}, bf16[4]{0:T(256)(128)(2,1)S(1)},...) all-reduce(bf16[2048]{0:T(1024)(128)(2,1)S(1)} %get-tuple-element.1, ...), channel_id=1, replica_groups=mesh['seq'=32,'head'=4] {'seq'}, use_global_device_ids=true, to_apply=%region_37.38 | all-reduce | flops 12552 | bytes 50208 | tf_op jit(solution)/shard_map/psum | solution.py:317
  (841 shorter events, 573.1 us)
Async XLA Ops:
  7.2 71.0 %all-gather.13.cloned.1.call-start = ((), (), s32[]{:S(2)}) async-start(), calls=%async_computation.5 | async-start | bytes 12976128 | tf_op jit(solution)/shard_map/all_gather | solution.py:180
  9.1 273.8 %all-gather.21.cloned.1.call-start = ((), (), s32[]{:S(2)}) async-start(), calls=%async_computation.14 | async-start | bytes 4325376 | tf_op jit(solution)/shard_map/all_gather | solution.py:25
  41.2 50.1 %copy-start.40 = (f32[4,512]{1,0:T(4,128)}, f32[4,512]{1,0:T(4,128)S(1)}, u32[]{:S(2)}) copy-start(f32[4,512]{1,0:T(4,128)S(1)} %get-tuple-element.2177) | copy-start | bytes 24580
  41.2 50.1 %copy-start.42 = (f32[4,512]{1,0:T(4,128)}, f32[4,512]{1,0:T(4,128)S(1)}, u32[]{:S(2)}) copy-start(f32[4,512]{1,0:T(4,128)S(1)} %get-tuple-element.2178) | copy-start | bytes 24580
  41.2 50.1 %copy-start.44 = (f32[4,512]{1,0:T(4,128)}, f32[4,512]{1,0:T(4,128)S(1)}, u32[]{:S(2)}) copy-start(f32[4,512]{1,0:T(4,128)S(1)} %get-tuple-element.2179) | copy-start | bytes 24580
  86.8 3.6 collective-permute-start
  234.7 103.4 %all-gather.23.cloned.1.call-start = ((), (), s32[]{:S(2)}) async-start(), calls=%async_computation.15 | async-start | bytes 8650752 | tf_op jit(solution)/shard_map/all_gather | solution.py:25
  236.0 192.2 %all-gather.15.cloned.1.call-start = ((), (), s32[]{:S(2)}) async-start(), calls=%async_computation.6 | async-start | bytes 4325376 | tf_op jit(solution)/shard_map/all_gather | solution.py:182
  237.7 238.8 %all-reduce.23.cloned.1.call-start = ((), (), s32[]{:S(2)}) async-start(), calls=%async_computation.7 | async-start | bytes 2097152 | tf_op jit(solution)/shard_map/psum | solution.py:212
  432.9 109.8 %copy-start.38 = (f32[2048]{0:T(1024)S(1)}, f32[2048]{0:T(1024)}, u32[]{:S(2)}) copy-start(f32[2048]{0:T(1024)} %param.32) | copy-start | bytes 24580
  432.9 109.8 %all-gather.17.cloned.1.call-start = ((), (), s32[]{:S(2)}) async-start(), calls=%async_computation.8 | async-start | bytes 11894784 | tf_op jit(solution)/shard_map/all_gather | solution.py:215
  434.7 158.3 %all-gather.19.cloned.1.call-start = ((), (), s32[]{:S(2)}) async-start(), calls=%async_computation.9 | async-start | bytes 5947392 | tf_op jit(solution)/shard_map/all_gather | solution.py:216
  435.5 217.1 %all-reduce.25.cloned.1.call-start = ((), (), s32[]{:S(2)}) async-start(), calls=%async_computation.10 | async-start | bytes 2097152 | tf_op jit(solution)/shard_map/psum | solution.py:239
  478.5 190.2 %copy-start.63 = (f32[256]{0:T(256)}, f32[256]{0:T(256)S(1)}, u32[]{:S(2)}) copy-start(f32[256]{0:T(256)S(1)} %fusion.247) | copy-start | bytes 3076
  609.4 283.6 %all-gather.25.cloned.1.call-start = ((), (), s32[]{:S(2)}) async-start(), calls=%async_computation.16 | async-start | bytes 4325376 | tf_op jit(solution)/shard_map/all_gather | solution.py:48
  611.8 281.2 %all-gather.27.cloned.1.call-start = ((), (), s32[]{:S(2)}) async-start(), calls=%async_computation.17 | async-start | bytes 8650752 | tf_op jit(solution)/shard_map/all_gather | solution.py:48
  668.6 529.3 %reduce-scatter.12.cloned.1.call-start = ((), (), s32[]{:S(2)}) async-start(), calls=%async_computation.12 | async-start | bytes 4325376 | tf_op jit(solution)/shard_map/reduce_scatter | solution.py:306
  674.9 524.6 %reduce-scatter.18.cloned.1.call-start = ((), (), s32[]{:S(2)}) async-start(), calls=%async_computation.19 | async-start | bytes 5947392
  691.7 510.0 %reduce-scatter.14.cloned.1.call-start = ((), (), s32[]{:S(2)}) async-start(), calls=%async_computation.13 | async-start | bytes 11894784 | tf_op jit(solution)/shard_map/reduce_scatter | solution.py:309
  886.9 358.7 %reduce-scatter.16.cloned.1.call-start = ((), (), s32[]{:S(2)}) async-start(), calls=%async_computation.18 | async-start | bytes 540672
  1160.8 8.9 collective-permute-start.1
  1169.6 138.7 %all-reduce.27.cloned.1.call-start = ((), (), s32[]{:S(2)}) async-start(), calls=%async_computation.20 | async-start | bytes 4194304 | tf_op jit(solution)/shard_map/psum | solution.py:221
  1180.8 263.6 %reduce-scatter.10.cloned.1.call-start = ((), (), s32[]{:S(2)}) async-start(), calls=%async_computation.11 | async-start | bytes 12976128 | tf_op jit(solution)/shard_map/reduce_scatter | solution.py:300
  1200.7 238.5 %copy-start.9 = (bf16[256,2048]{1,0:T(8,128)(2,1)S(1)}, bf16[256,2048]{1,0:T(8,128)(2,1)}, u32[]{:S(2)}) copy-start(bf16[256,2048]{1,0:T(8,128)(2,1)} %all-reduce.23.cloned.1.call-done) | copy-start | bytes 3145732
  1200.7 238.5 %copy-start.20 = (bf16[256,2048]{1,0:T(8,128)(2,1)S(1)}, bf16[256,2048]{1,0:T(8,128)(2,1)}, u32[]{:S(2)}) copy-start(bf16[256,2048]{1,0:T(8,128)(2,1)} %param.35) | copy-start | bytes 3145732
  1200.7 238.5 %copy-start.39 = (f32[2048]{0:T(1024)S(1)}, f32[2048]{0:T(1024)}, u32[]{:S(2)}) copy-start(f32[2048]{0:T(1024)} %param.32) | copy-start | bytes 24580
  1201.6 109.0 %copy-start.65 = (bf16[2048]{0:T(1024)(128)(2,1)S(1)}, bf16[2048]{0:T(1024)(128)(2,1)}, u32[]{:S(2)}) copy-start(bf16[2048]{0:T(1024)(128)(2,1)} %get-tuple-element.1934) | copy-start | bytes 12292
  1201.6 109.0 %copy-start.75 = (bf16[256]{0:T(256)(128)(2,1)S(1)}, bf16[256]{0:T(256)(128)(2,1)}, u32[]{:S(2)}) copy-start(bf16[256]{0:T(256)(128)(2,1)} %psum.85) | copy-start | bytes 1540
  1201.6 237.5 %copy-start.67 = (f32[256]{0:T(256)S(1)}, f32[256]{0:T(256)}, u32[]{:S(2)}) copy-start(f32[256]{0:T(256)} %copy-done.66) | copy-start | bytes 3076
  1201.6 237.5 %copy-start.62 = (f32[256]{0:T(256)S(1)}, f32[256]{0:T(256)}, u32[]{:S(2)}) copy-start(f32[256]{0:T(256)} %copy-done.60) | copy-start | bytes 3076
  1201.6 237.6 %copy-start.64 = (f32[256]{0:T(256)S(1)}, f32[256]{0:T(256)}, u32[]{:S(2)}) copy-start(f32[256]{0:T(256)} %copy-done.63) | copy-start | bytes 3076
  1201.7 237.6 %copy-start.74 = (f32[256]{0:T(256)S(1)}, f32[256]{0:T(256)}, u32[]{:S(2)}) copy-start(f32[256]{0:T(256)} %copy-done.73) | copy-start | bytes 3076
  (82 other events, 627.6 us)
Sparse Core Ops, SparseCore 0:
  10.9 67.2 all-gather.12
  234.9 48.0 all-gather.20
  285.8 52.3 all-gather.22
  341.0 45.8 all-gather.14
  433.0 43.4 all-reduce.22
  479.5 63.1 all-gather.16
  545.2 47.8 all-gather.18
  609.5 43.0 all-reduce.24
  654.9 49.0 all-gather.24
  706.6 52.7 all-gather.26
  763.1 79.9 reduce-scatter.11
  847.1 84.7 reduce-scatter.17
  935.7 101.0 reduce-scatter.13
  1169.8 75.7 reduce-scatter.15
  1248.6 59.7 all-reduce.26
  1312.1 103.2 reduce-scatter.9
where the time goes:
time: 1470 us; the launch traced here: 1450 us
  waiting for transfers between devices  425 us (29%)
  matrix products  383 us (26%)
  other arithmetic  326 us (22%)
  blocking collectives  162 us (11%)
  local copies, waits for them, and re-layouts  130 us (9%)
  between operations  15.3 us (1%)
    another operation x52, other arithmetic, group_rule(): jax.scipy.linalg.solve_triangular(lower + identity, targets, lower=True,...  260 us
    psum x1, blocking collectives, per_device(): lax.psum(grad_mixer_gain.astype(jnp.bfloat16), 'seq').astype(jnp.float32)  125 us
    dot_general x64, matrix products, compose(): jnp.einsum('hij,hjk->hik', later[0], earlier[1], precision=HIGH) + later[1]  106 us
    all_gather x2, waiting for transfers between devices, carried_in(): lax.all_gather(part.astype(kind), axis)  100 us
    all_gather x1, waiting for transfers between devices, per_device(): lax.all_gather(gate_up_weight, 'seq', axis=0, tiled=True)  64.2 us
    psum x1, waiting for transfers between devices, per_device(): lax.psum(ffn_part.astype(jnp.bfloat16), 'head').astype(jnp.float32)  61.4 us
    psum x1, waiting for transfers between devices, per_device(): lax.psum(branch_part.astype(jnp.bfloat16), 'head').astype(jnp.float32)  41 us
    unnamed x18, waiting for transfers between devices  40.8 us
  transfers between devices with their start and end apart: 18, of which 9 were waited for; matrix products, arithmetic and copies ran while one was open for 45% of the time, Pallas kernels for 0%

commit v1 on v0

v1 whole, which is shorter than its diff:
```python
import functools

import jax
import jax.numpy as jnp
from jax import lax
from jax.experimental import pallas as pl
from jax.experimental.pallas import tpu as pltpu
from jax.sharding import PartitionSpec as P

DK = 128
DV = 256
KW = 4
CONV = 512
PROJ = 768
LANES = 128
HALO = 8
HALVES = DV // DK
MESH = pl.DeviceIdType.MESH

F32 = jnp.float32
BF16 = jnp.bfloat16
EXACT = lax.Precision.HIGHEST
FINE = lax.Precision.HIGH
VMEM_LIMIT = 56 * 1024 * 1024


def dot(a, b, dims, precision=None):
    return lax.dot_general(a, b, (dims, ((), ())), precision=precision, preferred_element_type=F32)


def mm(a, b, precision=None):
    return dot(a, b, ((1,), (0,)), precision)


def mmt(a, b, precision=None):
    return dot(a, b, ((1,), (1,)), precision)


def mtm(a, b, precision=None):
    return dot(a, b, ((0,), (0,)), precision)


def iota(shape, dim):
    return lax.broadcasted_iota(jnp.int32, shape, dim)


def softplus(x):
    return jnp.maximum(x, 0.0) + jnp.log1p(jnp.exp(-jnp.abs(x)))


def column(block, index):
    lanes = iota(block.shape, 1)
    return jnp.sum(jnp.where(lanes == index, block, 0.0), axis=1, keepdims=True)


def triangles(size):
    rows, columns = iota((size, size), 0), iota((size, size), 1)
    return rows, columns


def gates(rates, scales, head, heads):
    size = rates.shape[0]
    log_rate = column(scales[0:1], head)
    bias = column(scales[1:2], head)
    pre = column(rates, head) + bias
    beta = jax.nn.sigmoid(column(rates, heads + head))
    decay = -jnp.exp(log_rate) * softplus(pre)
    rows, columns = triangles(size)
    below = (columns <= rows).astype(F32)
    gamma_wide = mm(below, jnp.broadcast_to(decay, (size, LANES)), EXACT)
    gamma = gamma_wide[:, 0:1]
    gamma_row = gamma_wide.T[0:1, :]
    return beta, decay, gamma, gamma_row, pre


def decays_of(gamma, gamma_row):
    size = gamma.shape[0]
    rows, columns = triangles(size)
    inside = columns <= rows
    return jnp.where(inside, jnp.exp(jnp.where(inside, gamma - gamma_row, 0.0)), 0.0)


def inverse(lower):
    size = lower[0].shape[0]
    rows, columns = triangles(size)
    unit = (rows == columns).astype(F32)
    known = [unit - jnp.where(rows // 2 == columns // 2, a, 0.0) for a in lower]
    width = 2
    while width < size:
        fresh = (rows // (2 * width) == columns // (2 * width)) & (rows // width != columns // width)
        parts = [jnp.where(fresh, a, 0.0) for a in lower]
        first = [mm(c, x, FINE) for c, x in zip(parts, known)]
        known = [x - mm(x, y, FINE) for x, y in zip(known, first)]
        width *= 2
    return known


def convolved(extended, taps):
    length = extended.shape[0]
    total = None
    for j in range(KW):
        shift = KW - 1 - j
        moved = extended if shift == 0 else pltpu.roll(extended, shift, 0)
        term = taps[j : j + 1] * moved[HALO:]
        total = term if total is None else total + term
    return total


def unit_rows(values):
    return lax.rsqrt(jnp.sum(values * values, axis=-1, keepdims=True) + 1e-06)


def mixer_inputs(projected, taps):
    extended = projected[:, :CONV].astype(BF16).astype(F32)
    mixed = convolved(extended, taps)
    gate = jax.nn.sigmoid(mixed)
    active = mixed * gate
    q_raw, k_raw = active[:, :DK], active[:, DK : 2 * DK]
    q_scale, k_scale = unit_rows(q_raw), unit_rows(k_raw)
    queries = (q_raw * q_scale * DK ** (-0.5)).astype(BF16)
    keys = (k_raw * k_scale).astype(BF16)
    values = active[:, 2 * DK :].astype(BF16)
    return extended, mixed, gate, (q_raw, q_scale), (k_raw, k_scale), queries, keys, values


def local_forward(heads, proj_ref, taps_ref, scales_ref, q_ref, k_ref, v_ref, inv_ref, out_ref, map_ref, sum_ref):
    size = proj_ref.shape[0] - HALO
    rows, columns = triangles(size)
    rates = proj_ref[HALO:, heads * PROJ :]
    scales = scales_ref[...]
    lower, kept = [], []
    for h in range(heads):
        projected = proj_ref[:, h * PROJ : h * PROJ + CONV]
        taps = taps_ref[:, h * CONV : (h + 1) * CONV]
        *_, queries, keys, values = mixer_inputs(projected, taps)
        q_ref[h], k_ref[h], v_ref[h] = queries, keys, values
        beta, decay, gamma, gamma_row, _ = gates(rates, scales, h, heads)
        spread = decays_of(gamma, gamma_row)
        lower.append(jnp.where(columns < rows, beta * spread * mmt(keys, keys), 0.0))
        kept.append((queries, keys, values, beta, gamma, spread))
    inverses = inverse(lower)
    for h in range(heads):
        queries, keys, values, beta, gamma, spread = kept[h]
        inv_ref[h] = inverses[h]
        growth = jnp.exp(gamma)
        targets = jnp.concatenate([growth * beta * keys.astype(F32), beta * values.astype(F32)], axis=1)
        written = mm(inverses[h], targets, FINE)
        scores = spread * mmt(queries, keys)
        through = mm(scores, written, FINE)
        map_ref[h] = growth * queries.astype(F32) - through[:, :DK]
        out_ref[h] = through[:, DK:]
        final = gamma[size - 1 : size]
        faded = jnp.exp(final - gamma) * keys.astype(F32)
        summary = mtm(faded, written, FINE)
        unit = (iota((DK, DK), 0) == iota((DK, DK), 1)).astype(F32)
        passed = (jnp.exp(final) * unit - summary[:, :DK]).astype(BF16)
        for half in range(HALVES):
            sum_ref[HALVES * h + half, :, :DK] = passed
            sum_ref[HALVES * h + half, :, DK:] = summary[:, (half + 1) * DK : (half + 2) * DK].astype(BF16)


def whole_state(units_ref, head):
    return jnp.concatenate([units_ref[HALVES * head + half] for half in range(HALVES)], axis=1).astype(F32)


def mix_outputs(heads, out_ref, map_ref, state_ref, proj_ref, gain_ref, mixed_ref, gated_ref):
    gain = gain_ref[...]
    for h in range(heads):
        mixer_out = out_ref[h] + mm(map_ref[h], whole_state(state_ref, h), FINE)
        mixed_ref[h] = mixer_out
        gate = proj_ref[HALO:, h * PROJ + CONV : (h + 1) * PROJ]
        scale = lax.rsqrt(jnp.mean(mixer_out * mixer_out, axis=-1, keepdims=True) + 1e-05)
        gated = mixer_out * scale * gain * (gate * jax.nn.sigmoid(gate))
        gated_ref[:, h * DV : (h + 1) * DV] = gated.astype(BF16)


def mix_outputs_back(heads, grad_ref, mixed_ref, map_ref, proj_ref, gain_ref, grad_mixed_ref, grad_gate_ref, grad_gain_ref, carried_ref):
    gain = gain_ref[...]
    total = jnp.zeros_like(gain)
    for h in range(heads):
        grad = grad_ref[:, h * DV : (h + 1) * DV]
        mixer_out = mixed_ref[h]
        z = proj_ref[HALO:, h * PROJ + CONV : (h + 1) * PROJ]
        scale = lax.rsqrt(jnp.mean(mixer_out * mixer_out, axis=-1, keepdims=True) + 1e-05)
        normal = mixer_out * scale
        s = jax.nn.sigmoid(z)
        silu = z * s
        total = total + jnp.sum(grad * normal * silu, axis=0, keepdims=True)
        grad_gate_ref[:, h * DV : (h + 1) * DV] = (grad * normal * gain * s * (1.0 + z * (1.0 - s))).astype(BF16)
        u = grad * gain * silu
        grad_mixed = scale * u - normal * (scale * jnp.mean(u * normal, axis=-1, keepdims=True))
        grad_mixed_ref[h] = grad_mixed
        carried = mtm(map_ref[h], grad_mixed, FINE).astype(BF16)
        for half in range(HALVES):
            carried_ref[HALVES * h + half] = carried[:, half * DK : (half + 1) * DK]
    grad_gain_ref[...] = total


def norm_back(grad, values, scale):
    return scale * grad - values * (scale * scale * scale * jnp.sum(values * grad, axis=-1, keepdims=True))


def local_backward(
    heads, proj_ref, taps_ref, scales_ref, q_ref, k_ref, v_ref, inv_ref, grad_ref, state_ref, leaving_ref, gate_ref,
    out_ref, halo_ref, tail_ref, taps_out_ref, scales_out_ref,
):
    size = proj_ref.shape[0] - HALO
    rows, columns = triangles(size)
    rates = proj_ref[HALO:, heads * PROJ :]
    scales = scales_ref[...]
    lanes = iota((size, LANES), 1)
    grad_rates = jnp.zeros((size, LANES), F32)
    rates_total = jnp.zeros((8, LANES), F32)
    row8, lane8 = iota((8, LANES), 0), iota((8, LANES), 1)
    ones = jnp.ones((size, LANES), F32)
    above = (columns >= rows).astype(F32)
    for h in range(heads):
        queries, keys, values = q_ref[h], k_ref[h], v_ref[h]
        qf, kf, vf = queries.astype(F32), keys.astype(F32), values.astype(F32)
        beta, decay, gamma, gamma_row, pre = gates(rates, scales, h, heads)
        spread = decays_of(gamma, gamma_row)
        strict = columns < rows
        growth = jnp.exp(gamma)
        final = gamma[size - 1 : size]
        fade = jnp.exp(final - gamma)
        state, leaving = whole_state(state_ref, h), whole_state(leaving_ref, h)
        inv, grad = inv_ref[h], grad_ref[h]
        products = mmt(keys, keys)
        scores = spread * mmt(queries, keys)
        lower = jnp.where(strict, beta * spread * products, 0.0)
        residual = vf - growth * mm(kf, state, FINE)
        written = mm(inv, beta * residual, FINE)
        faded = fade * kf
        grad_written = mtm(scores, grad, FINE) + mm(faded, leaving, FINE)
        grad_scores = mmt(grad, written, FINE)
        grad_targets = mtm(inv, grad_written, FINE)
        grad_lower = jnp.where(strict, -mmt(grad_targets, written, FINE), 0.0)
        grad_values = beta * grad_targets
        grad_beta = jnp.sum(grad_targets * residual, axis=-1, keepdims=True)
        grad_beta = grad_beta + jnp.sum(grad_lower * spread * products, axis=-1, keepdims=True)
        q_first = growth * mmt(grad, state, FINE)
        k_first = -growth * mmt(grad_values, state, FINE)
        spread_scores = spread * grad_scores
        spread_lower = grad_lower * beta * spread
        grad_faded = mmt(written, leaving, FINE)
        grad_queries = q_first + mm(spread_scores, kf, FINE)
        grad_keys = (
            k_first
            + mtm(spread_scores, qf, FINE)
            + mm(spread_lower, kf, FINE)
            + mtm(spread_lower, kf, FINE)
            + fade * grad_faded
        )
        energy = grad_scores * scores + grad_lower * lower
        fading = jnp.sum(grad_faded * faded, axis=-1, keepdims=True)
        grad_gamma = jnp.sum(qf * q_first + kf * k_first, axis=-1, keepdims=True) - fading
        grad_gamma = grad_gamma + jnp.sum(energy, axis=-1, keepdims=True)
        at_end = jnp.sum(fading, axis=0, keepdims=True) + jnp.exp(final) * jnp.sum(
            jnp.sum(state * leaving, axis=1, keepdims=True), axis=0, keepdims=True
        )
        grad_gamma = grad_gamma + jnp.where(iota((size, 1), 0) == size - 1, at_end, 0.0)
        wide = jnp.broadcast_to(grad_gamma, (size, LANES)) - mtm(energy, ones, EXACT)
        grad_decay = mm(above, wide, EXACT)[:, 0:1]

        projected = proj_ref[:, h * PROJ : h * PROJ + CONV]
        taps = taps_ref[:, h * CONV : (h + 1) * CONV]
        extended, mixed, gate, (q_raw, q_scale), (k_raw, k_scale), *_ = mixer_inputs(projected, taps)
        grad_active = jnp.concatenate(
            [
                norm_back(grad_queries * DK ** (-0.5), q_raw, q_scale),
                norm_back(grad_keys, k_raw, k_scale),
                grad_values,
            ],
            axis=1,
        )
        grad_mixed = grad_active * gate * (1.0 + mixed * (1.0 - gate))
        padding = jnp.zeros((HALO, CONV), F32)
        full = jnp.concatenate([padding, grad_mixed, padding], axis=0)
        total = None
        for j in range(KW):
            shift = KW - 1 - j
            moved = full if shift == 0 else pltpu.roll(full, size + 2 * HALO - shift, 0)
            term = taps[j : j + 1] * moved[: size + HALO]
            total = term if total is None else total + term
            back = extended if shift == 0 else pltpu.roll(extended, shift, 0)
            taps_out_ref[j : j + 1, h * CONV : (h + 1) * CONV] = jnp.sum(
                grad_mixed * back[HALO:], axis=0, keepdims=True
            )
        halo_ref[:, h * CONV : (h + 1) * CONV] = total[:HALO]
        tail_ref[:, h * CONV : (h + 1) * CONV] = total[size:]
        out_ref[:, h * PROJ : h * PROJ + CONV] = total[HALO:].astype(BF16)
        out_ref[:, h * PROJ + CONV : (h + 1) * PROJ] = gate_ref[:, h * DV : (h + 1) * DV]

        grad_pre = -jnp.exp(column(scales[0:1], h)) * jax.nn.sigmoid(pre) * grad_decay
        grad_strength = grad_beta * beta * (1.0 - beta)
        grad_rates = grad_rates + jnp.where(lanes == h, grad_pre, 0.0)
        grad_rates = grad_rates + jnp.where(lanes == heads + h, grad_strength, 0.0)
        log_total = jnp.sum(grad_decay * decay, axis=0, keepdims=True)
        bias_total = jnp.sum(grad_pre, axis=0, keepdims=True)
        rates_total = rates_total + jnp.where((row8 == 0) & (lane8 == h), log_total, 0.0)
        rates_total = rates_total + jnp.where((row8 == 1) & (lane8 == h), bias_total, 0.0)
    out_ref[:, heads * PROJ :] = grad_rates.astype(BF16)
    scales_out_ref[...] = rates_total


def start_barrier(peers):
    barrier = pltpu.get_barrier_semaphore()
    for peer in peers:
        pl.semaphore_signal(barrier, inc=1, device_id=peer, device_id_type=MESH)
    pl.semaphore_wait(barrier, len(peers))


def send(source, target, sends, receives, slot, peer):
    copy = pltpu.make_async_remote_copy(
        src_ref=source,
        dst_ref=target,
        send_sem=sends.at[slot],
        recv_sem=receives.at[slot],
        device_id=peer,
        device_id_type=MESH,
    )
    copy.start()
    return copy


def twice(left, right):
    high = right.astype(BF16)
    low = (right - high.astype(F32)).astype(BF16)
    return mm(left, high) + mm(left, low)


def scan_places(members, groups):
    seq, head = lax.axis_index("seq"), lax.axis_index("head")
    member, group = seq % members, seq // members
    near = [(member + d) % members for d in range(members)]
    far = [(group + d) % groups for d in range(groups)]
    near_ids = [(group * members + place, head) for place in near]
    far_ids = [(place * members + member, head) for place in far]
    return member, group, near, near_ids, far_ids


def scan_forward(
    groups, pack_ref, out_ref, kept_ref, totals_ref, near_in, before, far_out, far_in, back_out, back_in,
    near_s, near_r, far_s, far_r, back_s, back_r,
):
    members = pack_ref.shape[0]
    member, group, near, near_ids, far_ids = scan_places(members, groups)
    start_barrier(near_ids[1:] + far_ids[1:])
    copies = [
        send(pack_ref.at[near[d]], near_in.at[member], near_s, near_r, d, near_ids[d]) for d in range(1, members)
    ]
    near_in[member] = pack_ref[member]
    for copy in copies:
        copy.wait()
    unit = (iota((DK, DK), 0) == iota((DK, DK), 1)).astype(F32)
    total = jnp.concatenate([unit, jnp.zeros((DK, DK), F32)], axis=1)
    for j in range(members):
        before[j] = total
        kept_ref[j] = near_in[j, :, :DK]
        moved = twice(near_in[j, :, :DK], total)
        total = jnp.concatenate([moved[:, :DK], moved[:, DK:] + near_in[j, :, DK:].astype(F32)], axis=1)
    far_out[...] = total.astype(BF16)
    copies = [send(far_out, far_in.at[group], far_s, far_r, d, far_ids[d]) for d in range(1, groups)]
    far_in[group] = far_out[...]
    for copy in copies:
        copy.wait()
    state = jnp.zeros((DK, DK), F32)
    for j in range(groups):
        totals_ref[j] = far_in[j, :, :DK]
        fresh = twice(far_in[j, :, :DK], state) + far_in[j, :, DK:].astype(F32)
        state = jnp.where(j < group, fresh, state)
    for j in range(members):
        back_out[j] = (mm(before[j, :, :DK], state, FINE) + before[j, :, DK:]).astype(BF16)
    copies = [
        send(back_out.at[near[d]], back_in.at[member], back_s, back_r, d, near_ids[d]) for d in range(1, members)
    ]
    back_in[member] = back_out[member]
    for copy in copies:
        copy.wait()
    out_ref[...] = back_in[...]


def scan_backward(
    groups, pack_ref, kept_ref, totals_ref, out_ref, near_in, turned, before, after, far_out, far_in, back_out, back_in,
    near_s, near_r, far_s, far_r, back_s, back_r,
):
    members = pack_ref.shape[0]
    member, group, near, near_ids, far_ids = scan_places(members, groups)
    start_barrier(near_ids[1:] + far_ids[1:])
    copies = [
        send(pack_ref.at[near[d]], near_in.at[member], near_s, near_r, d, near_ids[d]) for d in range(1, members)
    ]
    near_in[member] = pack_ref[member]
    passed = (iota((DK, DK), 0) == iota((DK, DK), 1)).astype(F32)
    for j in reversed(range(members)):
        turned[j] = kept_ref[j].astype(F32).T.astype(BF16)
        before[j] = passed
        passed = twice(turned[j], passed)
    for copy in copies:
        copy.wait()
    total = jnp.zeros((DK, DK), F32)
    for j in reversed(range(members)):
        after[j] = total
        total = twice(turned[j], total) + near_in[j].astype(F32)
    far_out[...] = total.astype(BF16)
    copies = [send(far_out, far_in.at[group], far_s, far_r, d, far_ids[d]) for d in range(1, groups)]
    far_in[group] = far_out[...]
    turned_totals = [totals_ref[j].astype(F32).T.astype(BF16) for j in range(groups)]
    for copy in copies:
        copy.wait()
    state = jnp.zeros((DK, DK), F32)
    for j in reversed(range(groups)):
        fresh = twice(turned_totals[j], state) + far_in[j].astype(F32)
        state = jnp.where(j > group, fresh, state)
    for j in range(members):
        back_out[j] = (mm(before[j], state, FINE) + after[j]).astype(BF16)
    copies = [
        send(back_out.at[near[d]], back_in.at[member], back_s, back_r, d, near_ids[d]) for d in range(1, members)
    ]
    back_in[member] = back_out[member]
    for copy in copies:
        copy.wait()
    out_ref[...] = back_in[...]


def ring_places(axis):
    seq, head = lax.axis_index("seq"), lax.axis_index("head")
    size = lax.axis_size(axis)
    me = lax.axis_index(axis)
    places = [(me + d) % size for d in range(size)]
    return me, places, [(seq, place) for place in places]


def start_reduce(part_ref, recv, sends, receives, places, ids, rows):
    return [
        send(part_ref.at[pl.ds(pl.multiple_of(places[d] * rows, rows), rows)], recv.at[d - 1], sends, receives, d - 1, ids[d])
        for d in range(1, len(places))
    ]


def end_reduce(copies, part_ref, recv, me, rows):
    for copy in copies:
        copy.wait()
    total = part_ref[pl.ds(pl.multiple_of(me * rows, rows), rows)].astype(F32)
    for d in range(len(copies)):
        total = total + recv[d].astype(F32)
    return total


def start_gather(full_ref, sends, receives, me, ids, rows):
    mine = full_ref.at[pl.ds(pl.multiple_of(me * rows, rows), rows)]
    return [send(mine, mine, sends, receives, d - 1, ids[d]) for d in range(1, len(ids))]


def rms_scale(values):
    return lax.rsqrt(jnp.mean(values * values, axis=-1, keepdims=True) + 1e-05)


def rms_back(grad, values, gain):
    scale = rms_scale(values)
    u = grad * gain
    back = scale * u - values * (scale * scale * scale * jnp.mean(u * values, axis=-1, keepdims=True))
    return back, jnp.sum(grad * values * scale, axis=0, keepdims=True)


def middle_kernel(part_ref, tokens_ref, gain_ref, second_ref, middle_ref, recv, red_s, red_r, gat_s, gat_r):
    me, places, ids = ring_places("head")
    rows = middle_ref.shape[0]
    mine = pl.ds(pl.multiple_of(me * rows, rows), rows)
    start_barrier(ids[1:])
    copies = start_reduce(part_ref, recv, red_s, red_r, places, ids, rows)
    middle = tokens_ref[mine].astype(F32) + end_reduce(copies, part_ref, recv, me, rows)
    second_ref[mine] = (middle * rms_scale(middle) * gain_ref[...]).astype(BF16)
    copies = start_gather(second_ref, gat_s, gat_r, me, ids, rows)
    middle_ref[...] = middle
    for copy in copies:
        copy.wait()


def middle_back_kernel(
    part_ref, middle_ref, cotangent_ref, gain_ref, branch_ref, grad_ref, grad_gain_ref, recv, red_s, red_r, gat_s, gat_r
):
    me, places, ids = ring_places("head")
    rows = middle_ref.shape[0]
    mine = pl.ds(pl.multiple_of(me * rows, rows), rows)
    start_barrier(ids[1:])
    copies = start_reduce(part_ref, recv, red_s, red_r, places, ids, rows)
    grad_second = end_reduce(copies, part_ref, recv, me, rows)
    back, grad_gain = rms_back(grad_second, middle_ref[...], gain_ref[...])
    grad = cotangent_ref[mine].astype(F32) + back
    branch_ref[mine] = grad.astype(BF16)
    copies = start_gather(branch_ref, gat_s, gat_r, me, ids, rows)
    grad_ref[...] = grad
    grad_gain_ref[...] = grad_gain
    for copy in copies:
        copy.wait()


def tokens_back_kernel(
    normed_part_ref, ffn_part_ref, tokens_ref, middle_ref, grad_ref, gain_ref, output_ref, grad_tokens_ref, grad_gain_ref,
    low_ref, recv, recv_2, red_s, red_r, gat_s, gat_r, red_s2, red_r2, gat_s2, gat_r2,
):
    me, places, ids = ring_places("head")
    rows = middle_ref.shape[0]
    mine = pl.ds(pl.multiple_of(me * rows, rows), rows)
    start_barrier(ids[1:])
    copies = start_reduce(normed_part_ref, recv, red_s, red_r, places, ids, rows)
    copies_2 = start_reduce(ffn_part_ref, recv_2, red_s2, red_r2, places, ids, rows)
    grad_normed = end_reduce(copies, normed_part_ref, recv, me, rows)
    back, grad_gain = rms_back(grad_normed, tokens_ref[mine].astype(F32), gain_ref[...])
    low_ref[mine] = (grad_ref[...] + back).astype(BF16)
    copies = start_gather(low_ref, gat_s, gat_r, me, ids, rows)
    grad_gain_ref[...] = grad_gain
    output_ref[mine] = (middle_ref[...] + end_reduce(copies_2, ffn_part_ref, recv_2, me, rows)).astype(BF16)
    copies_2 = start_gather(output_ref, gat_s2, gat_r2, me, ids, rows)
    for copy in copies:
        copy.wait()
    grad_tokens_ref[...] = low_ref[...].astype(F32)
    for copy in copies_2:
        copy.wait()


def call(kernel, outs, *args, name):
    return pl.pallas_call(
        kernel,
        out_shape=[jax.ShapeDtypeStruct(shape, kind) for shape, kind in outs],
        compiler_params=pltpu.CompilerParams(vmem_limit_bytes=VMEM_LIMIT),
        name=name,
    )(*args)


def remote_call(kernel, outs, scratch, identity, *args, name):
    return pl.pallas_call(
        kernel,
        in_specs=[pl.BlockSpec(memory_space=pltpu.VMEM)] * len(args),
        out_specs=[pl.BlockSpec(memory_space=pltpu.VMEM)] * len(outs),
        out_shape=[jax.ShapeDtypeStruct(shape, kind) for shape, kind in outs],
        scratch_shapes=scratch,
        compiler_params=pltpu.CompilerParams(
            vmem_limit_bytes=VMEM_LIMIT, collective_id=identity, has_side_effects=True
        ),
        name=name,
    )(*args)


def pairs(*sizes):
    return [pltpu.SemaphoreType.DMA((size,)) for size in sizes for _ in range(2)]


def shifted(block, axis, distance):
    devices = range(lax.axis_size(axis))
    route = [(i - distance, i) for i in devices if i - distance in devices]
    return lax.ppermute(block, axis, route)


def per_device(
    tokens,
    mixer_gain,
    in_weight,
    rate_weight,
    conv_weight,
    decay_log,
    decay_bias,
    out_gain,
    out_weight,
    ffn_gain,
    gate_up_weight,
    down_weight,
    cotangent,
):
    count, width = tokens.shape
    heads = in_weight.shape[1]
    hidden_units = down_weight.shape[1]
    slab = in_weight.shape[0]
    projections = heads * PROJ + LANES
    units = heads * HALVES
    peers, sharers = lax.axis_size("seq"), lax.axis_size("head")
    groups = peers // units
    rows = count // sharers

    first = jnp.concatenate(
        [
            in_weight.reshape(slab, heads * PROJ),
            rate_weight.reshape(slab, 2 * heads),
            jnp.zeros((slab, LANES - 2 * heads), BF16),
        ],
        axis=1,
    )
    rest = jnp.concatenate(
        [out_weight.reshape(slab, heads * DV), gate_up_weight.reshape(slab, 2 * hidden_units), down_weight], axis=1
    )
    first_full = lax.all_gather(first, "seq", axis=0, tiled=True)
    rest_full = lax.all_gather(rest, "seq", axis=0, tiled=True)
    out_full = rest_full[:, : heads * DV]
    gate_up_full = rest_full[:, heads * DV : heads * DV + 2 * hidden_units]
    down_full = rest_full[:, heads * DV + 2 * hidden_units :]

    behind = shifted(tokens[count - HALO :], "seq", 1)
    source = jnp.concatenate([behind, tokens], axis=0).astype(F32)
    normed_long = (source * rms_scale(source) * mixer_gain).astype(BF16)
    normed = normed_long[HALO:]
    projected = mm(normed_long, first_full)

    taps = conv_weight.reshape(KW, heads * CONV)
    scales = jnp.pad(jnp.stack([decay_log, decay_bias]), ((0, 6), (0, LANES - heads)))
    queries, keys, values, inv, out_local, out_map, summary = call(
        functools.partial(local_forward, heads),
        [
            ((heads, count, DK), BF16),
            ((heads, count, DK), BF16),
            ((heads, count, DV), BF16),
            ((heads, count, count), F32),
            ((heads, count, DV), F32),
            ((heads, count, DK), F32),
            ((units, DK, 2 * DK), BF16),
        ],
        projected,
        taps,
        scales,
        name="local_forward",
    )
    block = (DK, DK)
    double = (DK, 2 * DK)
    entering, kept, totals = remote_call(
        functools.partial(scan_forward, groups),
        [((units, *block), BF16), ((units, *block), BF16), ((groups, *block), BF16)],
        [
            pltpu.VMEM((units, *double), BF16),
            pltpu.VMEM((units, *double), F32),
            pltpu.VMEM(double, BF16),
            pltpu.VMEM((groups, *double), BF16),
            pltpu.VMEM((units, *block), BF16),
            pltpu.VMEM((units, *block), BF16),
            *pairs(units, groups, units),
        ],
        1,
        summary,
        name="scan_forward",
    )
    gain_row = out_gain.reshape(1, DV)
    mixer_out, gated = call(
        functools.partial(mix_outputs, heads),
        [((heads, count, DV), F32), ((count, heads * DV), BF16)],
        out_local,
        out_map,
        entering,
        projected,
        gain_row,
        name="mix_outputs",
    )
    branch = mmt(gated, out_full)
    ring = [pltpu.VMEM((sharers - 1, rows, width), BF16)]
    second, middle = remote_call(
        middle_kernel,
        [((count, width), BF16), ((rows, width), F32)],
        ring + pairs(sharers - 1, sharers - 1),
        2,
        branch.astype(BF16),
        tokens,
        ffn_gain.reshape(1, width),
        name="middle",
    )
    gate_up = mm(second, gate_up_full)
    z, up = gate_up[:, :hidden_units], gate_up[:, hidden_units:]
    s = jax.nn.sigmoid(z)
    hidden = (z * s * up).astype(BF16)
    ffn_part = mmt(hidden, down_full)
    grad_hidden = mm(cotangent, down_full)
    grad_gate_up = jnp.concatenate([grad_hidden * up * s * (1.0 + z * (1.0 - s)), grad_hidden * z * s], axis=1).astype(
        BF16
    )
    second_part = mmt(grad_gate_up, gate_up_full)
    grad_branch, grad_middle, grad_ffn_gain = remote_call(
        middle_back_kernel,
        [((count, width), BF16), ((rows, width), F32), ((1, width), F32)],
        ring + pairs(sharers - 1, sharers - 1),
        3,
        second_part.astype(BF16),
        middle,
        cotangent,
        ffn_gain.reshape(1, width),
        name="middle_back",
    )
    grad_gated = mm(grad_branch, out_full)
    grad_mixed, grad_gate, grad_out_gain, carried = call(
        functools.partial(mix_outputs_back, heads),
        [
            ((heads, count, DV), F32),
            ((count, heads * DV), BF16),
            ((1, DV), F32),
            ((units, DK, DK), BF16),
        ],
        grad_gated,
        mixer_out,
        out_map,
        projected,
        gain_row,
        name="mix_outputs_back",
    )
    leaving = remote_call(
        functools.partial(scan_backward, groups),
        [((units, *block), BF16)],
        [
            pltpu.VMEM((units, *block), BF16),
            pltpu.VMEM((units, *block), BF16),
            pltpu.VMEM((units, *block), F32),
            pltpu.VMEM((units, *block), F32),
            pltpu.VMEM(block, BF16),
            pltpu.VMEM((groups, *block), BF16),
            pltpu.VMEM((units, *block), BF16),
            pltpu.VMEM((units, *block), BF16),
            *pairs(units, groups, units),
        ],
        4,
        carried,
        kept,
        totals,
        name="scan_backward",
    )[0]
    grad_projected, halo, tail, grad_taps, grad_scales = call(
        functools.partial(local_backward, heads),
        [
            ((count, projections), BF16),
            ((HALO, heads * CONV), F32),
            ((HALO, heads * CONV), F32),
            ((KW, heads * CONV), F32),
            ((8, LANES), F32),
        ],
        projected,
        taps,
        scales,
        queries,
        keys,
        values,
        inv,
        grad_mixed,
        entering,
        leaving,
        grad_gate,
        name="local_backward",
    )
    tail = (tail + shifted(halo, "seq", -1)).astype(BF16)
    for h in range(heads):
        grad_projected = lax.dynamic_update_slice(
            grad_projected, tail[:, h * CONV : (h + 1) * CONV], (count - HALO, h * PROJ)
        )
    normed_part = mmt(grad_projected, first_full)
    output, grad_tokens, grad_mixer_gain = remote_call(
        tokens_back_kernel,
        [((count, width), BF16), ((count, width), F32), ((1, width), F32)],
        [pltpu.VMEM((count, width), BF16)] + ring + ring + pairs(*[sharers - 1] * 4),
        5,
        normed_part.astype(BF16),
        ffn_part.astype(BF16),
        tokens,
        middle,
        grad_middle,
        mixer_gain.reshape(1, width),
        name="tokens_back",
    )
    grad_rest = jnp.concatenate(
        [
            mtm(grad_branch, gated).astype(BF16),
            mtm(second, grad_gate_up).astype(BF16),
            mtm(cotangent, hidden).astype(BF16),
        ],
        axis=1,
    )
    grad_first = mtm(normed, grad_projected).astype(BF16)
    grad_rest = lax.psum_scatter(grad_rest, "seq", scatter_dimension=0, tiled=True).astype(F32)
    grad_first = lax.psum_scatter(grad_first, "seq", scatter_dimension=0, tiled=True).astype(F32)
    gains = jnp.concatenate([grad_mixer_gain[0], grad_ffn_gain[0], grad_out_gain[0]])
    gains = lax.psum(gains, ("seq", "head"))
    small = jnp.concatenate([grad_taps.reshape(-1), grad_scales[0, :heads], grad_scales[1, :heads]])
    small = lax.psum(small, "seq")
    at_taps = KW * heads * CONV
    rates_at = heads * PROJ
    gate_at = heads * DV
    down_at = gate_at + 2 * hidden_units
    return (
        output,
        grad_tokens,
        gains[:width],
        grad_first[:, :rates_at].reshape(slab, heads, PROJ),
        grad_first[:, rates_at : rates_at + 2 * heads].reshape(slab, 2, heads),
        small[:at_taps].reshape(KW, heads, CONV),
        small[at_taps : at_taps + heads],
        small[at_taps + heads :],
        gains[2 * width :],
        grad_rest[:, :gate_at].reshape(slab, heads, DV),
        gains[width : 2 * width],
        grad_rest[:, gate_at:down_at].reshape(slab, 2, hidden_units),
        grad_rest[:, down_at:],
    )


def solution(mesh):
    in_specs = (
        P("seq", None),
        P(),
        P("seq", "head", None),
        P("seq", None, "head"),
        P(None, "head", None),
        P("head"),
        P("head"),
        P(),
        P("seq", "head", None),
        P(),
        P("seq", None, "head"),
        P("seq", "head"),
        P("seq", None),
    )
    out_specs = (
        P("seq", None),
        P("seq", None),
        P(),
        P("seq", "head", None),
        P("seq", None, "head"),
        P(None, "head", None),
        P("head"),
        P("head"),
        P(),
        P("seq", "head", None),
        P(),
        P("seq", None, "head"),
        P("seq", "head"),
    )
    return jax.shard_map(
        per_device, mesh=mesh, in_specs=in_specs, out_specs=out_specs, check_vma=False
    )
```

time: 1470 us -> 639 us (0.43)
  waiting for transfers between devices: 425 us -> 94.3 us
  other arithmetic: 326 us -> 16.7 us
  matrix products: 383 us -> 76.8 us
  Pallas kernels: 0 us -> 208 us
  local copies, waits for them, and re-layouts: 130 us -> 30 us
  blocking collectives: 162 us -> 188 us
    dot_general x177 -> x12, matrix products: 361 us -> 76.8 us  [dot(): lax.dot_general(a, b, (dims, ((), ())), precision=precision, preferred_el...]
    another operation x90 -> x1, other arithmetic: 265 us -> 0.6 us  [per_device(): jnp.stack([decay_log, decay_bias])]
    pallas_call x0 -> x9, Pallas kernels: none -> 208 us  [the longest x5 164 us: remote_call(): pl.pallas_call(kernel, in_specs=[pl.BlockSpec(memory_space=pltpu.VMEM)] *...]
    all_gather x8 -> x2, waiting for transfers between devices: 241 us -> 90.7 us  [the longest x1 60.6 us: per_device(): first_full = lax.all_gather(first, 'seq', axis=0, tiled=True)]
    psum x3 -> x0, waiting for transfers between devices: 143 us -> none  [the longest x1 61.4 us: per_device(): lax.psum(ffn_part.astype(jnp.bfloat16), 'head').astype(jnp.float32)]
    psum x2, blocking collectives: 133 us -> 188 us  [the longest x1 120 us: per_device(): small = lax.psum(small, 'seq')]
    unnamed x18 -> x4, waiting for transfers between devices: 40.8 us -> 0.07 us
    all_gather x1 -> x0, blocking collectives: 28.3 us -> none  [per_device(): lax.all_gather(rate_weight, 'seq', axis=0, tiled=True)]
  transfers between devices with their start and end apart: 18 -> 6, of which waited for: 9 -> 3; matrix products, arithmetic and copies ran while one was open for 45% -> 11% of each run, Pallas kernels for 0% -> 15%
where the time goes in v1:
time: 639 us; the launch traced here: 635 us
  Pallas kernels  208 us (33%)
  blocking collectives  188 us (29%)
  waiting for transfers between devices  94.3 us (15%)
  matrix products  76.8 us (12%)
  local copies, waits for them, and re-layouts  30 us (5%)
  other arithmetic  16.7 us (3%)
  between operations  14.4 us (2%)
  starting transfers between devices  7.34 us (1%)
    pallas_call x5, Pallas kernels, remote_call(): pl.pallas_call(kernel, in_specs=[pl.BlockSpec(memory_space=pltpu.VMEM)] *...  164 us
    psum x1, blocking collectives, per_device(): small = lax.psum(small, 'seq')  120 us
    dot_general x12, matrix products, dot(): lax.dot_general(a, b, (dims, ((), ())), precision=precision, preferred_el...  76.8 us
    psum x1, blocking collectives, per_device(): gains = lax.psum(gains, ('seq', 'head'))  67.7 us
    all_gather x1, waiting for transfers between devices, per_device(): first_full = lax.all_gather(first, 'seq', axis=0, tiled=True)  60.6 us
    pallas_call x4, Pallas kernels, call(): pl.pallas_call(kernel, out_shape=[jax.ShapeDtypeStruct(shape, kind) for s...  44.3 us
    all_gather x1, waiting for transfers between devices, per_device(): rest_full = lax.all_gather(rest, 'seq', axis=0, tiled=True)  30.1 us
    concatenate x1, other arithmetic, per_device(): jnp.concatenate([mtm(grad_branch, gated).astype(BF16), mtm(second, grad_g...  13 us
  transfers between devices with their start and end apart: 6, of which 3 were waited for; matrix products, arithmetic and copies ran while one was open for 11% of the time, Pallas kernels for 15%

profile of v1, /device:TPU:1, one launch (start us, length us, event | category | flops | bytes accessed | tf_op | source)
XLA Modules:
  0.0 635.4 jit_solution(9134530656012617408)
XLA Ops:
  11.2 4.9 collective-permute-start
  18.0 60.6 %all-gather.3.cloned.1.call-done = bf16[2048,3200]{1,0:T(8,128)(2,1)} async-done(((bf16[64,3200]{1,0:T(8,128)(2,1)}), bf16[2048,3200]{1,0:T(8,128)(2,1)}) %all-gather.3.cloned.1.call-update) | async-done | bytes 13107216 | tf_op jit(solution)/shard_map/all_gather | solution.py:592
  78.7 8.7 %fusion.33.proj_ref = f32[264,3200]{1,0:T(8,128)} fusion(bf16[264,2048]{1,0:T(8,128)(2,1)S(1)} %fusion.27, bf16[2048,3200]{1,0:T(8,128)(2,1)} %all-gather.3.cloned.1.call-done), kind=kOutput, calls=%fused_computation.52 | convolution fusion | flops 3460300800 | bytes 17567744 | tf_op jit(solution)/shard_map/dot_general | solution.py:28
  87.4 15.0 %local_forward.1 = (bf16[4,256,128]{2,1,0:T(8,128)(2,1)}, bf16[4,256,128]{2,1,0:T(8,128)(2,1)}, bf16[4,256,256]{2,1,0:T(8,128)(2,1)}, f32[4,256,256]{2,1,0:T(8,1...) custom-call(f32[264,3200]{1,0:T(8,128)} %fusion.33.proj_ref, ...), custom_call_target="tpu_custom_call" | custom-call | tf_op jit(solution)/shard_map/local_forward/pallas_call | solution.py:524
  102.4 30.5 %scan_forward.1 = (bf16[8,128,128]{2,1,0:T(8,128)(2,1)}, bf16[8,128,128]{2,1,0:T(8,128)(2,1)}, bf16[4,128,128]{2,1,0:T(8,128)(2,1)}) custom-call(bf16[8,128,256]{2,1,0:T(8,128)(2,1)} %get-tuple-element.48.pack_ref), custom_call_target="tpu_custom_call" | custom-call | tf_op jit(solution)/shard_map/scan_forward/pallas_call | solution.py:533
  133.0 4.4 mix_outputs.1
  137.3 30.1 %all-gather.5.cloned.1.call-done = bf16[2048,5248]{1,0:T(8,128)(2,1)} async-done(((bf16[64,5248]{1,0:T(8,128)(2,1)}), bf16[2048,5248]{1,0:T(8,128)(2,1)}) %all-gather.5.cloned.1.call-update) | async-done | bytes 21495824 | tf_op jit(solution)/shard_map/all_gather | solution.py:593
  167.5 4.6 fusion.19.part_ref
  172.1 31.8 %middle.1 = (bf16[256,2048]{1,0:T(8,128)(2,1)}, f32[64,2048]{1,0:T(8,128)}) custom-call(bf16[256,2048]{1,0:T(8,128)(2,1)} %fusion.19.part_ref, bf16[256,2048]{1,0:T(8,128)(2,1)} %tokens_ref.3, f32[1,2048]{1,0:T(1,128)} %bitcast.52), custom_call_target="tpu_custom_call" | custom-call | tf_op jit(solution)/shard_map/middle/pallas_call | solution.py:533
  203.9 7.8 %fusion.2 = f32[256,2816]{0,1:T(8,128)S(1)} fusion(bf16[256,2048]{1,0:T(8,128)(2,1)} %get-tuple-element.51, bf16[2048,5248]{1,0:T(8,128)(2,1)} %all-gather.5.cloned.1.call-done), kind=kOutput, calls=%fused_computation.5 | convolution fusion | flops 2952790016 | bytes 15466496 | tf_op jit(solution)/shard_map/dot_general | solution.py:28
  211.7 4.8 multiply_convert_fusion.2
  216.6 9.2 %fusion.16.part_ref = bf16[256,2048]{1,0:T(8,128)(2,1)} fusion(bf16[2048,5248]{1,0:T(8,128)(2,1)} %all-gather.5.cloned.1.call-done, bf16[256,1408]{0,1:T(8,128)(2,1)S(1)} %get-tuple-element.85, bf16[256,1408]{0,1:T(8,128)(2,1)S(1)} %get-tuple-element.84), kind=kOutput, calls=%fused_computation.21 | convolution fusion | flops 2956197888 | bytes 14024704 | tf_op jit(solution)/shard_map/dot_general | solution.py:28
  225.8 29.8 %middle_back.1 = (bf16[256,2048]{1,0:T(8,128)(2,1)}, f32[64,2048]{1,0:T(8,128)}, f32[1,2048]{1,0:T(1,128)}) custom-call(bf16[256,2048]{1,0:T(8,128)(2,1)} %fusion.16.part_ref, f32[64,2048]{1,0:T(8,128)} %get-tuple-element.52.middle_ref, bf16[256,2048]{1,0:T(8,128)(2,1)} %cotangent_ref.1, f32[1,2048]{1,0:T(1,128)} %bitcast.53), custom_call_target="tpu_custom_call" | custom-call | tf_op jit(solution)/shard_map/middle_back/pallas_call | solution.py:533
  255.6 4.7 fusion.9.grad_ref
  260.3 4.9 mix_outputs_back.1
  265.2 23.5 %scan_backward.1.leaving_ref = bf16[8,128,128]{2,1,0:T(8,128)(2,1)} custom-call(bf16[8,128,128]{2,1,0:T(8,128)(2,1)} %get-tuple-element.56.pack_ref, bf16[8,128,128]{2,1,0:T(8,128)(2,1)} %get-tuple-element.57.kept_ref, bf16[4,128,128]{2,1,0:T(8,128)(2,1)} %get-tuple-element.58.totals_ref), custom_call_target="tpu_custom_call" | custom-call | tf_op jit(solution)/shard_map/scan_backward/pallas_call | solution.py:533
  288.7 20.0 %local_backward.1 = (bf16[256,3200]{1,0:T(8,128)(2,1)}, f32[8,2048]{1,0:T(8,128)}, f32[8,2048]{1,0:T(8,128)}, f32[4,2048]{1,0:T(4,128)}, f32[8,128]{1,0:T(8,128)}) custom-call(f32[264,3200]{1,0:T(8,128)} %fusion.33.proj_ref, f32[4,2048]{1,0:T(4,128)} %bitcast.49, f32[8,128]{1,0:T(8,128)} %select_maximum_fusion.scales_ref, ...), custom_call_target="tpu_custom_call" | custom-call | tf_op jit(solution)/shard_map/local_backward/pallas_call | solution.py:524
  308.7 2.2 collective-permute-start.1
  311.0 3.5 collective-permute-done.1
  317.7 8.1 %convolution_convert_fusion = bf16[2048,3200]{1,0:T(8,128)(2,1)} fusion(bf16[256,3200]{1,0:T(8,128)(2,1)} %slice_dynamic-update-slice_fusion, bf16[264,2048]{1,0:T(8,128)(2,1)S(1)} %fusion.27), kind=kOutput, calls=%fused_computation.1 | convolution fusion | flops 3361996800 | bytes 15794176 | tf_op jit(solution)/shard_map/dot_general | solution.py:28
  327.2 3.4 convolution_convert_fusion.3
  330.6 6.6 %copy.37 = bf16[2048,1024]{1,0:T(8,128)(2,1)} copy(bf16[2048,1024]{0,1:T(8,128)(2,1)} %convolution_convert_fusion.3) | data formatting | bytes 8388608 | tf_op jit(solution)/shard_map/convert_element_type | solution.py:763
  337.2 4.2 fusion.4
  341.5 5.2 convolution_convert_fusion.1
  346.7 13.0 %pad_maximum_fusion = bf16[2048,5248]{1,0:T(8,128)(2,1)} fusion(bf16[2048,1408]{1,0:T(8,128)(2,1)} %fusion.4, bf16[2048,2816]{1,0:T(8,128)(2,1)S(1)} %convolution_convert_fusion.1, bf16[2048,1024]{1,0:T(8,128)(2,1)S(1)} %copy-done.1), kind=kLoop, calls=%fused_computation | loop fusion | flops 64487424 | bytes 42991616 | tf_op jit(solution)/shard_map/concatenate | solution.py:761
  361.3 120.2 %psum.15 = f32[8200]{0:T(1024)S(1)} all-reduce(f32[8200]{0:T(1024)S(1)} %concatenate.27), channel_id=1, replica_groups=mesh['seq'=32,'head'=4] {'seq'}, use_global_device_ids=true, to_apply=%region_3.4 | all-reduce | flops 8200 | bytes 65600 | tf_op jit(solution)/shard_map/psum | solution.py:775
  482.7 5.6 fusion.22.ffn_part_ref
  488.2 10.4 %convolution_convert_fusion.4.normed_part_ref = bf16[256,2048]{1,0:T(8,128)(2,1)} fusion(bf16[256,3200]{1,0:T(8,128)(2,1)S(1)} %copy-done.7, bf16[2048,3200]{1,0:T(8,128)(2,1)} %all-gather.3.cloned.1.call-done), kind=kOutput, calls=%fused_computation.24 | convolution fusion | flops 3355967488 | bytes 15794176 | tf_op jit(solution)/shard_map/dot_general | solution.py:28
  498.7 48.0 %tokens_back.1 = (bf16[256,2048]{1,0:T(8,128)(2,1)}, f32[256,2048]{1,0:T(8,128)}, f32[1,2048]{1,0:T(1,128)}) custom-call(bf16[256,2048]{1,0:T(8,128)(2,1)} %convolution_convert_fusion.4.normed_part_ref, bf16[256,2048]{1,0:T(8,128)(2,1)} %fusion.22.ffn_part_ref, bf16[256,2048]{1,0:T(8,128)(2,1)} %tokens_ref.3, f32[64,2048]{1,0:T(8,128)} %get-tuple-element.52.middle_ref, ...), custom_call_target="tpu_custom_call" | custom-call | tf_op jit(solution)/shard_map/tokens_back/pallas_call | solution.py:533
  547.4 67.7 %psum.14 = f32[4352]{0:T(1024)S(1)} all-reduce(f32[4352]{0:T(1024)S(1)} %pad_maximum_fusion.6), channel_id=1, replica_groups=mesh['seq'=32,'head'=4] {'seq','head'}, use_global_device_ids=true, to_apply=%region_1.2 | all-reduce | flops 4352 | bytes 34816 | tf_op jit(solution)/shard_map/psum | solution.py:773
  624.9 2.3 copy.51
  627.2 1.3 copy.52
  (93 shorter events, 23.6 us)
Async XLA Ops:
  7.2 2.9 copy-start.15
  7.2 3.0 copy-start.13
  7.2 3.0 copy-start.14
  7.2 71.4 %all-gather.3.cloned.1.call-start = ((), (), s32[]{:S(2)}) async-start(), calls=%async_computation.2 | async-start | bytes 13516800 | tf_op jit(solution)/shard_map/all_gather | solution.py:592
  9.1 2.1 copy-start
  9.2 7.0 %copy-start.21 = (f32[4]{0:T(128)S(1)}, f32[4]{0:T(128)}, u32[]{:S(2)}) copy-start(f32[4]{0:T(128)} %param.19) | copy-start | bytes 52
  9.2 7.0 %copy-start.22 = (f32[4]{0:T(128)S(1)}, f32[4]{0:T(128)}, u32[]{:S(2)}) copy-start(f32[4]{0:T(128)} %param.18) | copy-start | bytes 52
  9.2 7.6 %copy-start.17 = (f32[4,4,512]{2,1,0:T(4,128)S(1)}, f32[4,4,512]{2,1,0:T(4,128)}, u32[]{:S(2)}) copy-start(f32[4,4,512]{2,1,0:T(4,128)} %param.17) | copy-start | bytes 98308
  10.1 7.7 %copy-start.16 = (f32[2048]{0:T(1024)S(1)}, f32[2048]{0:T(1024)}, u32[]{:S(2)}) copy-start(f32[2048]{0:T(1024)} %param.14) | copy-start | bytes 24580
  10.1 157.4 %all-gather.5.cloned.1.call-start = ((), (), s32[]{:S(2)}) async-start(), calls=%async_computation.3 | async-start | bytes 22167552 | tf_op jit(solution)/shard_map/all_gather | solution.py:593
  11.1 605.2 %reduce-scatter.3.cloned.1.call-start = ((), (), s32[]{:S(2)}) async-start(), calls=%async_computation.4 | async-start | bytes 13516800 | tf_op jit(solution)/shard_map/reduce_scatter | solution.py:771
  11.2 6.2 collective-permute-start
  203.9 7.8 %copy-start.2 = (bf16[256,2048]{1,0:T(8,128)(2,1)S(1)}, bf16[256,2048]{1,0:T(8,128)(2,1)}, u32[]{:S(2)}) copy-start(bf16[256,2048]{1,0:T(8,128)(2,1)} %cotangent_ref.1) | copy-start | bytes 3145732
  216.5 9.3 %copy-start.10 = (bf16[256,1408]{0,1:T(8,128)(2,1)}, bf16[256,1408]{0,1:T(8,128)(2,1)S(1)}, u32[]{:S(2)}) copy-start(bf16[256,1408]{0,1:T(8,128)(2,1)S(1)} %get-tuple-element.84) | copy-start | bytes 2162692
  216.5 9.2 %copy-start.11 = (bf16[256,1408]{0,1:T(8,128)(2,1)}, bf16[256,1408]{0,1:T(8,128)(2,1)S(1)}, u32[]{:S(2)}) copy-start(bf16[256,1408]{0,1:T(8,128)(2,1)S(1)} %get-tuple-element.85) | copy-start | bytes 2162692
  216.6 120.7 %copy-start.8 = (bf16[256,1408]{0,1:T(8,128)(2,1)}, bf16[256,1408]{0,1:T(8,128)(2,1)S(1)}, u32[]{:S(2)}) copy-start(bf16[256,1408]{0,1:T(8,128)(2,1)S(1)} %get-tuple-element.86) | copy-start | bytes 2162692
  308.7 5.8 collective-permute-start.1
  325.9 1.2 copy-start.5
  325.9 1.4 copy-start.12
  325.9 294.1 %reduce-scatter.5.cloned.1.call-start = ((), (), s32[]{:S(2)}) async-start(), calls=%async_computation.5 | async-start | bytes 22167552 | tf_op jit(solution)/shard_map/reduce_scatter | solution.py:770
  330.6 6.6 %copy-start.3 = (bf16[256,2048]{1,0:T(8,128)(2,1)S(1)}, bf16[256,2048]{1,0:T(8,128)(2,1)}, u32[]{:S(2)}) copy-start(bf16[256,2048]{1,0:T(8,128)(2,1)} %cotangent_ref.1) | copy-start | bytes 3145732
  341.5 5.2 copy-start.1
  359.7 0.8 copy-start.18
  359.7 123.0 %copy-start.9 = (bf16[256,1408]{0,1:T(8,128)(2,1)S(1)}, bf16[256,1408]{0,1:T(8,128)(2,1)}, u32[]{:S(2)}) copy-start(bf16[256,1408]{0,1:T(8,128)(2,1)} %copy-done.8) | copy-start | bytes 2162692
  482.7 5.6 copy-start.7
  498.7 48.1 %copy-start.19 = (f32[1,2048]{1,0:T(1,128)S(1)}, f32[1,2048]{1,0:T(1,128)}, u32[]{:S(2)}) copy-start(f32[1,2048]{1,0:T(1,128)} %get-tuple-element.67) | copy-start | bytes 24580
  498.7 48.1 %copy-start.20 = (f32[1,256]{1,0:T(1,128)S(1)}, f32[1,256]{1,0:T(1,128)}, u32[]{:S(2)}) copy-start(f32[1,256]{1,0:T(1,128)} %get-tuple-element.68) | copy-start | bytes 3076
  620.0 4.2 copy-start.4
  622.9 4.4 copy-start.6
Sparse Core Ops, SparseCore 0:
  10.9 67.7 all-gather.2
  81.5 85.9 all-gather.4
  326.0 102.9 reduce-scatter.2
  433.4 129.5 reduce-scatter.4

commit v2 on v1

--- a/solution.py
+++ b/solution.py
@@ -46,6 +46,17 @@
 
 def softplus(x):
     return jnp.maximum(x, 0.0) + jnp.log1p(jnp.exp(-jnp.abs(x)))
+
+
+def split_by_core(values, slab):
+    width = values.shape[1]
+    lanes = iota((values.shape[0], 2 * slab), 1)
+    firsts, seconds = [], []
+    for at in range(0, width, 4 * slab):
+        a, b = values[:, at : at + 2 * slab], values[:, at + 2 * slab : at + 4 * slab]
+        firsts.append(jnp.where(lanes < slab, a, pltpu.roll(b, slab, 1)))
+        seconds.append(jnp.where(lanes < slab, pltpu.roll(a, slab, 1), b))
+    return jnp.concatenate(firsts + seconds, axis=1)
 
 
 def column(block, index):
@@ -123,8 +134,11 @@
     return extended, mixed, gate, (q_raw, q_scale), (k_raw, k_scale), queries, keys, values
 
 
-def local_forward(heads, proj_ref, taps_ref, scales_ref, q_ref, k_ref, v_ref, inv_ref, out_ref, map_ref, sum_ref):
+def local_forward(
+    heads, slab, proj_ref, taps_ref, scales_ref, normed_ref, q_ref, k_ref, v_ref, inv_ref, out_ref, map_ref, sum_ref, split_ref
+):
     size = proj_ref.shape[0] - HALO
+    split_ref[...] = split_by_core(normed_ref[HALO:].astype(F32), slab).astype(BF16)
     rows, columns = triangles(size)
     rates = proj_ref[HALO:, heads * PROJ :]
     scales = scales_ref[...]
@@ -174,8 +188,12 @@
         gated_ref[:, h * DV : (h + 1) * DV] = gated.astype(BF16)
 
 
-def mix_outputs_back(heads, grad_ref, mixed_ref, map_ref, proj_ref, gain_ref, grad_mixed_ref, grad_gate_ref, grad_gain_ref, carried_ref):
+def mix_outputs_back(
+    heads, slab, grad_ref, mixed_ref, map_ref, proj_ref, gain_ref, branch_ref,
+    grad_mixed_ref, grad_gate_ref, grad_gain_ref, carried_ref, split_ref,
+):
     gain = gain_ref[...]
+    split_ref[...] = split_by_core(branch_ref[...].astype(F32), slab).astype(BF16)
     total = jnp.zeros_like(gain)
     for h in range(heads):
         grad = grad_ref[:, h * DV : (h + 1) * DV]
@@ -202,9 +220,17 @@
 
 def local_backward(
     heads, proj_ref, taps_ref, scales_ref, q_ref, k_ref, v_ref, inv_ref, grad_ref, state_ref, leaving_ref, gate_ref,
-    out_ref, halo_ref, tail_ref, taps_out_ref, scales_out_ref,
+    out_ref, sibling_ref, taps_out_ref, scales_out_ref, halo_out, halo_in, tails,
+    halo_s, halo_r, body_s, body_r, tail_s, tail_r, rate_s, rate_r,
 ):
     size = proj_ref.shape[0] - HALO
+    seq, head_place = lax.axis_index("seq"), lax.axis_index("head")
+    peers = lax.axis_size("seq")
+    before, after = (lax.rem(seq + peers - 1, peers), head_place), (lax.rem(seq + 1, peers), head_place)
+    sibling = (seq + 1 - 2 * (seq % 2), head_place)
+    start_barrier([before, after, sibling])
+    copies = []
+    body = size - 2 * HALO
     rows, columns = triangles(size)
     rates = proj_ref[HALO:, heads * PROJ :]
     scales = scales_ref[...]
@@ -286,10 +312,13 @@
             taps_out_ref[j : j + 1, h * CONV : (h + 1) * CONV] = jnp.sum(
                 grad_mixed * back[HALO:], axis=0, keepdims=True
             )
-        halo_ref[:, h * CONV : (h + 1) * CONV] = total[:HALO]
-        tail_ref[:, h * CONV : (h + 1) * CONV] = total[size:]
+        halo_out[h] = total[:HALO]
+        tails[h] = total[size - HALO :]
         out_ref[:, h * PROJ : h * PROJ + CONV] = total[HALO:].astype(BF16)
         out_ref[:, h * PROJ + CONV : (h + 1) * PROJ] = gate_ref[:, h * DV : (h + 1) * DV]
+        copies.append(send(halo_out.at[h], halo_in.at[h], halo_s, halo_r, h, before))
+        upper = (pl.ds(0, body), pl.ds(h * PROJ, PROJ))
+        copies.append(send(out_ref.at[upper], sibling_ref.at[upper], body_s, body_r, h, sibling))
 
         grad_pre = -jnp.exp(column(scales[0:1], h)) * jax.nn.sigmoid(pre) * grad_decay
         grad_strength = grad_beta * beta * (1.0 - beta)
@@ -301,6 +330,18 @@
         rates_total = rates_total + jnp.where((row8 == 1) & (lane8 == h), bias_total, 0.0)
     out_ref[:, heads * PROJ :] = grad_rates.astype(BF16)
     scales_out_ref[...] = rates_total
+    side = (pl.ds(0, size), pl.ds(heads * PROJ, LANES))
+    last = [send(out_ref.at[side], sibling_ref.at[side], rate_s, rate_r, 0, sibling)]
+    for copy in copies:
+        copy.wait()
+    for h in range(heads):
+        arrived = jnp.where(seq < peers - 1, halo_in[h], 0.0)
+        fixed = tails[h] + jnp.concatenate([jnp.zeros_like(arrived), arrived], axis=0)
+        out_ref[body:, h * PROJ : h * PROJ + CONV] = fixed.astype(BF16)
+        lower = (pl.ds(body, 2 * HALO), pl.ds(h * PROJ, PROJ))
+        last.append(send(out_ref.at[lower], sibling_ref.at[lower], tail_s, tail_r, h, sibling))
+    for copy in last:
+        copy.wait()
 
 
 def start_barrier(peers):
@@ -339,9 +380,23 @@
     return member, group, near, near_ids, far_ids
 
 
+def to_sibling(slots, sends, receives):
+    seq, head = lax.axis_index("seq"), lax.axis_index("head")
+    sibling = seq + 1 - 2 * (seq % 2)
+    return [
+        send(source, target, sends, receives, index, (sibling, head)) for index, (source, target) in enumerate(slots)
+    ]
+
+
+def other_half(ref):
+    half = ref.shape[1] // 2
+    at = (1 - lax.axis_index("seq") % 2) * half
+    return ref.at[:, pl.ds(pl.multiple_of(at, half), half)]
+
+
 def scan_forward(
-    groups, pack_ref, out_ref, kept_ref, totals_ref, near_in, before, far_out, far_in, back_out, back_in,
-    near_s, near_r, far_s, far_r, back_s, back_r,
+    groups, pack_ref, split_ref, out_ref, sibling_ref, kept_ref, totals_ref, near_in, before, far_out, far_in, back_out, back_in,
+    near_s, near_r, far_s, far_r, back_s, back_r, core_s, core_r,
 ):
     members = pack_ref.shape[0]
     member, group, near, near_ids, far_ids = scan_places(members, groups)
@@ -349,6 +404,7 @@
     copies = [
         send(pack_ref.at[near[d]], near_in.at[member], near_s, near_r, d, near_ids[d]) for d in range(1, members)
     ]
+    aside = to_sibling([(other_half(split_ref), sibling_ref)], core_s, core_r)
     near_in[member] = pack_ref[member]
     for copy in copies:
         copy.wait()
@@ -378,11 +434,13 @@
     for copy in copies:
         copy.wait()
     out_ref[...] = back_in[...]
+    for copy in aside:
+        copy.wait()
 
 
 def scan_backward(
-    groups, pack_ref, kept_ref, totals_ref, out_ref, near_in, turned, before, after, far_out, far_in, back_out, back_in,
-    near_s, near_r, far_s, far_r, back_s, back_r,
+    groups, pack_ref, kept_ref, totals_ref, split_ref, gated_ref, out_ref, sibling_ref, sibling_gated_ref, near_in, turned, before, after, far_out, far_in, back_out, back_in,
+    near_s, near_r, far_s, far_r, back_s, back_r, core_s, core_r,
 ):
     members = pack_ref.shape[0]
     member, group, near, near_ids, far_ids = scan_places(members, groups)
@@ -390,6 +448,7 @@
     copies = [
         send(pack_ref.at[near[d]], near_in.at[member], near_s, near_r, d, near_ids[d]) for d in range(1, members)
     ]
+    aside = to_sibling([(other_half(split_ref), sibling_ref), (gated_ref, sibling_gated_ref)], core_s, core_r)
     near_in[member] = pack_ref[member]
     passed = (iota((DK, DK), 0) == iota((DK, DK), 1)).astype(F32)
     for j in reversed(range(members)):
@@ -421,35 +480,90 @@
     for copy in copies:
         copy.wait()
     out_ref[...] = back_in[...]
-
-
-def ring_places(axis):
+    for copy in aside:
+        copy.wait()
+
+
+def ring_ids(axis):
     seq, head = lax.axis_index("seq"), lax.axis_index("head")
-    size = lax.axis_size(axis)
-    me = lax.axis_index(axis)
-    places = [(me + d) % size for d in range(size)]
-    return me, places, [(seq, place) for place in places]
-
-
-def start_reduce(part_ref, recv, sends, receives, places, ids, rows):
-    return [
-        send(part_ref.at[pl.ds(pl.multiple_of(places[d] * rows, rows), rows)], recv.at[d - 1], sends, receives, d - 1, ids[d])
-        for d in range(1, len(places))
-    ]
-
-
-def end_reduce(copies, part_ref, recv, me, rows):
-    for copy in copies:
+    size = {"x": lax.axis_size("seq") // 8, "y": lax.axis_size("head"), "z": 4}[axis]
+    me = {"x": seq // 8, "y": head, "z": (seq // 2) % 4}[axis]
+
+    def at(place):
+        if axis == "y":
+            return (seq, place)
+        if axis == "x":
+            return (place * 8 + seq % 8, head)
+        return ((seq // 8) * 8 + place * 2 + seq % 2, head)
+
+    right, left = lax.rem(me + 1, size), lax.rem(me + size - 1, size)
+    return me, right, left, lax.rem(me + 2, size), at(right), at(left)
+
+
+def add_into(target, pieces, rows):
+    step = min(rows, 32)
+
+    @pl.loop(0, rows // step)
+    def _(k):
+        part = pl.ds(pl.multiple_of(k * step, step), step)
+        total = pieces[0][part].astype(F32)
+        for piece in pieces[1:]:
+            total = total + piece[part].astype(F32)
+        target[part] = total.astype(target.dtype)
+
+
+def ring_reduce(ring, blocks, result, landing, sends, receives):
+    me, right, left, across, right_id, left_id = ring
+    rows = blocks.shape[1]
+    half = rows // 2
+    upper, lower = pl.ds(0, half), pl.ds(half, half)
+    by_right = send(blocks.at[across, upper], landing.at[0], sends, receives, 0, right_id)
+    by_left = send(blocks.at[across, lower], landing.at[1], sends, receives, 1, left_id)
+    plain_right = send(blocks.at[right, lower], landing.at[2], sends, receives, 2, right_id)
+    plain_left = send(blocks.at[left, upper], landing.at[3], sends, receives, 3, left_id)
+    yield
+    by_right.wait()
+    add_into(landing.at[0], [blocks.at[right, upper], landing.at[0]], half)
+    summed_right = send(landing.at[0], landing.at[4], sends, receives, 4, right_id)
+    by_left.wait()
+    add_into(landing.at[1], [blocks.at[left, lower], landing.at[1]], half)
+    summed_left = send(landing.at[1], landing.at[5], sends, receives, 5, left_id)
+    yield
+    plain_right.wait()
+    plain_left.wait()
+    summed_right.wait()
+    summed_left.wait()
+    add_into(result.at[upper], [blocks.at[me, upper], landing.at[4], landing.at[3]], half)
+    add_into(result.at[lower], [blocks.at[me, lower], landing.at[2], landing.at[5]], half)
+
+
+def ring_gather(ring, blocks, sends, receives):
+    me, right, left, across, right_id, left_id = ring
+    rows = blocks.shape[1]
+    half = rows // 2
+    upper, lower = pl.ds(0, half), pl.ds(half, half)
+
+    def go(place, part, slot, peer):
+        return send(blocks.at[place, part], blocks.at[place, part], sends, receives, slot, peer)
+
+    upper_right = go(me, upper, 0, right_id)
+    lower_left = go(me, lower, 1, left_id)
+    lower_right = go(me, lower, 2, right_id)
+    upper_left = go(me, upper, 3, left_id)
+    yield
+    upper_right.wait()
+    far_right = go(left, upper, 4, right_id)
+    lower_left.wait()
+    far_left = go(right, lower, 5, left_id)
+    yield
+    for copy in (lower_right, upper_left, far_right, far_left):
         copy.wait()
-    total = part_ref[pl.ds(pl.multiple_of(me * rows, rows), rows)].astype(F32)
-    for d in range(len(copies)):
-        total = total + recv[d].astype(F32)
-    return total
-
-
-def start_gather(full_ref, sends, receives, me, ids, rows):
-    mine = full_ref.at[pl.ds(pl.multiple_of(me * rows, rows), rows)]
-    return [send(mine, mine, sends, receives, d - 1, ids[d]) for d in range(1, len(ids))]
+
+
+def finish(*generators):
+    active = list(generators)
+    while active:
+        active = [g for g in active if next(g, active) is not active]
 
 
 def rms_scale(values):
@@ -463,66 +577,168 @@
     return back, jnp.sum(grad * values * scale, axis=0, keepdims=True)
 
 
-def middle_kernel(part_ref, tokens_ref, gain_ref, second_ref, middle_ref, recv, red_s, red_r, gat_s, gat_r):
-    me, places, ids = ring_places("head")
-    rows = middle_ref.shape[0]
-    mine = pl.ds(pl.multiple_of(me * rows, rows), rows)
-    start_barrier(ids[1:])
-    copies = start_reduce(part_ref, recv, red_s, red_r, places, ids, rows)
-    middle = tokens_ref[mine].astype(F32) + end_reduce(copies, part_ref, recv, me, rows)
-    second_ref[mine] = (middle * rms_scale(middle) * gain_ref[...]).astype(BF16)
-    copies = start_gather(second_ref, gat_s, gat_r, me, ids, rows)
+def middle_kernel(part_ref, tokens_ref, gain_ref, second_ref, middle_ref, landing, red_s, red_r, gat_s, gat_r):
+    ring = ring_ids("y")
+    me = ring[0]
+    start_barrier(ring[4:])
+    finish(ring_reduce(ring, part_ref, middle_ref, landing, red_s, red_r))
+    middle = tokens_ref[me].astype(F32) + middle_ref[...]
+    second_ref[me] = (middle * rms_scale(middle) * gain_ref[...]).astype(BF16)
+    gather = ring_gather(ring, second_ref, gat_s, gat_r)
+    next(gather)
     middle_ref[...] = middle
-    for copy in copies:
-        copy.wait()
+    finish(gather)
 
 
 def middle_back_kernel(
-    part_ref, middle_ref, cotangent_ref, gain_ref, branch_ref, grad_ref, grad_gain_ref, recv, red_s, red_r, gat_s, gat_r
+    part_ref, middle_ref, cotangent_ref, gain_ref, branch_ref, grad_ref, grad_gain_ref, landing, red_s, red_r, gat_s, gat_r
 ):
-    me, places, ids = ring_places("head")
-    rows = middle_ref.shape[0]
-    mine = pl.ds(pl.multiple_of(me * rows, rows), rows)
-    start_barrier(ids[1:])
-    copies = start_reduce(part_ref, recv, red_s, red_r, places, ids, rows)
-    grad_second = end_reduce(copies, part_ref, recv, me, rows)
-    back, grad_gain = rms_back(grad_second, middle_ref[...], gain_ref[...])
-    grad = cotangent_ref[mine].astype(F32) + back
-    branch_ref[mine] = grad.astype(BF16)
-    copies = start_gather(branch_ref, gat_s, gat_r, me, ids, rows)
+    ring = ring_ids("y")
+    me = ring[0]
+    start_barrier(ring[4:])
+    finish(ring_reduce(ring, part_ref, grad_ref, landing, red_s, red_r))
+    back, grad_gain = rms_back(grad_ref[...], middle_ref[...], gain_ref[...])
+    grad = cotangent_ref[me].astype(F32) + back
+    branch_ref[me] = grad.astype(BF16)
+    gather = ring_gather(ring, branch_ref, gat_s, gat_r)
+    next(gather)
     grad_ref[...] = grad
     grad_gain_ref[...] = grad_gain
-    for copy in copies:
-        copy.wait()
-
-
-def tokens_back_kernel(
-    normed_part_ref, ffn_part_ref, tokens_ref, middle_ref, grad_ref, gain_ref, output_ref, grad_tokens_ref, grad_gain_ref,
-    low_ref, recv, recv_2, red_s, red_r, gat_s, gat_r, red_s2, red_r2, gat_s2, gat_r2,
+    finish(gather)
+
+
+def swap_add(value, partner, outgoing, incoming, sends, receives, slot, mask=None):
+    outgoing[slot] = value
+    copy = send(outgoing.at[slot], incoming.at[slot], sends, receives, slot, partner)
+    yield
+    copy.wait()
+    other = incoming[slot]
+    return value + (other if mask is None else jnp.where(mask, other, 0.0))
+
+
+def last_kernel(
+    heads, slab, normed_part_ref, ffn_part_ref, tokens_ref, middle_ref, grad_ref, gain_ref, small_ref,
+    split_ref, split_sib_ref, proj_ref, proj_sib_ref, branch_ref, branch_sib_ref, gated_ref, gated_sib_ref,
+    output_ref, low_ref, small_out_ref, first_a_ref, first_b_ref,
+    land_n, land_f, sum_n, sum_f, swap_out, swap_in, part_a, part_b, land_a, land_b, mid_a, mid_b, land_a2, land_b2,
+    rn_s, rn_r, gn_s, gn_r, rf_s, rf_r, gf_s, gf_r, sw_s, sw_r, a1_s, a1_r, b1_s, b1_r, a2_s, a2_r, b2_s, b2_r,
 ):
-    me, places, ids = ring_places("head")
-    rows = middle_ref.shape[0]
-    mine = pl.ds(pl.multiple_of(me * rows, rows), rows)
-    start_barrier(ids[1:])
-    copies = start_reduce(normed_part_ref, recv, red_s, red_r, places, ids, rows)
-    copies_2 = start_reduce(ffn_part_ref, recv_2, red_s2, red_r2, places, ids, rows)
-    grad_normed = end_reduce(copies, normed_part_ref, recv, me, rows)
-    back, grad_gain = rms_back(grad_normed, tokens_ref[mine].astype(F32), gain_ref[...])
-    low_ref[mine] = (grad_ref[...] + back).astype(BF16)
-    copies = start_gather(low_ref, gat_s, gat_r, me, ids, rows)
-    grad_gain_ref[...] = grad_gain
-    output_ref[mine] = (middle_ref[...] + end_reduce(copies_2, ffn_part_ref, recv_2, me, rows)).astype(BF16)
-    copies_2 = start_gather(output_ref, gat_s2, gat_r2, me, ids, rows)
-    for copy in copies:
-        copy.wait()
-    grad_tokens_ref[...] = low_ref[...].astype(F32)
-    for copy in copies_2:
-        copy.wait()
+    seq, head = lax.axis_index("seq"), lax.axis_index("head")
+    core = seq % 2
+    ring_x, ring_y, ring_z = ring_ids("x"), ring_ids("y"), ring_ids("z")
+    sibling = (seq + 1 - 2 * core, head)
+    start_barrier(ring_x[4:] + ring_y[4:] + ring_z[4:] + (sibling,))
+    me = ring_y[0]
+    reduce_n = ring_reduce(ring_y, normed_part_ref, sum_n, land_n, rn_s, rn_r)
+    next(reduce_n)
+
+    half = split_ref.shape[1] // 2
+    own = core * half
+    wide_a, wide_b = part_a.shape[2], part_b.shape[2]
+    rest = proj_ref.shape[1] - wide_a
+    places = 4
+    many = places * slab
+
+    def product(x, x_sib, y, y_sib, block, columns):
+        at = pl.ds(pl.multiple_of(own + block * many, many), many)
+        here = pl.ds(pl.multiple_of(block * many, many), many)
+        return mtm(x[:, at], y[:, columns]) + mtm(x_sib[:, here], y_sib[:, columns])
+
+    @pl.loop(0, places)
+    def _(block):
+        rows = pl.ds(pl.multiple_of(block * slab, slab), slab)
+        in_part = product(split_ref, split_sib_ref, proj_ref, proj_sib_ref, block, pl.ds(wide_a, rest)).astype(BF16)
+        out_part = product(branch_ref, branch_sib_ref, gated_ref, gated_sib_ref, block, pl.ds(0, wide_b - rest)).astype(BF16)
+        for place in range(places):
+            part_b[place, rows, :rest] = in_part[place * slab : (place + 1) * slab]
+            part_b[place, rows, rest:] = out_part[place * slab : (place + 1) * slab]
+
+    reduce_b = ring_reduce(ring_z, part_b, mid_b, land_b, b1_s, b1_r)
+    next(reduce_b)
+
+    @pl.loop(0, places)
+    def _(block):
+        part_a[block] = product(split_ref, split_sib_ref, proj_ref, proj_sib_ref, block, pl.ds(0, wide_a)).astype(BF16)
+
+    reduce_a = ring_reduce(ring_x, part_a, mid_a, land_a, a1_s, a1_r)
+    next(reduce_a)
+
+    next(reduce_n)
+    finish(reduce_n)
+    back, grad_gain = rms_back(sum_n[...], tokens_ref[me].astype(F32), gain_ref[...])
+    low_ref[me] = (grad_ref[...] + back).astype(BF16)
+    gather_n = ring_gather(ring_y, low_ref, gn_s, gn_r)
+    next(gather_n)
+    reduce_f = ring_reduce(ring_y, ffn_part_ref, sum_f, land_f, rf_s, rf_r)
+    next(reduce_f)
+    next(reduce_b)
+    next(reduce_a)
+    next(gather_n)
+
+    def all_small():
+        rows8, lanes = iota(small_ref.shape, 0), iota(small_ref.shape, 1)
+        value = small_ref[...] + jnp.where(rows8 == 0, grad_gain, 0.0)
+        shared = (rows8 < 2) | ((rows8 == 2) & (lanes < DV))
+        slot = 0
+        for ring, mask in ((ring_y, shared), (ring_x, None), (ring_z, None)):
+            place, right_id, left_id = ring[0], ring[4], ring[5]
+            even = lax.rem(place, 2) == 0
+            for flip in (False, True):
+                ids = tuple(
+                    jnp.where(jnp.logical_xor(even, flip), r, l) for r, l in zip(right_id, left_id)
+                )
+                value = yield from swap_add(value, ids, swap_out, swap_in, sw_s, sw_r, slot, mask)
+                slot += 1
+        value = yield from swap_add(value, sibling, swap_out, swap_in, sw_s, sw_r, slot)
+        small_out_ref[...] = value
+
+    small = all_small()
+    next(small)
+    next(reduce_f)
+    next(small)
+    next(small)
+    finish(reduce_b)
+    reduce_b2 = ring_reduce(ring_x, mid_b.reshape(places, slab, wide_b), first_b_ref, land_b2, b2_s, b2_r)
+    next(reduce_b2)
+    finish(reduce_a)
+    reduce_a2 = ring_reduce(ring_z, mid_a.reshape(places, slab, wide_a), first_a_ref, land_a2, a2_s, a2_r)
+    next(reduce_a2)
+    finish(reduce_f)
+    output_ref[me] = (middle_ref[...] + sum_f[...]).astype(BF16)
+    gather_f = ring_gather(ring_y, output_ref, gf_s, gf_r)
+    next(gather_f)
+    next(reduce_b2)
+    next(reduce_a2)
+    finish(small, gather_n, gather_f, reduce_b2, reduce_a2)
+
+
+def mlp_grads(second_ref, cotangent_ref, gate_up_ref, hidden_ref, out_ref):
+    wide = gate_up_ref.shape[1]
+    out_ref[:, :wide] = mtm(second_ref[...], gate_up_ref[...]).astype(BF16)
+    out_ref[:, wide:] = mtm(cotangent_ref[...], hidden_ref[...]).astype(BF16)
+
+
+def finish_kernel(heads, first_a_ref, first_b_ref, mlp_ref, low_ref, in_ref, rate_ref, out_ref, gate_up_ref, down_ref, tokens_ref):
+    wide = first_a_ref.shape[1]
+    rates = heads * PROJ
+    both = jnp.concatenate([first_a_ref[...], first_b_ref[...]], axis=1)
+    for h in range(heads):
+        in_ref[:, h] = both[:, h * PROJ : (h + 1) * PROJ]
+        out_ref[:, h] = both[:, rates + LANES + h * DV : rates + LANES + (h + 1) * DV]
+    for g in range(2):
+        rate_ref[:, g] = both[:, rates + g * heads : rates + (g + 1) * heads]
+    units = down_ref.shape[1]
+    for g in range(2):
+        gate_up_ref[:, g] = mlp_ref[:, g * units : (g + 1) * units].astype(F32)
+    down_ref[...] = mlp_ref[:, 2 * units :].astype(F32)
+    tokens_ref[...] = low_ref[...].astype(F32)
 
 
 def call(kernel, outs, *args, name):
     return pl.pallas_call(
         kernel,
+        in_specs=[pl.BlockSpec(memory_space=pltpu.VMEM)] * len(args),
+        out_specs=[pl.BlockSpec(memory_space=pltpu.VMEM)] * len(outs),
         out_shape=[jax.ShapeDtypeStruct(shape, kind) for shape, kind in outs],
         compiler_params=pltpu.CompilerParams(vmem_limit_bytes=VMEM_LIMIT),
         name=name,
@@ -598,13 +814,12 @@
     behind = shifted(tokens[count - HALO :], "seq", 1)
     source = jnp.concatenate([behind, tokens], axis=0).astype(F32)
     normed_long = (source * rms_scale(source) * mixer_gain).astype(BF16)
-    normed = normed_long[HALO:]
     projected = mm(normed_long, first_full)
 
     taps = conv_weight.reshape(KW, heads * CONV)
     scales = jnp.pad(jnp.stack([decay_log, decay_bias]), ((0, 6), (0, LANES - heads)))
-    queries, keys, values, inv, out_local, out_map, summary = call(
-        functools.partial(local_forward, heads),
+    queries, keys, values, inv, out_local, out_map, summary, normed_split = call(
+        functools.partial(local_forward, heads, slab),
         [
             ((heads, count, DK), BF16),
             ((heads, count, DK), BF16),
@@ -613,17 +828,19 @@
             ((heads, count, DV), F32),
             ((heads, count, DK), F32),
             ((units, DK, 2 * DK), BF16),
+            ((count, width), BF16),
         ],
         projected,
         taps,
         scales,
+        normed_long,
         name="local_forward",
     )
     block = (DK, DK)
     double = (DK, 2 * DK)
-    entering, kept, totals = remote_call(
+    entering, normed_sibling, kept, totals = remote_call(
         functools.partial(scan_forward, groups),
-        [((units, *block), BF16), ((units, *block), BF16), ((groups, *block), BF16)],
+        [((units, *block), BF16), ((count, width // 2), BF16), ((units, *block), BF16), ((groups, *block), BF16)],
         [
             pltpu.VMEM((units, *double), BF16),
             pltpu.VMEM((units, *double), F32),
@@ -631,10 +848,11 @@
             pltpu.VMEM((groups, *double), BF16),
             pltpu.VMEM((units, *block), BF16),
             pltpu.VMEM((units, *block), BF16),
-            *pairs(units, groups, units),
+            *pairs(units, groups, units, 1),
         ],
         1,
         summary,
+        normed_split,
         name="scan_forward",
     )
     gain_row = out_gain.reshape(1, DV)
@@ -649,17 +867,22 @@
         name="mix_outputs",
     )
     branch = mmt(gated, out_full)
-    ring = [pltpu.VMEM((sharers - 1, rows, width), BF16)]
+    def landing(*shape):
+        return pltpu.VMEM((6, *shape), BF16)
+
+    blocked = (sharers, rows, width)
+    ring = [landing(rows // 2, width)]
     second, middle = remote_call(
         middle_kernel,
-        [((count, width), BF16), ((rows, width), F32)],
-        ring + pairs(sharers - 1, sharers - 1),
+        [(blocked, BF16), ((rows, width), F32)],
+        ring + pairs(6, 6),
         2,
-        branch.astype(BF16),
-        tokens,
+        branch.astype(BF16).reshape(blocked),
+        tokens.reshape(blocked),
         ffn_gain.reshape(1, width),
         name="middle",
     )
+    second = second.reshape(count, width)
     gate_up = mm(second, gate_up_full)
     z, up = gate_up[:, :hidden_units], gate_up[:, hidden_units:]
     s = jax.nn.sigmoid(z)
@@ -670,36 +893,55 @@
         BF16
     )
     second_part = mmt(grad_gate_up, gate_up_full)
+    grad_mlp = pl.pallas_call(
+        mlp_grads,
+        grid=(width // 256,),
+        in_specs=[
+            pl.BlockSpec((count, 256), lambda i: (0, i)),
+            pl.BlockSpec((count, 256), lambda i: (0, i)),
+            pl.BlockSpec((count, 2 * hidden_units), lambda i: (0, 0)),
+            pl.BlockSpec((count, hidden_units), lambda i: (0, 0)),
+        ],
+        out_specs=pl.BlockSpec((256, 3 * hidden_units), lambda i: (i, 0)),
+        out_shape=jax.ShapeDtypeStruct((width, 3 * hidden_units), BF16),
+        compiler_params=pltpu.CompilerParams(vmem_limit_bytes=VMEM_LIMIT),
+        name="mlp_grads",
+    )(second, cotangent, grad_gate_up, hidden)
+    second_part, grad_mlp = lax.optimization_barrier((second_part.astype(BF16), grad_mlp))
+    grad_mlp = lax.psum_scatter(grad_mlp, "seq", scatter_dimension=0, tiled=True)
     grad_branch, grad_middle, grad_ffn_gain = remote_call(
         middle_back_kernel,
-        [((count, width), BF16), ((rows, width), F32), ((1, width), F32)],
-        ring + pairs(sharers - 1, sharers - 1),
+        [(blocked, BF16), ((rows, width), F32), ((1, width), F32)],
+        ring + pairs(6, 6),
         3,
-        second_part.astype(BF16),
+        second_part.reshape(blocked),
         middle,
-        cotangent,
+        cotangent.reshape(blocked),
         ffn_gain.reshape(1, width),
         name="middle_back",
     )
+    grad_branch = grad_branch.reshape(count, width)
     grad_gated = mm(grad_branch, out_full)
-    grad_mixed, grad_gate, grad_out_gain, carried = call(
-        functools.partial(mix_outputs_back, heads),
+    grad_mixed, grad_gate, grad_out_gain, carried, branch_split = call(
+        functools.partial(mix_outputs_back, heads, slab),
         [
             ((heads, count, DV), F32),
             ((count, heads * DV), BF16),
             ((1, DV), F32),
             ((units, DK, DK), BF16),
+            ((count, width), BF16),
         ],
         grad_gated,
         mixer_out,
         out_map,
         projected,
         gain_row,
+        grad_branch,
         name="mix_outputs_back",
     )
-    leaving = remote_call(
+    leaving, branch_sibling, gated_sibling = remote_call(
         functools.partial(scan_backward, groups),
-        [((units, *block), BF16)],
+        [((units, *block), BF16), ((count, width // 2), BF16), ((count, heads * DV), BF16)],
         [
             pltpu.VMEM((units, *block), BF16),
             pltpu.VMEM((units, *block), BF16),
@@ -709,23 +951,31 @@
             pltpu.VMEM((groups, *block), BF16),
             pltpu.VMEM((units, *block), BF16),
             pltpu.VMEM((units, *block), BF16),
-            *pairs(units, groups, units),
+            *pairs(units, groups, units, 2),
         ],
         4,
         carried,
         kept,
         totals,
+        branch_split,
+        gated,
         name="scan_backward",
-    )[0]
-    grad_projected, halo, tail, grad_taps, grad_scales = call(
+    )
+    grad_projected, grad_sibling, grad_taps, grad_scales = remote_call(
         functools.partial(local_backward, heads),
         [
             ((count, projections), BF16),
-            ((HALO, heads * CONV), F32),
-            ((HALO, heads * CONV), F32),
+            ((count, projections), BF16),
             ((KW, heads * CONV), F32),
             ((8, LANES), F32),
         ],
+        [
+            pltpu.VMEM((heads, HALO, CONV), F32),
+            pltpu.VMEM((heads, HALO, CONV), F32),
+            pltpu.VMEM((heads, 2 * HALO, CONV), F32),
+            *pairs(heads, heads, heads, 1),
+        ],
+        6,
         projected,
         taps,
         scales,
@@ -739,58 +989,102 @@
         grad_gate,
         name="local_backward",
     )
-    tail = (tail + shifted(halo, "seq", -1)).astype(BF16)
-    for h in range(heads):
-        grad_projected = lax.dynamic_update_slice(
-            grad_projected, tail[:, h * CONV : (h + 1) * CONV], (count - HALO, h * PROJ)
-        )
     normed_part = mmt(grad_projected, first_full)
-    output, grad_tokens, grad_mixer_gain = remote_call(
-        tokens_back_kernel,
-        [((count, width), BF16), ((count, width), F32), ((1, width), F32)],
-        [pltpu.VMEM((count, width), BF16)] + ring + ring + pairs(*[sharers - 1] * 4),
+    small = jnp.concatenate(
+        [
+            jnp.zeros((1, width), F32),
+            grad_ffn_gain,
+            jnp.concatenate(
+                [
+                    grad_out_gain,
+                    grad_scales[0:1],
+                    grad_scales[1:2],
+                    jnp.zeros((1, width - DV - 2 * LANES), F32),
+                ],
+                axis=1,
+            ),
+            grad_taps,
+            jnp.zeros((1, width), F32),
+        ],
+        axis=0,
+    )
+    wide_a = -(-(projections + heads * DV) // (2 * LANES)) * LANES
+    wide_b = projections + heads * DV - wide_a
+    many = 4 * slab
+    output, low, small, first_a, first_b = remote_call(
+        functools.partial(last_kernel, heads, slab),
+        [
+            (blocked, BF16),
+            (blocked, BF16),
+            ((8, width), F32),
+            ((slab, wide_a), F32),
+            ((slab, wide_b), F32),
+        ],
+        [
+            landing(rows // 2, width),
+            landing(rows // 2, width),
+            pltpu.VMEM((rows, width), F32),
+            pltpu.VMEM((rows, width), F32),
+            pltpu.VMEM((7, 8, width), F32),
+            pltpu.VMEM((7, 8, width), F32),
+            pltpu.VMEM((4, many, wide_a), BF16),
+            pltpu.VMEM((4, many, wide_b), BF16),
+            landing(many // 2, wide_a),
+            landing(many // 2, wide_b),
+            pltpu.VMEM((many, wide_a), BF16),
+            pltpu.VMEM((many, wide_b), BF16),
+            landing(slab // 2, wide_a),
+            landing(slab // 2, wide_b),
+            *pairs(6, 6, 6, 6, 7, 6, 6, 6, 6),
+        ],
         5,
-        normed_part.astype(BF16),
-        ffn_part.astype(BF16),
-        tokens,
+        normed_part.astype(BF16).reshape(blocked),
+        ffn_part.astype(BF16).reshape(blocked),
+        tokens.reshape(blocked),
         middle,
         grad_middle,
         mixer_gain.reshape(1, width),
-        name="tokens_back",
-    )
-    grad_rest = jnp.concatenate(
+        small,
+        normed_split,
+        normed_sibling,
+        grad_projected,
+        grad_sibling,
+        branch_split,
+        branch_sibling,
+        gated,
+        gated_sibling,
+        name="last",
+    )
+    grad_in, grad_rate, grad_out, grad_gate_up_weight, grad_down, grad_tokens = call(
+        functools.partial(finish_kernel, heads),
         [
-            mtm(grad_branch, gated).astype(BF16),
-            mtm(second, grad_gate_up).astype(BF16),
-            mtm(cotangent, hidden).astype(BF16),
+            ((slab, heads, PROJ), F32),
+            ((slab, 2, heads), F32),
+            ((slab, heads, DV), F32),
+            ((slab, 2, hidden_units), F32),
+            ((slab, hidden_units), F32),
+            ((count, width), F32),
         ],
-        axis=1,
-    )
-    grad_first = mtm(normed, grad_projected).astype(BF16)
-    grad_rest = lax.psum_scatter(grad_rest, "seq", scatter_dimension=0, tiled=True).astype(F32)
-    grad_first = lax.psum_scatter(grad_first, "seq", scatter_dimension=0, tiled=True).astype(F32)
-    gains = jnp.concatenate([grad_mixer_gain[0], grad_ffn_gain[0], grad_out_gain[0]])
-    gains = lax.psum(gains, ("seq", "head"))
-    small = jnp.concatenate([grad_taps.reshape(-1), grad_scales[0, :heads], grad_scales[1, :heads]])
-    small = lax.psum(small, "seq")
-    at_taps = KW * heads * CONV
-    rates_at = heads * PROJ
-    gate_at = heads * DV
-    down_at = gate_at + 2 * hidden_units
+        first_a,
+        first_b,
+        grad_mlp,
+        low.reshape(count, width),
+        name="finish",
+    )
     return (
-        output,
+        output.reshape(count, width),
         grad_tokens,
-        gains[:width],
-        grad_first[:, :rates_at].reshape(slab, heads, PROJ),
-        grad_first[:, rates_at : rates_at + 2 * heads].reshape(slab, 2, heads),
-        small[:at_taps].reshape(KW, heads, CONV),
-        small[at_taps : at_taps + heads],
-        small[at_taps + heads :],
-        gains[2 * width :],
-        grad_rest[:, :gate_at].reshape(slab, heads, DV),
-        gains[width : 2 * width],
-        grad_rest[:, gate_at:down_at].reshape(slab, 2, hidden_units),
-        grad_rest[:, down_at:],
+        small[0],
+        grad_in,
+        grad_rate,
+        small[3 : 3 + KW].reshape(KW, heads, CONV),
+        small[2, DV : DV + heads],
+        small[2, DV + LANES : DV + LANES + heads],
+        small[2, :DV],
+        grad_out,
+        small[1],
+        grad_gate_up_weight,
+        grad_down,
     )
 
 

time: 639 us -> 434 us (0.68)
  blocking collectives: 188 us -> 0 us
  Pallas kernels: 208 us -> 251 us
  matrix products: 76.8 us -> 54.9 us
  local copies, waits for them, and re-layouts: 30 us -> 13.8 us
  other arithmetic: 16.7 us -> 3.31 us
  waiting for transfers between devices: 94.3 us -> 87.7 us
    psum x2 -> x0, blocking collectives: 188 us -> none  [the longest x1 120 us: per_device(): small = lax.psum(small, 'seq')]
    pallas_call x5 -> x6, Pallas kernels: 164 us -> 208 us  [remote_call(): pl.pallas_call(kernel, in_specs=[pl.BlockSpec(memory_space=pltpu.VMEM)] *...]
    dot_general x12 -> x8, matrix products: 76.8 us -> 54.9 us  [dot(): lax.dot_general(a, b, (dims, ((), ())), precision=precision, preferred_el...]
    concatenate x2, other arithmetic: 13.7 us -> 1.2 us  [the longest x1 1.2 us: per_device(): jnp.concatenate([grad_hidden * up * s * (1.0 + z * (1.0 - s)), grad_hidde...]
    convert_element_type x1 -> x0, local copies, waits for them, and re-layouts: 6.64 us -> none  [per_device(): mtm(grad_branch, gated).astype(BF16)]
    pallas_call x4 -> x5, Pallas kernels: 44.3 us -> 42.8 us  [the longest x4 31 us: call(): pl.pallas_call(kernel, in_specs=[pl.BlockSpec(memory_space=pltpu.VMEM)] *...]
  transfers between devices with their start and end apart: 6 -> 4, of which waited for: 3 -> 2; matrix products, arithmetic and copies ran while one was open for 11% -> 9% of each run, Pallas kernels for 15% -> 49%
where the time goes in v2:
time: 434 us; the launch traced here: 430 us
  Pallas kernels  251 us (58%)
  waiting for transfers between devices  87.7 us (20%)
  matrix products  54.9 us (13%)
  between operations  14.4 us (3%)
  local copies, waits for them, and re-layouts  13.8 us (3%)
  starting transfers between devices  5.06 us (1%)
    pallas_call x6, Pallas kernels, remote_call(): pl.pallas_call(kernel, in_specs=[pl.BlockSpec(memory_space=pltpu.VMEM)] *...  208 us
    all_gather x1, waiting for transfers between devices, per_device(): first_full = lax.all_gather(first, 'seq', axis=0, tiled=True)  60.6 us
    dot_general x8, matrix products, dot(): lax.dot_general(a, b, (dims, ((), ())), precision=precision, preferred_el...  54.9 us
    pallas_call x4, Pallas kernels, call(): pl.pallas_call(kernel, in_specs=[pl.BlockSpec(memory_space=pltpu.VMEM)] *...  31 us
    all_gather x1, waiting for transfers between devices, per_device(): rest_full = lax.all_gather(rest, 'seq', axis=0, tiled=True)  27.1 us
    pallas_call x1, Pallas kernels, per_device(): pl.pallas_call(mlp_grads, grid=(width // 256,), in_specs=[pl.BlockSpec((c...  11.8 us
  transfers between devices with their start and end apart: 4, of which 2 were waited for; matrix products, arithmetic and copies ran while one was open for 9% of the time, Pallas kernels for 49%

profile of v2, /device:TPU:1, one launch (start us, length us, event | category | flops | bytes accessed | tf_op | source)
XLA Modules:
  0.0 430.0 jit_solution(10520352632725238250)
XLA Ops:
  8.1 1.0 copy.30
  10.2 0.9 pad_maximum_fusion.2
  11.2 4.9 %collective-permute-start = (bf16[8,2048]{1,0:T(8,128)(2,1)S(1)}, bf16[8,2048]{1,0:T(8,128)(2,1)S(1)}, u32[]{:S(2)}, u32[]{:S(2)}) collective-permute-start(bf16[8,2048]{1,0:T(8,128)(2,1)S(1)} %slice.42), channel_id=1, source_target_pairs={{0,4},{4,8},{8,12},{12,16},{16,20},{20,24},{24,28},{28,32},{32,36}... | collective-permute-start | bytes 98312 | tf_op jit(solution)/shard_map/ppermute | solution.py:769
  18.1 60.6 %all-gather.3.cloned.1.call-done = bf16[2048,3200]{1,0:T(8,128)(2,1)} async-done(((bf16[64,3200]{1,0:T(8,128)(2,1)}), bf16[2048,3200]{1,0:T(8,128)(2,1)}) %all-gather.3.cloned.1.call-update) | async-done | bytes 13107216 | tf_op jit(solution)/shard_map/all_gather | solution.py:808
  78.7 8.9 %fusion.29.proj_ref = f32[264,3200]{1,0:T(8,128)} fusion(bf16[264,2048]{1,0:T(8,128)(2,1)S(1)} %fusion.26.normed_ref, bf16[2048,3200]{1,0:T(8,128)(2,1)} %all-gather.3.cloned.1.call-done), kind=kOutput, calls=%fused_computation.38 | convolution fusion | flops 3460300800 | bytes 17567744 | tf_op jit(solution)/shard_map/dot_general | solution.py:28
  87.5 15.7 %local_forward.1 = (bf16[4,256,128]{2,1,0:T(8,128)(2,1)}, bf16[4,256,128]{2,1,0:T(8,128)(2,1)}, bf16[4,256,256]{2,1,0:T(8,128)(2,1)}, f32[4,256,256]{2,1,0:T(8,1...) custom-call(f32[264,3200]{1,0:T(8,128)} %fusion.29.proj_ref, ...), custom_call_target="tpu_custom_call" | custom-call | tf_op jit(solution)/shard_map/local_forward/pallas_call | solution.py:738
  103.2 32.5 %scan_forward.1 = (bf16[8,128,128]{2,1,0:T(8,128)(2,1)}, bf16[256,1024]{1,0:T(8,128)(2,1)}, bf16[8,128,128]{2,1,0:T(8,128)(2,1)}, bf16[4,128,128]{2,1,0:T(8,128)(2,1)}) custom-call(bf16[8,128,256]{2,1,0:T(8,128)(2,1)} %get-tuple-element.63.pack_ref, bf16[256,2048]{1,0:T(8,128)(2,1)} %get-tuple-element.64.split_ref), custom_call_target="tpu_custom_call" | custom-call | tf_op jit(solution)/shard_map/scan_forward/pallas_call | solution.py:749
  135.8 4.6 %mix_outputs.1 = (f32[4,256,256]{2,1,0:T(8,128)}, bf16[256,1024]{1,0:T(8,128)(2,1)}) custom-call(f32[4,256,256]{2,1,0:T(8,128)} %get-tuple-element.61.out_ref, f32[4,256,128]{2,1,0:T(8,128)} %get-tuple-element.62.map_ref, bf16[8,128,128]{2,1,0:T(8,128)(2,1)} %get-tuple-element.65.state_ref, f32[264,3200]{1,0:T(8,128)} %fusion.29.proj_ref, f32[1,256]{1,0:T(1,128)} %bitcast.71), custom_call_target="tpu_custom_call" | custom-call | tf_op jit(solution)/shard_map/mix_outputs/pallas_call | solution.py:738
  140.4 27.1 %all-gather.5.cloned.1.call-done = bf16[2048,5248]{1,0:T(8,128)(2,1)} async-done(((bf16[64,5248]{1,0:T(8,128)(2,1)}), bf16[2048,5248]{1,0:T(8,128)(2,1)}) %all-gather.5.cloned.1.call-update) | async-done | bytes 21495824 | tf_op jit(solution)/shard_map/all_gather | solution.py:809
  167.4 4.6 %fusion.18 = bf16[256,2048]{1,0:T(8,128)(2,1)} fusion(bf16[256,1024]{1,0:T(8,128)(2,1)} %get-tuple-element.66.gated_ref, bf16[2048,5248]{1,0:T(8,128)(2,1)} %all-gather.5.cloned.1.call-done), kind=kOutput, calls=%fused_computation.16 | convolution fusion | flops 1074266112 | bytes 5767168 | tf_op jit(solution)/shard_map/dot_general | solution.py:28
  172.0 25.8 %middle.1 = (bf16[4,64,2048]{2,1,0:T(8,128)(2,1)}, f32[64,2048]{1,0:T(8,128)}) custom-call(bf16[4,64,2048]{2,1,0:T(8,128)(2,1)} %bitcast.54, bf16[4,64,2048]{2,1,0:T(8,128)(2,1)} %bitcast.43, f32[1,2048]{1,0:T(1,128)} %bitcast.64), custom_call_target="tpu_custom_call" | custom-call | tf_op jit(solution)/shard_map/middle/pallas_call | solution.py:749
  197.8 6.6 %fusion.2 = f32[256,2816]{1,0:T(8,128)S(1)} fusion(bf16[256,2048]{1,0:T(8,128)(2,1)} %bitcast.56, bf16[2048,5248]{1,0:T(8,128)(2,1)} %all-gather.5.cloned.1.call-done), kind=kOutput, calls=%fused_computation.2 | convolution fusion | flops 2952790016 | bytes 15466496 | tf_op jit(solution)/shard_map/dot_general | solution.py:28
  204.5 5.8 %multiply_convert_fusion.2 = (bf16[256,1408]{1,0:T(8,128)(2,1)S(1)}, bf16[256,1408]{1,0:T(8,128)(2,1)S(1)}, bf16[256,1408]{1,0:T(8,128)(2,1)}) fusion(f32[256,2816]{1,0:T(8,128)S(1)} %fusion.2, bf16[256,2048]{1,0:T(8,128)(2,1)S(1)} %copy-done.2, bf16[2048,5248]{1,0:T(8,128)(2,1)} %all-gather.5.cloned.1.call-done), kind=kOutput, calls=%fused_computation.25 | convolution fusion | flops 1482162176 | bytes 11862016 | tf_op jit(solution)/shard_map/dot_general | solution.py:28
  210.2 1.2 pad_maximum_fusion.gate_up_ref
  211.4 11.8 %mlp_grads.1 = bf16[2048,4224]{1,0:T(8,128)(2,1)} custom-call(bf16[256,2048]{1,0:T(8,128)(2,1)} %bitcast.57, bf16[256,2048]{1,0:T(8,128)(2,1)} %cotangent_ref.1, bf16[256,2816]{1,0:T(8,128)(2,1)} %pad_maximum_fusion.gate_up_ref, bf16[256,1408]{1,0:T(8,128)(2,1)} %get-tuple-element.116.hidden_ref), custom_call_target="tpu_custom_call" | custom-call | tf_op jit(solution)/shard_map/mlp_grads/pallas_call | solution.py:896
  223.2 8.4 %fusion.15 = bf16[256,2048]{1,0:T(8,128)(2,1)} fusion(bf16[2048,5248]{1,0:T(8,128)(2,1)} %all-gather.5.cloned.1.call-done, bf16[256,1408]{1,0:T(8,128)(2,1)S(1)} %get-tuple-element.115, bf16[256,1408]{1,0:T(8,128)(2,1)S(1)} %get-tuple-element.114), kind=kOutput, calls=%fused_computation.15 | convolution fusion | flops 2956197888 | bytes 14024704 | tf_op jit(solution)/shard_map/dot_general | solution.py:28
  231.7 21.7 %middle_back.1 = (bf16[4,64,2048]{2,1,0:T(8,128)(2,1)}, f32[64,2048]{1,0:T(8,128)}, f32[1,2048]{1,0:T(1,128)}) custom-call(bf16[4,64,2048]{2,1,0:T(8,128)(2,1)} %bitcast.53, f32[64,2048]{1,0:T(8,128)} %get-tuple-element.69.middle_ref, bf16[4,64,2048]{2,1,0:T(8,128)(2,1)} %bitcast.45, f32[1,2048]{1,0:T(1,128)} %bitcast.65), custom_call_target="tpu_custom_call" | custom-call | tf_op jit(solution)/shard_map/middle_back/pallas_call | solution.py:749
  253.4 5.3 %fusion.8.grad_ref = f32[256,1024]{1,0:T(8,128)} fusion(bf16[256,2048]{1,0:T(8,128)(2,1)} %bitcast.50, bf16[2048,5248]{1,0:T(8,128)(2,1)} %all-gather.5.cloned.1.call-done), kind=kOutput, calls=%fused_computation.8 | convolution fusion | flops 1073741824 | bytes 6291456 | tf_op jit(solution)/shard_map/dot_general | solution.py:28
  258.7 6.7 %mix_outputs_back.1 = (f32[4,256,256]{2,1,0:T(8,128)}, bf16[256,1024]{1,0:T(8,128)(2,1)}, f32[1,256]{1,0:T(1,128)}, bf16[8,128,128]{2,1,0:T(8,128)(2,1)}, bf16[256,2048]{1,0:T(8,128)(2,1)}) custom-call(f32[256,1024]{1,0:T(8,128)} %fusion.8.grad_ref, f32[4,256,256]{2,1,0:T(8,128)} %get-tuple-element.71.mixed_ref, f32[4,256,128]{2,1,0:T(8,128)} %get-tuple-element.62.map_ref, ...), custom_call_target="tpu_custom_call" | custom-call | tf_op jit(solution)/shard_map/mix_outputs_back/pallas_call | solution.py:738
  265.4 25.2 %scan_backward.1 = (bf16[8,128,128]{2,1,0:T(8,128)(2,1)}, bf16[256,1024]{1,0:T(8,128)(2,1)}, bf16[256,1024]{1,0:T(8,128)(2,1)}) custom-call(bf16[8,128,128]{2,1,0:T(8,128)(2,1)} %get-tuple-element.73.pack_ref, bf16[8,128,128]{2,1,0:T(8,128)(2,1)} %get-tuple-element.74.kept_ref, bf16[4,128,128]{2,1,0:T(8,128)(2,1)} %get-tuple-element.75.totals_ref, ...), custom_call_target="tpu_custom_call" | custom-call | tf_op jit(solution)/shard_map/scan_backward/pallas_call | solution.py:749
  290.7 26.0 %local_backward.1 = (bf16[256,3200]{1,0:T(8,128)(2,1)}, bf16[256,3200]{1,0:T(8,128)(2,1)}, f32[4,2048]{1,0:T(4,128)}, f32[8,128]{1,0:T(8,128)}) custom-call(f32[264,3200]{1,0:T(8,128)} %fusion.29.proj_ref, f32[4,2048]{1,0:T(4,128)} %bitcast.62, f32[8,128]{1,0:T(8,128)} %select_maximum_fusion.scales_ref, bf16[4,256,128]{2,1,0:T(8,128)(2,1)} %get-tuple-element.57.q_ref, ...), custom_call_target="tpu_custom_call" | custom-call | tf_op jit(solution)/shard_map/local_backward/pallas_call | solution.py:749
  317.5 1.4 concatenate.24.small_ref
  318.9 5.6 %fusion.21 = bf16[256,2048]{1,0:T(8,128)(2,1)} fusion(bf16[256,1408]{1,0:T(8,128)(2,1)S(1)} %copy-done.5, bf16[2048,5248]{1,0:T(8,128)(2,1)} %all-gather.5.cloned.1.call-done), kind=kOutput, calls=%fused_computation.17 | convolution fusion | flops 1476919296 | bytes 7536640 | tf_op jit(solution)/shard_map/dot_general | solution.py:28
  324.6 9.7 %convolution_convert_fusion = bf16[256,2048]{1,0:T(8,128)(2,1)} fusion(bf16[256,3200]{1,0:T(8,128)(2,1)S(1)} %copy-done.3, bf16[2048,3200]{1,0:T(8,128)(2,1)} %all-gather.3.cloned.1.call-done), kind=kOutput, calls=%fused_computation.18 | convolution fusion | flops 3355967488 | bytes 15794176 | tf_op jit(solution)/shard_map/dot_general | solution.py:28
  334.3 76.9 %last.1 = (bf16[4,64,2048]{2,1,0:T(8,128)(2,1)}, bf16[4,64,2048]{2,1,0:T(8,128)(2,1)}, f32[8,2048]{1,0:T(8,128)}, f32[64,2176]{1,0:T(8,128)}, f32[64,2048]{1,0:T(8,128)}) custom-call(bf16[4,64,2048]{2,1,0:T(8,128)(2,1)} %bitcast.49, bf16[4,64,2048]{2,1,0:T(8,128)(2,1)} %bitcast.48, bf16[4,64,2048]{2,1,0:T(8,128)(2,1)} %bitcast.44, ...), custom_call_target="tpu_custom_call" | custom-call | tf_op jit(solution)/shard_map/last/pallas_call | solution.py:749
  411.2 1.3 slice.54
  412.5 0.8 slice.51
  414.0 1.2 slice_bitcast_fusion
  415.2 1.5 fusion.27
  416.7 4.0 finish.1
  420.8 1.5 copy.28
  422.3 1.0 copy.35
  (55 shorter events, 5.3 us)
Async XLA Ops:
  7.2 2.9 copy-start.8
  7.2 3.0 copy-start.6
  7.2 3.0 copy-start.7
  7.2 71.4 %all-gather.3.cloned.1.call-start = ((), (), s32[]{:S(2)}) async-start(), calls=%async_computation.1 | async-start | bytes 13516800 | tf_op jit(solution)/shard_map/all_gather | solution.py:808
  9.1 2.1 copy-start
  9.2 7.0 %copy-start.13 = (f32[4]{0:T(128)S(1)}, f32[4]{0:T(128)}, u32[]{:S(2)}) copy-start(f32[4]{0:T(128)} %param.19) | copy-start | bytes 52
  9.2 7.0 %copy-start.14 = (f32[4]{0:T(128)S(1)}, f32[4]{0:T(128)}, u32[]{:S(2)}) copy-start(f32[4]{0:T(128)} %param.18) | copy-start | bytes 52
  9.2 7.6 %copy-start.10 = (f32[4,4,512]{2,1,0:T(4,128)S(1)}, f32[4,4,512]{2,1,0:T(4,128)}, u32[]{:S(2)}) copy-start(f32[4,4,512]{2,1,0:T(4,128)} %param.17) | copy-start | bytes 98308
  10.1 7.7 %copy-start.9 = (f32[2048]{0:T(1024)S(1)}, f32[2048]{0:T(1024)}, u32[]{:S(2)}) copy-start(f32[2048]{0:T(1024)} %param.14) | copy-start | bytes 24580
  10.1 157.4 %all-gather.5.cloned.1.call-start = ((), (), s32[]{:S(2)}) async-start(), calls=%async_computation.2 | async-start | bytes 22167552 | tf_op jit(solution)/shard_map/all_gather | solution.py:809
  11.1 405.6 %reduce-scatter.2.cloned.1.call-start = ((), (), s32[]{:S(2)}) async-start(), calls=%async_computation.3 | async-start | bytes 17842176 | tf_op jit(solution)/shard_map/reduce_scatter | solution.py:911
  11.2 6.2 %collective-permute-start = (bf16[8,2048]{1,0:T(8,128)(2,1)S(1)}, bf16[8,2048]{1,0:T(8,128)(2,1)S(1)}, u32[]{:S(2)}, u32[]{:S(2)}) collective-permute-start(bf16[8,2048]{1,0:T(8,128)(2,1)S(1)} %slice.42), channel_id=1, source_target_pairs={{0,4},{4,8},{8,12},{12,16},{16,20},{20,24},{24,28},{28,32},{32,36}... | collective-permute-start | bytes 98312 | tf_op jit(solution)/shard_map/ppermute | solution.py:769
  18.1 69.5 %copy-start.1 = (bf16[264,2048]{1,0:T(8,128)(2,1)}, bf16[264,2048]{1,0:T(8,128)(2,1)S(1)}, u32[]{:S(2)}) copy-start(bf16[264,2048]{1,0:T(8,128)(2,1)S(1)} %fusion.26.normed_ref) | copy-start | bytes 3244036
  197.8 6.7 %copy-start.2 = (bf16[256,2048]{1,0:T(8,128)(2,1)S(1)}, bf16[256,2048]{1,0:T(8,128)(2,1)}, u32[]{:S(2)}) copy-start(bf16[256,2048]{1,0:T(8,128)(2,1)} %cotangent_ref.1) | copy-start | bytes 3145732
  290.6 26.8 %copy-start.12 = (f32[1,256]{1,0:T(1,128)S(1)}, f32[1,256]{1,0:T(1,128)}, u32[]{:S(2)}) copy-start(f32[1,256]{1,0:T(1,128)} %get-tuple-element.82) | copy-start | bytes 3076
  290.6 26.8 %copy-start.11 = (f32[1,2048]{1,0:T(1,128)S(1)}, f32[1,2048]{1,0:T(1,128)}, u32[]{:S(2)}) copy-start(f32[1,2048]{1,0:T(1,128)} %get-tuple-element.81) | copy-start | bytes 24580
  290.7 28.3 %copy-start.5 = (bf16[256,1408]{1,0:T(8,128)(2,1)S(1)}, bf16[256,1408]{1,0:T(8,128)(2,1)}, u32[]{:S(2)}) copy-start(bf16[256,1408]{1,0:T(8,128)(2,1)} %get-tuple-element.116.hidden_ref) | copy-start | bytes 2162692
  318.9 5.7 %copy-start.3 = (bf16[256,3200]{1,0:T(8,128)(2,1)S(1)}, bf16[256,3200]{1,0:T(8,128)(2,1)}, u32[]{:S(2)}) copy-start(bf16[256,3200]{1,0:T(8,128)(2,1)} %get-tuple-element.79.proj_ref) | copy-start | bytes 4915204
  411.2 11.1 %copy-start.4 = (bf16[4,64,2048]{2,1,0:T(8,128)(2,1)S(1)}, bf16[4,64,2048]{2,1,0:T(8,128)(2,1)}, u32[]{:S(2)}) copy-start(bf16[4,64,2048]{2,1,0:T(8,128)(2,1)} %get-tuple-element.89) | copy-start | bytes 3145732
Sparse Core Ops, SparseCore 0:
  10.9 67.7 all-gather.2
  81.5 85.9 all-gather.4
  231.8 116.4 reduce-scatter.1

commit v3 on v2

--- a/solution.py
+++ b/solution.py
@@ -140,11 +140,11 @@
     size = proj_ref.shape[0] - HALO
     split_ref[...] = split_by_core(normed_ref[HALO:].astype(F32), slab).astype(BF16)
     rows, columns = triangles(size)
-    rates = proj_ref[HALO:, heads * PROJ :]
+    rates = proj_ref[HALO:, heads * CONV : heads * CONV + LANES]
     scales = scales_ref[...]
     lower, kept = [], []
     for h in range(heads):
-        projected = proj_ref[:, h * PROJ : h * PROJ + CONV]
+        projected = proj_ref[:, h * CONV : (h + 1) * CONV]
         taps = taps_ref[:, h * CONV : (h + 1) * CONV]
         *_, queries, keys, values = mixer_inputs(projected, taps)
         q_ref[h], k_ref[h], v_ref[h] = queries, keys, values
@@ -173,6 +173,11 @@
             sum_ref[HALVES * h + half, :, DK:] = summary[:, (half + 1) * DK : (half + 2) * DK].astype(BF16)
 
 
+def gate_columns(heads, head):
+    at = heads * CONV + LANES + head * DV
+    return pl.ds(at, DV)
+
+
 def whole_state(units_ref, head):
     return jnp.concatenate([units_ref[HALVES * head + half] for half in range(HALVES)], axis=1).astype(F32)
 
@@ -182,7 +187,7 @@
     for h in range(heads):
         mixer_out = out_ref[h] + mm(map_ref[h], whole_state(state_ref, h), FINE)
         mixed_ref[h] = mixer_out
-        gate = proj_ref[HALO:, h * PROJ + CONV : (h + 1) * PROJ]
+        gate = proj_ref[HALO:, gate_columns(heads, h)]
         scale = lax.rsqrt(jnp.mean(mixer_out * mixer_out, axis=-1, keepdims=True) + 1e-05)
         gated = mixer_out * scale * gain * (gate * jax.nn.sigmoid(gate))
         gated_ref[:, h * DV : (h + 1) * DV] = gated.astype(BF16)
@@ -198,7 +203,7 @@
     for h in range(heads):
         grad = grad_ref[:, h * DV : (h + 1) * DV]
         mixer_out = mixed_ref[h]
-        z = proj_ref[HALO:, h * PROJ + CONV : (h + 1) * PROJ]
+        z = proj_ref[HALO:, gate_columns(heads, h)]
         scale = lax.rsqrt(jnp.mean(mixer_out * mixer_out, axis=-1, keepdims=True) + 1e-05)
         normal = mixer_out * scale
         s = jax.nn.sigmoid(z)
@@ -214,25 +219,71 @@
     grad_gain_ref[...] = total
 
 
+def weight_blocks(x, x_sib, y, y_sib, columns, target, slab, z_first):
+    places = target.shape[0]
+    many = places * slab
+    own = lax.axis_index("seq") % 2 * (x.shape[1] // 2)
+
+    @pl.loop(0, places)
+    def _(block):
+        at = pl.ds(pl.multiple_of(own + block * many, many), many)
+        here = pl.ds(pl.multiple_of(block * many, many), many)
+        part = (mtm(x[:, at], y[:, columns]) + mtm(x_sib[:, here], y_sib[:, columns])).astype(BF16)
+        if z_first:
+            rows = pl.ds(pl.multiple_of(block * slab, slab), slab)
+            for place in range(places):
+                target[place, rows] = part[place * slab : (place + 1) * slab]
+        else:
+            target[block] = part
+
+
+def sum_both(first, second, part, middle, result, landing, landing_2, semaphores):
+    places, many, wide = part.shape
+    yield from ring_reduce(first, part, middle, landing, semaphores[0], semaphores[1])
+    blocks = middle.reshape(places, many // places, wide)
+    yield from ring_reduce(second, blocks, result, landing_2, semaphores[2], semaphores[3])
+
+
 def norm_back(grad, values, scale):
     return scale * grad - values * (scale * scale * scale * jnp.sum(values * grad, axis=-1, keepdims=True))
 
 
 def local_backward(
-    heads, proj_ref, taps_ref, scales_ref, q_ref, k_ref, v_ref, inv_ref, grad_ref, state_ref, leaving_ref, gate_ref,
-    out_ref, sibling_ref, taps_out_ref, scales_out_ref, halo_out, halo_in, tails,
+    heads, slab, proj_ref, taps_ref, scales_ref, q_ref, k_ref, v_ref, inv_ref, grad_ref, state_ref, leaving_ref,
+    gate_ref, gate_sib_ref, gated_ref, gated_sib_ref, split_ref, split_sib_ref, branch_ref, branch_sib_ref,
+    ffn_part_ref, middle_ref,
+    out_ref, sibling_ref, taps_out_ref, scales_out_ref, first_out_ref, first_gate_ref, output_ref,
+    halo_out, halo_in, tails, part_o, part_g, land_o, land_g, mid_o, mid_g, land_o2, land_g2, land_f, sum_f,
     halo_s, halo_r, body_s, body_r, tail_s, tail_r, rate_s, rate_r,
+    o1_s, o1_r, g1_s, g1_r, o2_s, o2_r, g2_s, g2_r, rf_s, rf_r, gf_s, gf_r,
 ):
     size = proj_ref.shape[0] - HALO
     seq, head_place = lax.axis_index("seq"), lax.axis_index("head")
     peers = lax.axis_size("seq")
     before, after = (lax.rem(seq + peers - 1, peers), head_place), (lax.rem(seq + 1, peers), head_place)
     sibling = (seq + 1 - 2 * (seq % 2), head_place)
-    start_barrier([before, after, sibling])
+    ring_x, ring_y, ring_z = ring_ids("x"), ring_ids("y"), ring_ids("z")
+    start_barrier([before, after, sibling, *ring_x[4:], *ring_y[4:], *ring_z[4:]])
     copies = []
+
+    def output_sum():
+        yield from ring_reduce(ring_y, ffn_part_ref, sum_f, land_f, rf_s, rf_r)
+        output_ref[ring_y[0]] = (middle_ref[...] + sum_f[...]).astype(BF16)
+        yield from ring_gather(ring_y, output_ref, gf_s, gf_r)
+
+    weight_blocks(branch_ref, branch_sib_ref, gated_ref, gated_sib_ref, pl.ds(0, part_o.shape[2]), part_o, slab, False)
+    beside = [
+        output_sum(),
+        sum_both(ring_x, ring_z, part_o, mid_o, first_out_ref, land_o, land_o2, (o1_s, o1_r, o2_s, o2_r)),
+        sum_both(ring_z, ring_x, part_g, mid_g, first_gate_ref, land_g, land_g2, (g1_s, g1_r, g2_s, g2_r)),
+    ]
+    next(beside[0])
+    next(beside[1])
+    weight_blocks(split_ref, split_sib_ref, gate_ref, gate_sib_ref, pl.ds(0, part_g.shape[2]), part_g, slab, True)
+    next(beside[2])
     body = size - 2 * HALO
     rows, columns = triangles(size)
-    rates = proj_ref[HALO:, heads * PROJ :]
+    rates = proj_ref[HALO:, heads * CONV : heads * CONV + LANES]
     scales = scales_ref[...]
     lanes = iota((size, LANES), 1)
     grad_rates = jnp.zeros((size, LANES), F32)
@@ -288,7 +339,7 @@
         wide = jnp.broadcast_to(grad_gamma, (size, LANES)) - mtm(energy, ones, EXACT)
         grad_decay = mm(above, wide, EXACT)[:, 0:1]
 
-        projected = proj_ref[:, h * PROJ : h * PROJ + CONV]
+        projected = proj_ref[:, h * CONV : (h + 1) * CONV]
         taps = taps_ref[:, h * CONV : (h + 1) * CONV]
         extended, mixed, gate, (q_raw, q_scale), (k_raw, k_scale), *_ = mixer_inputs(projected, taps)
         grad_active = jnp.concatenate(
@@ -314,11 +365,13 @@
             )
         halo_out[h] = total[:HALO]
         tails[h] = total[size - HALO :]
-        out_ref[:, h * PROJ : h * PROJ + CONV] = total[HALO:].astype(BF16)
-        out_ref[:, h * PROJ + CONV : (h + 1) * PROJ] = gate_ref[:, h * DV : (h + 1) * DV]
+        out_ref[:, h * CONV : (h + 1) * CONV] = total[HALO:].astype(BF16)
         copies.append(send(halo_out.at[h], halo_in.at[h], halo_s, halo_r, h, before))
-        upper = (pl.ds(0, body), pl.ds(h * PROJ, PROJ))
+        upper = (pl.ds(0, body), pl.ds(h * CONV, CONV))
         copies.append(send(out_ref.at[upper], sibling_ref.at[upper], body_s, body_r, h, sibling))
+        if h > 0:
+            for stage in beside:
+                next(stage)
 
         grad_pre = -jnp.exp(column(scales[0:1], h)) * jax.nn.sigmoid(pre) * grad_decay
         grad_strength = grad_beta * beta * (1.0 - beta)
@@ -328,27 +381,36 @@
         bias_total = jnp.sum(grad_pre, axis=0, keepdims=True)
         rates_total = rates_total + jnp.where((row8 == 0) & (lane8 == h), log_total, 0.0)
         rates_total = rates_total + jnp.where((row8 == 1) & (lane8 == h), bias_total, 0.0)
-    out_ref[:, heads * PROJ :] = grad_rates.astype(BF16)
+    out_ref[:, heads * CONV :] = grad_rates.astype(BF16)
     scales_out_ref[...] = rates_total
-    side = (pl.ds(0, size), pl.ds(heads * PROJ, LANES))
+    side = (pl.ds(0, size), pl.ds(heads * CONV, LANES))
     last = [send(out_ref.at[side], sibling_ref.at[side], rate_s, rate_r, 0, sibling)]
     for copy in copies:
         copy.wait()
     for h in range(heads):
         arrived = jnp.where(seq < peers - 1, halo_in[h], 0.0)
         fixed = tails[h] + jnp.concatenate([jnp.zeros_like(arrived), arrived], axis=0)
-        out_ref[body:, h * PROJ : h * PROJ + CONV] = fixed.astype(BF16)
-        lower = (pl.ds(body, 2 * HALO), pl.ds(h * PROJ, PROJ))
+        out_ref[body:, h * CONV : (h + 1) * CONV] = fixed.astype(BF16)
+        lower = (pl.ds(body, 2 * HALO), pl.ds(h * CONV, CONV))
         last.append(send(out_ref.at[lower], sibling_ref.at[lower], tail_s, tail_r, h, sibling))
     for copy in last:
         copy.wait()
-
-
-def start_barrier(peers):
+    finish(*beside)
+
+
+def say_here(peers):
     barrier = pltpu.get_barrier_semaphore()
     for peer in peers:
         pl.semaphore_signal(barrier, inc=1, device_id=peer, device_id_type=MESH)
-    pl.semaphore_wait(barrier, len(peers))
+
+    def all_here():
+        pl.semaphore_wait(barrier, len(peers))
+
+    return all_here
+
+
+def start_barrier(peers):
+    say_here(peers)()
 
 
 def send(source, target, sends, receives, slot, peer):
@@ -439,7 +501,8 @@
 
 
 def scan_backward(
-    groups, pack_ref, kept_ref, totals_ref, split_ref, gated_ref, out_ref, sibling_ref, sibling_gated_ref, near_in, turned, before, after, far_out, far_in, back_out, back_in,
+    groups, pack_ref, kept_ref, totals_ref, split_ref, gated_ref, gate_ref,
+    out_ref, sibling_ref, sibling_gated_ref, sibling_gate_ref, near_in, turned, before, after, far_out, far_in, back_out, back_in,
     near_s, near_r, far_s, far_r, back_s, back_r, core_s, core_r,
 ):
     members = pack_ref.shape[0]
@@ -448,7 +511,9 @@
     copies = [
         send(pack_ref.at[near[d]], near_in.at[member], near_s, near_r, d, near_ids[d]) for d in range(1, members)
     ]
-    aside = to_sibling([(other_half(split_ref), sibling_ref), (gated_ref, sibling_gated_ref)], core_s, core_r)
+    aside = to_sibling(
+        [(other_half(split_ref), sibling_ref), (gated_ref, sibling_gated_ref), (gate_ref, sibling_gate_ref)], core_s, core_r
+    )
     near_in[member] = pack_ref[member]
     passed = (iota((DK, DK), 0) == iota((DK, DK), 1)).astype(F32)
     for j in reversed(range(members)):
@@ -590,21 +655,110 @@
     finish(gather)
 
 
-def middle_back_kernel(
-    part_ref, middle_ref, cotangent_ref, gain_ref, branch_ref, grad_ref, grad_gain_ref, landing, red_s, red_r, gat_s, gat_r
+def chunks_of(units):
+    return [(at, min(2 * LANES, units - at)) for at in range(0, units, 2 * LANES)]
+
+
+def ffn_kernel(
+    slab, second_ref, cotangent_ref, middle_ref, gain_ref, weights_ref,
+    branch_ref, grad_ref, grad_gain_ref, ffn_ref, gate_up_ref, down_a_ref, down_b_ref,
+    weights, hidden, grad_hidden, second_split, cotangent_split, second_sib, cotangent_sib, hidden_sib, grad_sib,
+    total, part, landing, gate_up_part, part_a, part_b, land_a, land_b, mid_a, mid_b, land_a2, land_b2,
+    load_s, store_s, half_s, half_r, hid_s, hid_r, gra_s, gra_r, red_s, red_r, gat_s, gat_r,
+    a1_s, a1_r, b1_s, b1_r, a2_s, a2_r, b2_s, b2_r,
 ):
-    ring = ring_ids("y")
-    me = ring[0]
-    start_barrier(ring[4:])
-    finish(ring_reduce(ring, part_ref, grad_ref, landing, red_s, red_r))
+    seq, head = lax.axis_index("seq"), lax.axis_index("head")
+    ring_x, ring_y, ring_z = ring_ids("x"), ring_ids("y"), ring_ids("z")
+    sibling = (seq + 1 - 2 * (seq % 2), head)
+    all_here = say_here(ring_x[4:] + ring_y[4:] + ring_z[4:] + (sibling,))
+    count, width = second_ref.shape
+    chunks = chunks_of(hidden.shape[1])
+    loads = []
+    for i, (at, length) in enumerate(chunks):
+        columns = pl.ds(3 * at, 3 * length)
+        loads.append(pltpu.make_async_copy(weights_ref.at[:, columns], weights.at[:, columns], load_s.at[i]))
+        loads[-1].start()
+    second_split[...] = split_by_core(second_ref[...].astype(F32), slab).astype(BF16)
+    cotangent_split[...] = split_by_core(cotangent_ref[...].astype(F32), slab).astype(BF16)
+    all_here()
+    aside = [
+        send(other_half(second_split), second_sib, half_s, half_r, 0, sibling),
+        send(other_half(cotangent_split), cotangent_sib, half_s, half_r, 1, sibling),
+    ]
+    step = 256
+    for i, (at, length) in enumerate(chunks):
+        loads[i].wait()
+        gate, up, down = (pl.ds(3 * at + k * length, length) for k in range(3))
+        z = mm(second_ref[...], weights[:, gate])
+        u = mm(second_ref[...], weights[:, up])
+        g = mm(cotangent_ref[...], weights[:, down])
+        s = jax.nn.sigmoid(z)
+        silu = z * s
+        here, both = pl.ds(at, length), pl.ds(2 * at, 2 * length)
+        hidden[:, here] = (silu * u).astype(BF16)
+        grad_hidden[:, pl.ds(2 * at, length)] = (g * u * s * (1.0 + z * (1.0 - s))).astype(BF16)
+        grad_hidden[:, pl.ds(2 * at + length, length)] = (g * silu).astype(BF16)
+        aside.append(send(hidden.at[:, here], hidden_sib.at[:, here], hid_s, hid_r, i, sibling))
+        aside.append(send(grad_hidden.at[:, both], grad_sib.at[:, both], gra_s, gra_r, i, sibling))
+
+        @pl.loop(0, width // step)
+        def _(k, at=at, length=length, both=both, i=i):
+            rows = pl.ds(pl.multiple_of(k * step, step), step)
+            product = mmt(grad_hidden[:, both], weights[rows, pl.ds(3 * at, 2 * length)])
+            if i == 0:
+                total[:, rows] = product
+            elif i < len(chunks) - 1:
+                total[:, rows] += product
+            else:
+                full = total[:, rows] + product
+                for p in range(part.shape[0]):
+                    n = part.shape[1]
+                    part[p, :, rows] = full[p * n : (p + 1) * n].astype(BF16)
+
+    reduce = ring_reduce(ring_y, part, grad_ref, landing, red_s, red_r)
+    next(reduce)
+    for copy in aside:
+        copy.wait()
+    wide_a, wide_b = part_a.shape[2], part_b.shape[2]
+    weight_blocks(cotangent_split, cotangent_sib, hidden, hidden_sib, pl.ds(0, wide_a), part_a, slab, False)
+    sum_a = sum_both(ring_x, ring_z, part_a, mid_a, down_a_ref, land_a, land_a2, (a1_s, a1_r, a2_s, a2_r))
+    next(sum_a)
+    weight_blocks(cotangent_split, cotangent_sib, hidden, hidden_sib, pl.ds(wide_a, wide_b), part_b, slab, True)
+    sum_b = sum_both(ring_z, ring_x, part_b, mid_b, down_b_ref, land_b, land_b2, (b1_s, b1_r, b2_s, b2_r))
+    next(sum_b)
+    next(reduce)
+
+    @pl.loop(0, width // step)
+    def _(k):
+        rows = pl.ds(pl.multiple_of(k * step, step), step)
+        product = None
+        for at, length in chunks:
+            term = mmt(hidden[:, pl.ds(at, length)], weights[rows, pl.ds(3 * at + 2 * length, length)])
+            product = term if product is None else product + term
+        for p in range(ffn_ref.shape[0]):
+            n = ffn_ref.shape[1]
+            ffn_ref[p, :, rows] = product[p * n : (p + 1) * n].astype(BF16)
+
+    finish(reduce)
     back, grad_gain = rms_back(grad_ref[...], middle_ref[...], gain_ref[...])
-    grad = cotangent_ref[me].astype(F32) + back
-    branch_ref[me] = grad.astype(BF16)
-    gather = ring_gather(ring, branch_ref, gat_s, gat_r)
+    grad = cotangent_ref[pl.ds(pl.multiple_of(ring_y[0] * slab, slab), slab)].astype(F32) + back
+    branch_ref[ring_y[0]] = grad.astype(BF16)
+    gather = ring_gather(ring_y, branch_ref, gat_s, gat_r)
     next(gather)
     grad_ref[...] = grad
     grad_gain_ref[...] = grad_gain
-    finish(gather)
+    next(sum_a)
+    next(sum_b)
+    weight_blocks(
+        second_split, second_sib, grad_hidden, grad_sib, pl.ds(0, grad_hidden.shape[1]), gate_up_part, slab, False
+    )
+    store = pltpu.make_async_copy(gate_up_part, gate_up_ref, store_s)
+    store.start()
+    next(gather)
+    next(sum_a)
+    next(sum_b)
+    finish(gather, sum_a, sum_b)
+    store.wait()
 
 
 def swap_add(value, partner, outgoing, incoming, sends, receives, slot, mask=None):
@@ -617,62 +771,60 @@
 
 
 def last_kernel(
-    heads, slab, normed_part_ref, ffn_part_ref, tokens_ref, middle_ref, grad_ref, gain_ref, small_ref,
-    split_ref, split_sib_ref, proj_ref, proj_sib_ref, branch_ref, branch_sib_ref, gated_ref, gated_sib_ref,
-    output_ref, low_ref, small_out_ref, first_a_ref, first_b_ref,
-    land_n, land_f, sum_n, sum_f, swap_out, swap_in, part_a, part_b, land_a, land_b, mid_a, mid_b, land_a2, land_b2,
-    rn_s, rn_r, gn_s, gn_r, rf_s, rf_r, gf_s, gf_r, sw_s, sw_r, a1_s, a1_r, b1_s, b1_r, a2_s, a2_r, b2_s, b2_r,
+    slab, gate_ref, tokens_ref, middle_grad_ref, gain_ref, ffn_gain_ref, out_gain_ref, scales_ref, taps_ref,
+    split_ref, split_sib_ref, proj_ref, proj_sib_ref, weights_ref,
+    low_ref, small_out_ref, first_a_ref, first_b_ref,
+    weights, small_ref, part_n, land_n, sum_n, swap_out, swap_in, part_a, part_b, land_a, land_b, mid_a, mid_b, land_a2, land_b2,
+    load_s, rn_s, rn_r, gn_s, gn_r, sw_s, sw_r, a1_s, a1_r, b1_s, b1_r, a2_s, a2_r, b2_s, b2_r,
 ):
     seq, head = lax.axis_index("seq"), lax.axis_index("head")
-    core = seq % 2
     ring_x, ring_y, ring_z = ring_ids("x"), ring_ids("y"), ring_ids("z")
-    sibling = (seq + 1 - 2 * core, head)
-    start_barrier(ring_x[4:] + ring_y[4:] + ring_z[4:] + (sibling,))
+    sibling = (seq + 1 - 2 * (seq % 2), head)
+    all_here = say_here(ring_x[4:] + ring_y[4:] + ring_z[4:] + (sibling,))
+    width, wide = weights.shape
+    step = 256
+
+    def load(k):
+        rows = pl.ds(pl.multiple_of(k * step, step), step)
+        return pltpu.make_async_copy(weights_ref.at[rows, pl.ds(0, wide)], weights.at[rows], load_s.at[k])
+
+    for k in range(width // step):
+        load(k).start()
+    small_ref[...] = jnp.zeros_like(small_ref)
+    small_ref[1:2] = ffn_gain_ref[...]
+    small_ref[2:3, :DV] = out_gain_ref[...]
+    small_ref[2:3, DV : DV + LANES] = scales_ref[0:1]
+    small_ref[2:3, DV + LANES : DV + 2 * LANES] = scales_ref[1:2]
+    small_ref[3 : 3 + KW] = taps_ref[...]
     me = ring_y[0]
-    reduce_n = ring_reduce(ring_y, normed_part_ref, sum_n, land_n, rn_s, rn_r)
+    wide_a, wide_b = part_a.shape[2], part_b.shape[2]
+    weight_blocks(split_ref, split_sib_ref, proj_ref, proj_sib_ref, pl.ds(0, wide_a), part_a, slab, False)
+    all_here()
+    sum_a = sum_both(ring_x, ring_z, part_a, mid_a, first_a_ref, land_a, land_a2, (a1_s, a1_r, a2_s, a2_r))
+    next(sum_a)
+    weight_blocks(split_ref, split_sib_ref, proj_ref, proj_sib_ref, pl.ds(wide_a, wide_b), part_b, slab, True)
+    sum_b = sum_both(ring_z, ring_x, part_b, mid_b, first_b_ref, land_b, land_b2, (b1_s, b1_r, b2_s, b2_r))
+    next(sum_b)
+    narrow = proj_ref.shape[1]
+
+    @pl.loop(0, width // step)
+    def _(k):
+        load(k).wait()
+        rows = pl.ds(pl.multiple_of(k * step, step), step)
+        product = mmt(proj_ref[...], weights[rows, :narrow]) + mmt(gate_ref[...], weights[rows, narrow:])
+        for p in range(part_n.shape[0]):
+            n = part_n.shape[1]
+            part_n[p, :, rows] = product[p * n : (p + 1) * n].astype(BF16)
+
+    reduce_n = ring_reduce(ring_y, part_n, sum_n, land_n, rn_s, rn_r)
     next(reduce_n)
-
-    half = split_ref.shape[1] // 2
-    own = core * half
-    wide_a, wide_b = part_a.shape[2], part_b.shape[2]
-    rest = proj_ref.shape[1] - wide_a
-    places = 4
-    many = places * slab
-
-    def product(x, x_sib, y, y_sib, block, columns):
-        at = pl.ds(pl.multiple_of(own + block * many, many), many)
-        here = pl.ds(pl.multiple_of(block * many, many), many)
-        return mtm(x[:, at], y[:, columns]) + mtm(x_sib[:, here], y_sib[:, columns])
-
-    @pl.loop(0, places)
-    def _(block):
-        rows = pl.ds(pl.multiple_of(block * slab, slab), slab)
-        in_part = product(split_ref, split_sib_ref, proj_ref, proj_sib_ref, block, pl.ds(wide_a, rest)).astype(BF16)
-        out_part = product(branch_ref, branch_sib_ref, gated_ref, gated_sib_ref, block, pl.ds(0, wide_b - rest)).astype(BF16)
-        for place in range(places):
-            part_b[place, rows, :rest] = in_part[place * slab : (place + 1) * slab]
-            part_b[place, rows, rest:] = out_part[place * slab : (place + 1) * slab]
-
-    reduce_b = ring_reduce(ring_z, part_b, mid_b, land_b, b1_s, b1_r)
-    next(reduce_b)
-
-    @pl.loop(0, places)
-    def _(block):
-        part_a[block] = product(split_ref, split_sib_ref, proj_ref, proj_sib_ref, block, pl.ds(0, wide_a)).astype(BF16)
-
-    reduce_a = ring_reduce(ring_x, part_a, mid_a, land_a, a1_s, a1_r)
-    next(reduce_a)
-
+    next(sum_a)
+    next(sum_b)
     next(reduce_n)
     finish(reduce_n)
     back, grad_gain = rms_back(sum_n[...], tokens_ref[me].astype(F32), gain_ref[...])
-    low_ref[me] = (grad_ref[...] + back).astype(BF16)
+    low_ref[me] = (middle_grad_ref[...] + back).astype(BF16)
     gather_n = ring_gather(ring_y, low_ref, gn_s, gn_r)
-    next(gather_n)
-    reduce_f = ring_reduce(ring_y, ffn_part_ref, sum_f, land_f, rf_s, rf_r)
-    next(reduce_f)
-    next(reduce_b)
-    next(reduce_a)
     next(gather_n)
 
     def all_small():
@@ -684,9 +836,7 @@
             place, right_id, left_id = ring[0], ring[4], ring[5]
             even = lax.rem(place, 2) == 0
             for flip in (False, True):
-                ids = tuple(
-                    jnp.where(jnp.logical_xor(even, flip), r, l) for r, l in zip(right_id, left_id)
-                )
+                ids = tuple(jnp.where(jnp.logical_xor(even, flip), r, l) for r, l in zip(right_id, left_id))
                 value = yield from swap_add(value, ids, swap_out, swap_in, sw_s, sw_r, slot, mask)
                 slot += 1
         value = yield from swap_add(value, sibling, swap_out, swap_in, sw_s, sw_r, slot)
@@ -694,44 +844,132 @@
 
     small = all_small()
     next(small)
-    next(reduce_f)
+    next(sum_a)
+    next(sum_b)
     next(small)
+    next(gather_n)
     next(small)
-    finish(reduce_b)
-    reduce_b2 = ring_reduce(ring_x, mid_b.reshape(places, slab, wide_b), first_b_ref, land_b2, b2_s, b2_r)
-    next(reduce_b2)
-    finish(reduce_a)
-    reduce_a2 = ring_reduce(ring_z, mid_a.reshape(places, slab, wide_a), first_a_ref, land_a2, a2_s, a2_r)
-    next(reduce_a2)
-    finish(reduce_f)
-    output_ref[me] = (middle_ref[...] + sum_f[...]).astype(BF16)
-    gather_f = ring_gather(ring_y, output_ref, gf_s, gf_r)
-    next(gather_f)
-    next(reduce_b2)
-    next(reduce_a2)
-    finish(small, gather_n, gather_f, reduce_b2, reduce_a2)
-
-
-def mlp_grads(second_ref, cotangent_ref, gate_up_ref, hidden_ref, out_ref):
-    wide = gate_up_ref.shape[1]
-    out_ref[:, :wide] = mtm(second_ref[...], gate_up_ref[...]).astype(BF16)
-    out_ref[:, wide:] = mtm(cotangent_ref[...], hidden_ref[...]).astype(BF16)
-
-
-def finish_kernel(heads, first_a_ref, first_b_ref, mlp_ref, low_ref, in_ref, rate_ref, out_ref, gate_up_ref, down_ref, tokens_ref):
-    wide = first_a_ref.shape[1]
-    rates = heads * PROJ
+    next(sum_a)
+    next(sum_b)
+    finish(small, gather_n, sum_a, sum_b)
+
+
+def finish_kernel(
+    heads, first_a_ref, first_b_ref, first_out_ref, first_gate_ref, gate_up_in_ref, down_a_ref, down_b_ref, low_ref, small_ref,
+    in_ref, rate_ref, out_ref, gate_up_ref, down_ref, tokens_ref, taps_ref, mixer_gain_ref, ffn_gain_ref, out_gain_ref,
+):
     both = jnp.concatenate([first_a_ref[...], first_b_ref[...]], axis=1)
     for h in range(heads):
-        in_ref[:, h] = both[:, h * PROJ : (h + 1) * PROJ]
-        out_ref[:, h] = both[:, rates + LANES + h * DV : rates + LANES + (h + 1) * DV]
+        in_ref[:, h, :CONV] = both[:, h * CONV : (h + 1) * CONV]
+        in_ref[:, h, CONV:] = first_gate_ref[:, h * DV : (h + 1) * DV]
+        out_ref[:, h] = first_out_ref[:, h * DV : (h + 1) * DV]
+        taps_ref[:, h] = small_ref[3 : 3 + KW, h * CONV : (h + 1) * CONV]
+    rates = heads * CONV
     for g in range(2):
         rate_ref[:, g] = both[:, rates + g * heads : rates + (g + 1) * heads]
-    units = down_ref.shape[1]
-    for g in range(2):
-        gate_up_ref[:, g] = mlp_ref[:, g * units : (g + 1) * units].astype(F32)
-    down_ref[...] = mlp_ref[:, 2 * units :].astype(F32)
+    for at, length in chunks_of(down_ref.shape[1]):
+        for g in range(2):
+            gate_up_ref[:, g, at : at + length] = gate_up_in_ref[:, pl.ds(2 * at + g * length, length)].astype(F32)
+    down_ref[:, : down_a_ref.shape[1]] = down_a_ref[...]
+    down_ref[:, down_a_ref.shape[1] :] = down_b_ref[...]
     tokens_ref[...] = low_ref[...].astype(F32)
+    mixer_gain_ref[...] = small_ref[0]
+    ffn_gain_ref[...] = small_ref[1]
+    out_gain_ref[...] = small_ref[2, :DV]
+
+
+def gather_weights(slab_ref, full_ref, own_s, core_s, core_r, ring_s, ring_r):
+    seq, head = lax.axis_index("seq"), lax.axis_index("head")
+    core = seq % 2
+    sibling = (seq + 1 - 2 * core, head)
+    ring_x, ring_z = ring_ids("x"), ring_ids("z")
+    x, z = ring_x[0], ring_z[0]
+    rows, wide = slab_ref.shape
+    cut = -(-wide // (2 * LANES)) * LANES
+    start_barrier(ring_x[4:] + ring_z[4:] + (sibling,))
+    own = pltpu.make_async_copy(slab_ref, full_ref.at[x, z, core], own_s)
+    own.start()
+    counts = {"core": 0, "ring": 0}
+    waiting = []
+
+    def slot(kind):
+        counts[kind] += 1
+        return counts[kind] - 1
+
+    def across(source, target):
+        waiting.append(send(source, target, core_s, core_r, slot("core"), sibling))
+
+    across(slab_ref, full_ref.at[x, z, core])
+    half = rows // 2
+    upper, lower = pl.ds(0, half), pl.ds(half, half)
+
+    def round_ring(ring, at, source, arrived):
+        me, right, left, opposite, right_id, left_id = ring
+
+        def go(place, part, peer):
+            index = slot("ring")
+            origin = source(part) if place is me else at(place, part)
+            return send(origin, at(place, part), ring_s, ring_r, index, peer)
+
+        upper_right = go(me, upper, right_id)
+        lower_left = go(me, lower, left_id)
+        lower_right = go(me, lower, right_id)
+        upper_left = go(me, upper, left_id)
+        yield
+        upper_right.wait()
+        far_right = go(left, upper, right_id)
+        lower_left.wait()
+        far_left = go(right, lower, left_id)
+        lower_right.wait()
+        arrived(left)
+        upper_left.wait()
+        arrived(right)
+        yield
+        far_right.wait()
+        far_left.wait()
+        arrived(opposite)
+
+    active = []
+    for ring_1, ring_2, columns, x_first in (
+        (ring_x, ring_z, pl.ds(0, cut), True),
+        (ring_z, ring_x, pl.ds(cut, wide - cut), False),
+    ):
+        def place_of(first, second, part, columns=columns, x_first=x_first):
+            where = (first, second) if x_first else (second, first)
+            return full_ref.at[where[0], where[1], core, part, columns]
+
+        everything = pl.ds(0, rows)
+
+        def start_second(first, source=None, ring_1=ring_1, ring_2=ring_2, place_of=place_of):
+            def at(place, part):
+                return place_of(first, place, part)
+
+            def arrived(place):
+                across(place_of(first, place, everything), place_of(first, place, everything))
+
+            active.append(round_ring(ring_2, at, source or (lambda part: at(ring_2[0], part)), arrived))
+
+        def at_first(place, part, ring_2=ring_2, place_of=place_of):
+            return place_of(place, ring_2[0], part)
+
+        def arrived_first(place, at_first=at_first, start_second=start_second):
+            across(at_first(place, everything), at_first(place, everything))
+            start_second(place)
+
+        def mine(part, columns=columns):
+            return slab_ref.at[part, columns]
+
+        active.append(round_ring(ring_1, at_first, mine, arrived_first))
+        start_second(ring_1[0], mine)
+    while active:
+        ended = []
+        for stage in list(active):
+            if next(stage, active) is active:
+                ended.append(stage)
+        active[:] = [stage for stage in active if stage not in ended]
+    own.wait()
+    for copy in waiting:
+        copy.wait()
 
 
 def call(kernel, outs, *args, name):
@@ -794,27 +1032,39 @@
     groups = peers // units
     rows = count // sharers
 
+    convolved_wide = heads * CONV + LANES
     first = jnp.concatenate(
         [
-            in_weight.reshape(slab, heads * PROJ),
+            in_weight[:, :, :CONV].reshape(slab, heads * CONV),
             rate_weight.reshape(slab, 2 * heads),
             jnp.zeros((slab, LANES - 2 * heads), BF16),
+            in_weight[:, :, CONV:].reshape(slab, heads * DV),
+            out_weight.reshape(slab, heads * DV),
         ],
         axis=1,
     )
-    rest = jnp.concatenate(
-        [out_weight.reshape(slab, heads * DV), gate_up_weight.reshape(slab, 2 * hidden_units), down_weight], axis=1
-    )
-    first_full = lax.all_gather(first, "seq", axis=0, tiled=True)
+    anywhere = pl.BlockSpec(memory_space=pl.ANY)
+    first_full = pl.pallas_call(
+        gather_weights,
+        in_specs=[anywhere],
+        out_specs=anywhere,
+        out_shape=jax.ShapeDtypeStruct((4, 4, 2, slab, projections + heads * DV), BF16),
+        scratch_shapes=[pltpu.SemaphoreType.DMA, *pairs(31, 60)],
+        compiler_params=pltpu.CompilerParams(vmem_limit_bytes=VMEM_LIMIT, collective_id=7, has_side_effects=True),
+        name="gather_weights",
+    )(first)
+    pieces = []
+    for at, length in chunks_of(hidden_units):
+        part = slice(at, at + length)
+        pieces += [gate_up_weight[:, 0, part], gate_up_weight[:, 1, part], down_weight[:, part]]
+    first_full, rest = lax.optimization_barrier((first_full, jnp.concatenate(pieces, axis=1)))
+    first_full = first_full.reshape(width, projections + heads * DV)
     rest_full = lax.all_gather(rest, "seq", axis=0, tiled=True)
-    out_full = rest_full[:, : heads * DV]
-    gate_up_full = rest_full[:, heads * DV : heads * DV + 2 * hidden_units]
-    down_full = rest_full[:, heads * DV + 2 * hidden_units :]
-
+    out_full = first_full[:, projections:]
     behind = shifted(tokens[count - HALO :], "seq", 1)
     source = jnp.concatenate([behind, tokens], axis=0).astype(F32)
     normed_long = (source * rms_scale(source) * mixer_gain).astype(BF16)
-    projected = mm(normed_long, first_full)
+    projected = mm(normed_long, first_full[:, :projections])
 
     taps = conv_weight.reshape(KW, heads * CONV)
     scales = jnp.pad(jnp.stack([decay_log, decay_bias]), ((0, 6), (0, LANES - heads)))
@@ -883,42 +1133,63 @@
         name="middle",
     )
     second = second.reshape(count, width)
-    gate_up = mm(second, gate_up_full)
-    z, up = gate_up[:, :hidden_units], gate_up[:, hidden_units:]
-    s = jax.nn.sigmoid(z)
-    hidden = (z * s * up).astype(BF16)
-    ffn_part = mmt(hidden, down_full)
-    grad_hidden = mm(cotangent, down_full)
-    grad_gate_up = jnp.concatenate([grad_hidden * up * s * (1.0 + z * (1.0 - s)), grad_hidden * z * s], axis=1).astype(
-        BF16
-    )
-    second_part = mmt(grad_gate_up, gate_up_full)
-    grad_mlp = pl.pallas_call(
-        mlp_grads,
-        grid=(width // 256,),
-        in_specs=[
-            pl.BlockSpec((count, 256), lambda i: (0, i)),
-            pl.BlockSpec((count, 256), lambda i: (0, i)),
-            pl.BlockSpec((count, 2 * hidden_units), lambda i: (0, 0)),
-            pl.BlockSpec((count, hidden_units), lambda i: (0, 0)),
+    gate_wide = heads * DV
+    many = 4 * slab
+
+    def sums_scratch(wide_1, wide_2):
+        return [
+            pltpu.VMEM((4, many, wide_1), BF16),
+            pltpu.VMEM((4, many, wide_2), BF16),
+            landing(many // 2, wide_1),
+            landing(many // 2, wide_2),
+            pltpu.VMEM((many, wide_1), BF16),
+            pltpu.VMEM((many, wide_2), BF16),
+            landing(slab // 2, wide_1),
+            landing(slab // 2, wide_2),
+        ]
+
+    down_a = -(-hidden_units // (2 * LANES)) * LANES
+    down_b = hidden_units - down_a
+    chunk_count = len(chunks_of(hidden_units))
+    in_vmem = pl.BlockSpec(memory_space=pltpu.VMEM)
+    grad_branch, grad_middle, grad_ffn_gain, ffn_part, gate_up_part, grad_down_a, grad_down_b = pl.pallas_call(
+        functools.partial(ffn_kernel, slab),
+        in_specs=[in_vmem] * 4 + [anywhere],
+        out_specs=[in_vmem] * 4 + [anywhere] + [in_vmem] * 2,
+        out_shape=[
+            jax.ShapeDtypeStruct(blocked, BF16),
+            jax.ShapeDtypeStruct((rows, width), F32),
+            jax.ShapeDtypeStruct((1, width), F32),
+            jax.ShapeDtypeStruct(blocked, BF16),
+            jax.ShapeDtypeStruct((4, many, 2 * hidden_units), BF16),
+            jax.ShapeDtypeStruct((slab, down_a), F32),
+            jax.ShapeDtypeStruct((slab, down_b), F32),
         ],
-        out_specs=pl.BlockSpec((256, 3 * hidden_units), lambda i: (i, 0)),
-        out_shape=jax.ShapeDtypeStruct((width, 3 * hidden_units), BF16),
-        compiler_params=pltpu.CompilerParams(vmem_limit_bytes=VMEM_LIMIT),
-        name="mlp_grads",
-    )(second, cotangent, grad_gate_up, hidden)
-    second_part, grad_mlp = lax.optimization_barrier((second_part.astype(BF16), grad_mlp))
-    grad_mlp = lax.psum_scatter(grad_mlp, "seq", scatter_dimension=0, tiled=True)
-    grad_branch, grad_middle, grad_ffn_gain = remote_call(
-        middle_back_kernel,
-        [(blocked, BF16), ((rows, width), F32), ((1, width), F32)],
-        ring + pairs(6, 6),
-        3,
-        second_part.reshape(blocked),
-        middle,
-        cotangent.reshape(blocked),
-        ffn_gain.reshape(1, width),
-        name="middle_back",
+        scratch_shapes=[
+            pltpu.VMEM((width, 3 * hidden_units), BF16),
+            pltpu.VMEM((count, hidden_units), BF16),
+            pltpu.VMEM((count, 2 * hidden_units), BF16),
+            pltpu.VMEM((count, width), BF16),
+            pltpu.VMEM((count, width), BF16),
+            pltpu.VMEM((count, width // 2), BF16),
+            pltpu.VMEM((count, width // 2), BF16),
+            pltpu.VMEM((count, hidden_units), BF16),
+            pltpu.VMEM((count, 2 * hidden_units), BF16),
+            pltpu.VMEM((count, width), F32),
+            pltpu.VMEM(blocked, BF16),
+            *ring,
+            pltpu.VMEM((4, many, 2 * hidden_units), BF16),
+            *sums_scratch(down_a, down_b),
+            pltpu.SemaphoreType.DMA((chunk_count,)),
+            pltpu.SemaphoreType.DMA,
+            *pairs(2, chunk_count, chunk_count, 6, 6, 6, 6, 6, 6),
+        ],
+        compiler_params=pltpu.CompilerParams(vmem_limit_bytes=VMEM_LIMIT, collective_id=3, has_side_effects=True),
+        name="ffn",
+    )(second, cotangent, middle, ffn_gain.reshape(1, width), rest_full)
+    same_core = [[device for device in range(peers) if device % 2 == core] for core in range(2)]
+    grad_gate_up_part = lax.psum_scatter(
+        gate_up_part.reshape(width // 2, 2 * hidden_units), "seq", scatter_dimension=0, axis_index_groups=same_core, tiled=True
     )
     grad_branch = grad_branch.reshape(count, width)
     grad_gated = mm(grad_branch, out_full)
@@ -939,9 +1210,14 @@
         grad_branch,
         name="mix_outputs_back",
     )
-    leaving, branch_sibling, gated_sibling = remote_call(
+    leaving, branch_sibling, gated_sibling, gate_sibling = remote_call(
         functools.partial(scan_backward, groups),
-        [((units, *block), BF16), ((count, width // 2), BF16), ((count, heads * DV), BF16)],
+        [
+            ((units, *block), BF16),
+            ((count, width // 2), BF16),
+            ((count, heads * DV), BF16),
+            ((count, heads * DV), BF16),
+        ],
         [
             pltpu.VMEM((units, *block), BF16),
             pltpu.VMEM((units, *block), BF16),
@@ -951,7 +1227,7 @@
             pltpu.VMEM((groups, *block), BF16),
             pltpu.VMEM((units, *block), BF16),
             pltpu.VMEM((units, *block), BF16),
-            *pairs(units, groups, units, 2),
+            *pairs(units, groups, units, 3),
         ],
         4,
         carried,
@@ -959,21 +1235,28 @@
         totals,
         branch_split,
         gated,
+        grad_gate,
         name="scan_backward",
     )
-    grad_projected, grad_sibling, grad_taps, grad_scales = remote_call(
-        functools.partial(local_backward, heads),
+    grad_projected, grad_sibling, grad_taps, grad_scales, first_out, first_gate, output = remote_call(
+        functools.partial(local_backward, heads, slab),
         [
-            ((count, projections), BF16),
-            ((count, projections), BF16),
+            ((count, convolved_wide), BF16),
+            ((count, convolved_wide), BF16),
             ((KW, heads * CONV), F32),
             ((8, LANES), F32),
+            ((slab, gate_wide), F32),
+            ((slab, gate_wide), F32),
+            (blocked, BF16),
         ],
         [
             pltpu.VMEM((heads, HALO, CONV), F32),
             pltpu.VMEM((heads, HALO, CONV), F32),
             pltpu.VMEM((heads, 2 * HALO, CONV), F32),
-            *pairs(heads, heads, heads, 1),
+            *sums_scratch(gate_wide, gate_wide),
+            landing(rows // 2, width),
+            pltpu.VMEM((rows, width), F32),
+            *pairs(heads, heads, heads, 1, 6, 6, 6, 6, 6, 6),
         ],
         6,
         projected,
@@ -987,75 +1270,59 @@
         entering,
         leaving,
         grad_gate,
+        gate_sibling,
+        gated,
+        gated_sibling,
+        normed_split,
+        normed_sibling,
+        branch_split,
+        branch_sibling,
+        ffn_part,
+        middle,
         name="local_backward",
     )
-    normed_part = mmt(grad_projected, first_full)
-    small = jnp.concatenate(
-        [
-            jnp.zeros((1, width), F32),
-            grad_ffn_gain,
-            jnp.concatenate(
-                [
-                    grad_out_gain,
-                    grad_scales[0:1],
-                    grad_scales[1:2],
-                    jnp.zeros((1, width - DV - 2 * LANES), F32),
-                ],
-                axis=1,
-            ),
-            grad_taps,
-            jnp.zeros((1, width), F32),
+    wide_a = -(-convolved_wide // (2 * LANES)) * LANES
+    wide_b = convolved_wide - wide_a
+    low, small, first_a, first_b = pl.pallas_call(
+        functools.partial(last_kernel, slab),
+        in_specs=[in_vmem] * 12 + [anywhere],
+        out_specs=[in_vmem] * 4,
+        out_shape=[
+            jax.ShapeDtypeStruct(blocked, BF16),
+            jax.ShapeDtypeStruct((8, width), F32),
+            jax.ShapeDtypeStruct((slab, wide_a), F32),
+            jax.ShapeDtypeStruct((slab, wide_b), F32),
         ],
-        axis=0,
-    )
-    wide_a = -(-(projections + heads * DV) // (2 * LANES)) * LANES
-    wide_b = projections + heads * DV - wide_a
-    many = 4 * slab
-    output, low, small, first_a, first_b = remote_call(
-        functools.partial(last_kernel, heads, slab),
-        [
-            (blocked, BF16),
-            (blocked, BF16),
-            ((8, width), F32),
-            ((slab, wide_a), F32),
-            ((slab, wide_b), F32),
-        ],
-        [
+        scratch_shapes=[
+            pltpu.VMEM((width, projections), BF16),
+            pltpu.VMEM((8, width), F32),
+            pltpu.VMEM(blocked, BF16),
             landing(rows // 2, width),
-            landing(rows // 2, width),
-            pltpu.VMEM((rows, width), F32),
             pltpu.VMEM((rows, width), F32),
             pltpu.VMEM((7, 8, width), F32),
             pltpu.VMEM((7, 8, width), F32),
-            pltpu.VMEM((4, many, wide_a), BF16),
-            pltpu.VMEM((4, many, wide_b), BF16),
-            landing(many // 2, wide_a),
-            landing(many // 2, wide_b),
-            pltpu.VMEM((many, wide_a), BF16),
-            pltpu.VMEM((many, wide_b), BF16),
-            landing(slab // 2, wide_a),
-            landing(slab // 2, wide_b),
-            *pairs(6, 6, 6, 6, 7, 6, 6, 6, 6),
+            *sums_scratch(wide_a, wide_b),
+            pltpu.SemaphoreType.DMA((width // 256,)),
+            *pairs(6, 6, 7, 6, 6, 6, 6),
         ],
-        5,
-        normed_part.astype(BF16).reshape(blocked),
-        ffn_part.astype(BF16).reshape(blocked),
+        compiler_params=pltpu.CompilerParams(vmem_limit_bytes=VMEM_LIMIT, collective_id=5, has_side_effects=True),
+        name="last",
+    )(
+        grad_gate,
         tokens.reshape(blocked),
-        middle,
         grad_middle,
         mixer_gain.reshape(1, width),
-        small,
+        grad_ffn_gain,
+        grad_out_gain,
+        grad_scales,
+        grad_taps,
         normed_split,
         normed_sibling,
         grad_projected,
         grad_sibling,
-        branch_split,
-        branch_sibling,
-        gated,
-        gated_sibling,
-        name="last",
-    )
-    grad_in, grad_rate, grad_out, grad_gate_up_weight, grad_down, grad_tokens = call(
+        first_full,
+    )
+    grad_in, grad_rate, grad_out, grad_gate_up_weight, grad_down, grad_tokens, grad_conv, *gains = call(
         functools.partial(finish_kernel, heads),
         [
             ((slab, heads, PROJ), F32),
@@ -1064,25 +1331,34 @@
             ((slab, 2, hidden_units), F32),
             ((slab, hidden_units), F32),
             ((count, width), F32),
+            ((KW, heads, CONV), F32),
+            ((width,), F32),
+            ((width,), F32),
+            ((DV,), F32),
         ],
         first_a,
         first_b,
-        grad_mlp,
+        first_out,
+        first_gate,
+        grad_gate_up_part,
+        grad_down_a,
+        grad_down_b,
         low.reshape(count, width),
+        small,
         name="finish",
     )
     return (
         output.reshape(count, width),
         grad_tokens,
-        small[0],
+        gains[0],
         grad_in,
         grad_rate,
-        small[3 : 3 + KW].reshape(KW, heads, CONV),
+        grad_conv,
         small[2, DV : DV + heads],
         small[2, DV + LANES : DV + LANES + heads],
-        small[2, :DV],
+        gains[2],
         grad_out,
-        small[1],
+        gains[1],
         grad_gate_up_weight,
         grad_down,
     )

time: 434 us -> 385 us (0.89)
  waiting for transfers between devices: 87.7 us -> 0.06 us
  Pallas kernels: 251 us -> 333 us
  matrix products: 54.9 us -> 20.1 us
    pallas_call x1 -> x3, Pallas kernels: 11.8 us -> 161 us  [the longest x1 61.6 us: per_device(): pl.pallas_call(gather_weights, in_specs=[anywhere], out_specs=anywhere, o...]
    pallas_call x6 -> x4, Pallas kernels: 208 us -> 142 us  [remote_call(): pl.pallas_call(kernel, in_specs=[pl.BlockSpec(memory_space=pltpu.VMEM)] *...]
    all_gather x1 -> x0, waiting for transfers between devices: 60.6 us -> none  [per_device(): first_full = lax.all_gather(first, 'seq', axis=0, tiled=True)]
    dot_general x8 -> x3, matrix products: 54.9 us -> 20.1 us  [dot(): lax.dot_general(a, b, (dims, ((), ())), precision=precision, preferred_el...]
    all_gather x1, waiting for transfers between devices: 27.1 us -> 0.02 us  [per_device(): rest_full = lax.all_gather(rest, 'seq', axis=0, tiled=True)]
  transfers between devices with their start and end apart: 4 -> 3, of which waited for: 2 -> 0; matrix products, arithmetic and copies ran while one was open for 9% -> 6% of each run, Pallas kernels for 49% -> 58%
where the time goes in v3:
time: 385 us; the launch traced here: 382 us
  Pallas kernels  333 us (86%)
  matrix products  20.1 us (5%)
  between operations  14.7 us (4%)
  local copies, waits for them, and re-layouts  9.7 us (3%)
    pallas_call x4, Pallas kernels, remote_call(): pl.pallas_call(kernel, in_specs=[pl.BlockSpec(memory_space=pltpu.VMEM)] *...  142 us
    pallas_call x1, Pallas kernels, per_device(): pl.pallas_call(gather_weights, in_specs=[anywhere], out_specs=anywhere, o...  61.6 us
    pallas_call x1, Pallas kernels, per_device(): pl.pallas_call(functools.partial(last_kernel, slab), in_specs=[in_vmem] *...  52.2 us
    pallas_call x1, Pallas kernels, per_device(): pl.pallas_call(functools.partial(ffn_kernel, slab), in_specs=[in_vmem] *...  47 us
    pallas_call x4, Pallas kernels, call(): pl.pallas_call(kernel, in_specs=[pl.BlockSpec(memory_space=pltpu.VMEM)] *...  30.4 us
    dot_general x3, matrix products, dot(): lax.dot_general(a, b, (dims, ((), ())), precision=precision, preferred_el...  20.1 us
  transfers between devices with their start and end apart: 3, of which 0 were waited for; matrix products, arithmetic and copies ran while one was open for 6% of the time, Pallas kernels for 58%

profile of v3, /device:TPU:1, one launch (start us, length us, event | category | flops | bytes accessed | tf_op | source)
XLA Modules:
  0.0 381.7 jit_solution(14420463629850120355)
XLA Ops:
  7.2 0.0 all-gather.2.cloned.1.call-start
  7.3 0.9 fusion.12
  8.2 1.8 fusion.13
  10.0 0.1 copy.40
  10.6 1.0 concatenate.10.slab_ref
  11.6 61.6 %gather_weights.1 = bf16[4,4,2,64,4224]{4,3,2,1,0:T(8,128)(2,1)} custom-call(bf16[64,4224]{1,0:T(8,128)(2,1)} %concatenate.10.slab_ref), custom_call_target="tpu_custom_call" | custom-call | tf_op jit(solution)/shard_map/gather_weights/pallas_call | solution.py:1047
  73.2 0.0 all-gather.2.cloned.1.call-update
  73.2 0.0 reduce-scatter.2.cloned.1.call-start
  73.3 2.4 collective-permute-start
  75.8 0.6 select_maximum_fusion.scales_ref
  76.4 0.6 copy.69
  77.0 0.3 fusion.9
  77.3 0.3 fusion.11.normed_ref
  77.6 11.1 %fusion.proj_ref = f32[264,3200]{1,0:T(8,128)} fusion(bf16[264,2048]{1,0:T(8,128)(2,1)S(1)} %fusion.11.normed_ref, bf16[2048,4224]{1,0:T(8,128)(2,1)} %bitcast.77), kind=kOutput, calls=%fused_computation | convolution fusion | flops 3460300800 | bytes 17567744 | tf_op jit(solution)/shard_map/dot_general | solution.py:28
  88.7 15.9 %local_forward.1 = (bf16[4,256,128]{2,1,0:T(8,128)(2,1)}, bf16[4,256,128]{2,1,0:T(8,128)(2,1)}, bf16[4,256,256]{2,1,0:T(8,128)(2,1)}, f32[4,256,256]{2,1,0:T(8,1...) custom-call(f32[264,3200]{1,0:T(8,128)} %fusion.proj_ref, ...), custom_call_target="tpu_custom_call" | custom-call | tf_op jit(solution)/shard_map/local_forward/pallas_call | solution.py:976
  104.6 40.3 %scan_forward.1 = (bf16[8,128,128]{2,1,0:T(8,128)(2,1)}, bf16[256,1024]{1,0:T(8,128)(2,1)}, bf16[8,128,128]{2,1,0:T(8,128)(2,1)}, bf16[4,128,128]{2,1,0:T(8,128)(2,1)}) custom-call(bf16[8,128,256]{2,1,0:T(8,128)(2,1)} %get-tuple-element.75.pack_ref, bf16[256,2048]{1,0:T(8,128)(2,1)} %get-tuple-element.76.split_ref), custom_call_target="tpu_custom_call" | custom-call | tf_op jit(solution)/shard_map/scan_forward/pallas_call | solution.py:987
  144.9 4.4 %mix_outputs.1 = (f32[4,256,256]{2,1,0:T(8,128)}, bf16[256,1024]{1,0:T(8,128)(2,1)}) custom-call(f32[4,256,256]{2,1,0:T(8,128)} %get-tuple-element.73.out_ref, f32[4,256,128]{2,1,0:T(8,128)} %get-tuple-element.74.map_ref, bf16[8,128,128]{2,1,0:T(8,128)(2,1)} %get-tuple-element.77.state_ref, f32[264,3200]{1,0:T(8,128)} %fusion.proj_ref, f32[1,256]{1,0:T(1,128)} %bitcast.102), custom_call_target="tpu_custom_call" | custom-call | tf_op jit(solution)/shard_map/mix_outputs/pallas_call | solution.py:976
  149.3 4.6 %fusion.6 = bf16[256,2048]{1,0:T(8,128)(2,1)} fusion(bf16[256,1024]{1,0:T(8,128)(2,1)} %get-tuple-element.78.gated_ref, bf16[2048,4224]{1,0:T(8,128)(2,1)} %bitcast.78), kind=kOutput, calls=%fused_computation.8 | convolution fusion | flops 1074266112 | bytes 5767168 | tf_op jit(solution)/shard_map/dot_general | solution.py:28
  153.9 27.0 %middle.1 = (bf16[4,64,2048]{2,1,0:T(8,128)(2,1)}, f32[64,2048]{1,0:T(8,128)}) custom-call(bf16[4,64,2048]{2,1,0:T(8,128)(2,1)} %bitcast.88, bf16[4,64,2048]{2,1,0:T(8,128)(2,1)} %bitcast.81, f32[1,2048]{1,0:T(1,128)} %bitcast.98), custom_call_target="tpu_custom_call" | custom-call | tf_op jit(solution)/shard_map/middle/pallas_call | solution.py:987
  180.9 0.0 all-gather.2.cloned.1.call-done.weights_ref
  180.9 47.0 %ffn.1 = (bf16[4,64,2048]{2,1,0:T(8,128)(2,1)}, f32[64,2048]{1,0:T(8,128)}, f32[1,2048]{1,0:T(1,128)}, bf16[4,64,2048]{2,1,0:T(8,128)(2,1)}, bf16[4,256,2816]{2,...) custom-call(bf16[256,2048]{1,0:T(8,128)(2,1)} %bitcast.86, bf16[256,2048]{1,0:T(8,128)(2,1)} %cotangent_ref.1, ...), custom_call_target="tpu_custom_call" | custom-call | tf_op jit(solution)/shard_map/ffn/pallas_call | solution.py:1155
  228.0 0.0 reduce-scatter.2.cloned.1.call-update
  228.0 1.2 copy-done.2
  229.2 4.5 %fusion.2.grad_ref = f32[256,1024]{1,0:T(8,128)} fusion(bf16[256,2048]{1,0:T(8,128)(2,1)S(1)} %bitcast.85, bf16[2048,4224]{1,0:T(8,128)(2,1)} %bitcast.79), kind=kOutput, calls=%fused_computation.2 | convolution fusion | flops 1073741824 | bytes 6291456 | tf_op jit(solution)/shard_map/dot_general | solution.py:28
  233.7 6.0 %mix_outputs_back.1 = (f32[4,256,256]{2,1,0:T(8,128)}, bf16[256,1024]{1,0:T(8,128)(2,1)}, f32[1,256]{1,0:T(1,128)}, bf16[8,128,128]{2,1,0:T(8,128)(2,1)}, bf16[256,2048]{1,0:T(8,128)(2,1)}) custom-call(f32[256,1024]{1,0:T(8,128)} %fusion.2.grad_ref, f32[4,256,256]{2,1,0:T(8,128)} %get-tuple-element.83.mixed_ref, f32[4,256,128]{2,1,0:T(8,128)} %get-tuple-element.74.map_ref, ...), custom_call_target="tpu_custom_call" | custom-call | tf_op jit(solution)/shard_map/mix_outputs_back/pallas_call | solution.py:976
  239.7 28.9 %scan_backward.1 = (bf16[8,128,128]{2,1,0:T(8,128)(2,1)}, bf16[256,1024]{1,0:T(8,128)(2,1)}, bf16[256,1024]{1,0:T(8,128)(2,1)}, bf16[256,1024]{1,0:T(8,128)(2,1)}) custom-call(bf16[8,128,128]{2,1,0:T(8,128)(2,1)} %get-tuple-element.85.pack_ref, bf16[8,128,128]{2,1,0:T(8,128)(2,1)} %get-tuple-element.86.kept_ref, ...), custom_call_target="tpu_custom_call" | custom-call | tf_op jit(solution)/shard_map/scan_backward/pallas_call | solution.py:987
  268.6 46.0 %local_backward.1 = (bf16[256,2176]{1,0:T(8,128)(2,1)}, bf16[256,2176]{1,0:T(8,128)(2,1)}, f32[4,2048]{1,0:T(4,128)}, f32[8,128]{1,0:T(8,128)}, f32[64,1024]{1,0...) custom-call(f32[264,3200]{1,0:T(8,128)} %fusion.proj_ref, f32[4,2048]{1,0:T(4,128)} %bitcast.96, ...), custom_call_target="tpu_custom_call" | custom-call | tf_op jit(solution)/shard_map/local_backward/pallas_call | solution.py:987
  314.6 52.2 %last.1 = (bf16[4,64,2048]{2,1,0:T(8,128)(2,1)}, f32[8,2048]{1,0:T(8,128)}, f32[64,1152]{1,0:T(8,128)}, f32[64,1024]{1,0:T(8,128)}) custom-call(bf16[256,1024]{1,0:T(8,128)(2,1)} %get-tuple-element.89.gate_ref, bf16[4,64,2048]{2,1,0:T(8,128)(2,1)} %bitcast.82, f32[64,2048]{1,0:T(8,128)} %get-tuple-element.97.middle_grad_ref, f32[1,2048]{1,0:T(1,128)} %bitcast.100, ...), custom_call_target="tpu_custom_call" | custom-call | tf_op jit(solution)/shard_map/last/pallas_call | solution.py:1286
  366.8 1.3 slice_bitcast_fusion
  368.1 4.1 %finish.1 = (f32[64,4,768]{2,1,0:T(4,128)}, f32[64,2,4]{2,1,0:T(2,128)}, f32[64,4,256]{2,1,0:T(4,128)}, f32[64,2,1408]{2,1,0:T(2,128)}, f32[64,1408]{1,0:T(8,128...) custom-call(f32[64,1152]{1,0:T(8,128)} %get-tuple-element.104.first_a_ref, ...), custom_call_target="tpu_custom_call" | custom-call | tf_op jit(solution)/shard_map/finish/pallas_call | solution.py:976
  372.2 1.5 copy.53
  373.7 1.0 copy.124
  (53 shorter events, 0.3 us)
Async XLA Ops:
  7.2 3.0 slice-start
  7.2 3.0 slice-start.1
  7.2 2.8 copy-start.9
  7.2 2.9 copy-start.6
  7.2 3.1 copy-start.5
  7.2 173.7 %all-gather.2.cloned.1.call-start = ((), (), s32[]{:S(2)}) async-start(), calls=%async_computation.1 | async-start | bytes 17842176 | tf_op jit(solution)/shard_map/all_gather | solution.py:1062
  10.5 62.6 %copy-start.4 = (bf16[64,4224]{1,0:T(8,128)(2,1)}, bf16[64,4224]{1,0:T(8,128)(2,1)S(1)}, u32[]{:S(2)}) copy-start(bf16[64,4224]{1,0:T(8,128)(2,1)S(1)} %constant_dynamic-update-slice_fusion) | copy-start | bytes 1622020
  11.5 61.7 %copy-start = (bf16[256,2048]{1,0:T(8,128)(2,1)S(1)}, bf16[256,2048]{1,0:T(8,128)(2,1)}, u32[]{:S(2)}) copy-start(bf16[256,2048]{1,0:T(8,128)(2,1)} %param.13) | copy-start | bytes 3145732
  11.6 64.2 %copy-start.10 = (f32[4]{0:T(128)S(1)}, f32[4]{0:T(128)}, u32[]{:S(2)}) copy-start(f32[4]{0:T(128)} %param.19) | copy-start | bytes 52
  11.6 64.2 %copy-start.11 = (f32[4]{0:T(128)S(1)}, f32[4]{0:T(128)}, u32[]{:S(2)}) copy-start(f32[4]{0:T(128)} %param.18) | copy-start | bytes 52
  11.6 64.8 %copy-start.8 = (f32[4,4,512]{2,1,0:T(4,128)S(1)}, f32[4,4,512]{2,1,0:T(4,128)}, u32[]{:S(2)}) copy-start(f32[4,4,512]{2,1,0:T(4,128)} %param.17) | copy-start | bytes 98308
  11.6 65.7 %copy-start.7 = (f32[2048]{0:T(1024)S(1)}, f32[2048]{0:T(1024)}, u32[]{:S(2)}) copy-start(f32[2048]{0:T(1024)} %param.14) | copy-start | bytes 24580
  73.2 294.9 %reduce-scatter.2.cloned.1.call-start = ((), (), s32[]{:S(2)}) async-start(), calls=%async_computation.2 | async-start | bytes 6127616 | tf_op jit(solution)/shard_map/reduce_scatter | solution.py:1191
  73.3 3.7 collective-permute-start
  77.6 11.1 %copy-start.1 = (bf16[264,2048]{1,0:T(8,128)(2,1)}, bf16[264,2048]{1,0:T(8,128)(2,1)S(1)}, u32[]{:S(2)}) copy-start(bf16[264,2048]{1,0:T(8,128)(2,1)S(1)} %fusion.11.normed_ref) | copy-start | bytes 3244036
  227.9 1.2 copy-start.2
  366.8 6.9 %copy-start.3 = (bf16[4,64,2048]{2,1,0:T(8,128)(2,1)S(1)}, bf16[4,64,2048]{2,1,0:T(8,128)(2,1)}, u32[]{:S(2)}) copy-start(bf16[4,64,2048]{2,1,0:T(8,128)(2,1)} %get-tuple-element.96) | copy-start | bytes 3145732
Sparse Core Ops, SparseCore 0:
  73.3 80.7 all-gather.1
  228.1 87.1 reduce-scatter.1
